TPU v7x, 512 devices: a whole 4x4x16 slice. The times are simulated.
512 devices in a mesh: dp: 64 (over y, z), col: 8 (over x, core).
Axes of the slice: x: 4, y: 4, z: 16, core: 2. Of those that a mesh axis runs over, the one named last changes fastest.
Arguments:
- tokens: bfloat16 [16384, 8192], P('dp', 'col'), may hold values from -6 to 6
- basis: bfloat16 [8192, 256], P('dp'), may hold values from -0.0625 to 0.0625
- grad_out: bfloat16 [16384, 28672], P('dp', 'col'), may hold values from -0.046875 to 0.046875
- first_moment: float32 [256, 28672], P('dp', 'col'), may hold values from -3 to 3
- second_moment: float32 [256, 28672], P('dp', 'col'), may hold values from 0.002 to 0.02
Outputs:
- new_first: float32 [256, 28672], P('dp', 'col')
- new_second: float32 [256, 28672], P('dp', 'col')
- update: float32 [8192, 28672], P('dp', 'col')
All inputs are finite; a program needn't handle non-finite values.
Results may differ from a plain program's by a relative error of at most 0.003.
Values may be sent and summed in bfloat16 or wider, within the bound.
No kernel may reach another device: no remote copies, remote signals or barrier semaphores. Data moves between devices by JAX's collectives and lax.ppermute only.
A program may use at most 64 MiB of HBM per device.

v0:
```python
import jax
import jax.numpy as jnp
from jax import lax
from jax.sharding import PartitionSpec as P

STEP = 10


def on_device(tokens, basis, grad_out, first_moment, second_moment):
    full_tokens = lax.all_gather(tokens, "col", axis=1, tiled=True)
    summed = jnp.dot(
        full_tokens,
        lax.all_gather(basis, "dp", axis=0, tiled=True),
        preferred_element_type=jnp.float32,
    )
    projected = summed.astype(jnp.bfloat16)
    share_rows = first_moment.shape[0]
    local_grad = lax.dot_general(
        projected, grad_out, (((0,), (0,)), ((), ())), preferred_element_type=jnp.float32
    )
    summed_grad = lax.psum(local_grad, "dp")
    gradient = lax.dynamic_slice_in_dim(
        summed_grad, lax.axis_index("dp") * share_rows, share_rows, 0
    )
    new_first = 0.9 * first_moment + 0.1 * gradient
    new_second = 0.999 * second_moment + 0.001 * gradient * gradient
    first_scale = 1.0 - 0.9**STEP
    second_scale = 1.0 - 0.999**STEP
    direction = new_first / first_scale / (jnp.sqrt(new_second / second_scale) + 1e-08)
    direction = direction.astype(jnp.bfloat16)
    all_direction = lax.all_gather(direction, "dp", axis=0, tiled=True)
    update = jnp.dot(basis, all_direction, preferred_element_type=jnp.float32)
    return (new_first, new_second, update)


def solution(mesh):
    in_specs = (P("dp", "col"), P("dp", None), P("dp", "col"), P("dp", "col"), P("dp", "col"))
    out_specs = (P("dp", "col"), P("dp", "col"), P("dp", "col"))
    return jax.shard_map(
        on_device, mesh=mesh, in_specs=in_specs, out_specs=out_specs, check_vma=False
    )
```

profile of v0, /device:TPU:1, one launch (start us, length us, event | category | flops | bytes accessed | tf_op | source)
XLA Modules:
  0.0 641.6 jit_solution(17936815145167767292)
XLA Ops:
  7.2 0.0 copy-start
  7.2 0.0 all-gather.5.cloned.1.call-start
  7.2 0.7 all-gather.5.cloned.1.call-update
  7.9 0.0 all-gather.7.cloned.1.call-start
  8.0 0.7 all-gather.7.cloned.1.call-update
  8.7 0.0 all-reduce.2.cloned.1.call-start
  8.7 46.9 %all-gather.5.cloned.1.call-done = bf16[256,8192]{1,0:T(8,128)(2,1)} async-done(((bf16[256,1024]{1,0:T(8,128)(2,1)}), bf16[256,8192]{1,0:T(8,128)(2,1)}) %all-gather.5.cloned.1.call-update) | async-done | bytes 4194320 | tf_op jit(solution)/shard_map/all_gather | solution.py:10
  55.7 141.1 %all-gather.7.cloned.1.call-done = bf16[8192,256]{1,0:T(8,128)(2,1)} async-done(((bf16[128,256]{1,0:T(8,128)(2,1)}), bf16[8192,256]{1,0:T(8,128)(2,1)}) %all-gather.7.cloned.1.call-update) | async-done | bytes 4194320 | tf_op jit(solution)/shard_map/all_gather | solution.py:13
  196.7 0.0 copy-done
  196.8 8.1 %fusion = f32[256,3584]{1,0:T(8,128)} fusion(bf16[256,3584]{1,0:T(8,128)(2,1)S(1)} %copy-done, bf16[256,8192]{1,0:T(8,128)(2,1)} %all-gather.5.cloned.1.call-done, bf16[8192,256]{1,0:T(8,128)(2,1)} %all-gather.7.cloned.1.call-done), kind=kOutput, calls=%fused_computation.2 | convolution fusion | flops 1543569408 | bytes 13893632 | tf_op jit(solution)/shard_map/dot_general | solution.py:18
  204.8 0.0 copy-start.2
  204.8 0.0 copy-start.3
  204.8 0.0 copy-start.1
  204.8 0.0 all-reduce.2.cloned.1.call-update
  204.9 0.0 all-gather.9.cloned.1.call-start
  204.9 280.3 %all-reduce.2.cloned.1.call-done = f32[256,3584]{1,0:T(8,128)} async-done(((f32[256,3584]{1,0:T(8,128)}), f32[256,3584]{1,0:T(8,128)}) %all-reduce.2.cloned.1.call-update) | async-done | bytes 3670032 | tf_op jit(solution)/shard_map/psum | solution.py:21
  485.3 0.0 copy-done.2
  485.3 0.0 copy-done.3
  485.3 1.6 fusion.3
  486.9 0.0 all-gather.9.cloned.1.call-update
  486.9 138.1 %all-gather.9.cloned.1.call-done = bf16[64,4,3584]{2,1,0:T(4,128)(2,1)} async-done(((bf16[1,4,3584]{2,1,0:T(4,128)(2,1)}), bf16[64,4,3584]{2,1,0:T(4,128)(2,1)}) %all-gather.9.cloned.1.call-update) | async-done | bytes 1835024 | tf_op jit(solution)/shard_map/all_gather | solution.py:31
  625.0 3.9 reshape.7
  628.9 0.0 copy-done.1
  628.9 3.5 convolution_bitcast_fusion
  632.4 2.7 copy.9
Async XLA Ops:
  7.2 189.6 %copy-start = (bf16[256,3584]{1,0:T(8,128)(2,1)S(1)}, bf16[256,3584]{1,0:T(8,128)(2,1)}, u32[]{:S(2)}) copy-start(bf16[256,3584]{1,0:T(8,128)(2,1)} %param.7) | copy-start | bytes 5505028
  7.2 48.5 %all-gather.5.cloned.1.call-start = ((), (), s32[]{:S(2)}) async-start(), calls=%async_computation | async-start | bytes 4718592 | tf_op jit(solution)/shard_map/all_gather | solution.py:10
  7.9 188.8 %all-gather.7.cloned.1.call-start = ((), (), s32[]{:S(2)}) async-start(), calls=%async_computation.1 | async-start | bytes 4259840 | tf_op jit(solution)/shard_map/all_gather | solution.py:13
  8.7 476.6 %all-reduce.2.cloned.1.call-start = ((), (), s32[]{:S(2)}) async-start(), calls=%async_computation.2 | async-start | bytes 7340032 | tf_op jit(solution)/shard_map/psum | solution.py:21
  204.8 280.4 %copy-start.2 = (f32[4,3584]{1,0:T(4,128)S(1)}, f32[4,3584]{1,0:T(4,128)}, u32[]{:S(2)}) copy-start(f32[4,3584]{1,0:T(4,128)} %param.9) | copy-start | bytes 172036
  204.8 280.4 %copy-start.3 = (f32[4,3584]{1,0:T(4,128)S(1)}, f32[4,3584]{1,0:T(4,128)}, u32[]{:S(2)}) copy-start(f32[4,3584]{1,0:T(4,128)} %param.8) | copy-start | bytes 172036
  204.8 424.1 %copy-start.1 = (bf16[128,256]{1,0:T(8,128)(2,1)S(1)}, bf16[128,256]{1,0:T(8,128)(2,1)}, u32[]{:S(2)}) copy-start(bf16[128,256]{1,0:T(8,128)(2,1)} %param.6) | copy-start | bytes 196612
  204.9 420.1 %all-gather.9.cloned.1.call-start = ((), (), s32[]{:S(2)}) async-start(), calls=%async_computation.3 | async-start | bytes 1863680 | tf_op jit(solution)/shard_map/all_gather | solution.py:31
Sparse Core Ops, SparseCore 0:
  10.1 45.4 all-gather.4
  58.6 138.1 all-gather.6
  205.0 280.2 all-reduce.1
  489.1 135.8 all-gather.8
where the time goes:
time: 650 us; the launch traced here: 642 us
  waiting for transfers between devices  608 us (94%)
  between operations  13.8 us (2%)
  matrix products  11.6 us (2%)
  local copies, waits for them, and re-layouts  6.64 us (1%)
    psum x1, waiting for transfers between devices, on_device(): summed_grad = lax.psum(local_grad, 'dp')  280 us
    all_gather x1, waiting for transfers between devices, on_device(): lax.all_gather(basis, 'dp', axis=0, tiled=True)  141 us
    all_gather x1, waiting for transfers between devices, on_device(): all_direction = lax.all_gather(direction, 'dp', axis=0, tiled=True)  138 us
    all_gather x1, waiting for transfers between devices, on_device(): full_tokens = lax.all_gather(tokens, 'col', axis=1, tiled=True)  46.9 us
  transfers between devices with their start and end apart: 4, of which 4 were waited for; matrix products, arithmetic and copies ran while one was open for 0% of the time, Pallas kernels for 0%

commit v1 on v0

v1 whole, which is shorter than its diff:
```python
import jax
import jax.numpy as jnp
from jax import lax
from jax.sharding import Mesh, PartitionSpec as P

STEP = 10
Y, Z, X, C = 4, 16, 4, 2
bf16, f32 = jnp.bfloat16, jnp.float32


def exchange(x, axes):
    return lax.all_to_all(x, axes, 0, 0, tiled=True)


def gather(x, axes, n):
    return exchange(jnp.broadcast_to(x[None], (n,) + x.shape), axes)


def rank_order(first, count, ranks):
    share = ranks // (Y * Z)
    place = lax.broadcasted_iota(jnp.int32, (ranks, count), 1) + first
    z, y, j = place // (Y * share), place // share % Y, place % share
    rank = (y * Z + z) * share + j
    return (lax.broadcasted_iota(jnp.int32, (ranks, count), 0) == rank).astype(bf16)


def adam(first_moment, second_moment, gradient):
    new_first = 0.9 * first_moment + 0.1 * gradient
    new_second = 0.999 * second_moment + 0.001 * gradient * gradient
    return new_first, new_second


def on_device(tokens, basis, grad_out, first_moment, second_moment):
    rows, ranks = basis.shape
    count, features = tokens.shape
    share, columns = first_moment.shape
    part = columns // Y
    half = ranks // C
    core = lax.axis_index("c")

    ordered_half = jnp.dot(basis, rank_order(core * half, half, ranks), preferred_element_type=f32).astype(bf16)
    turned = lax.ppermute(ordered_half, ("y", "x"), [(y * X + x, x * X + y) for y in range(Y) for x in range(X)])
    chip_basis = gather(turned, "z", Z).reshape(C, features, half)

    other = lax.ppermute(tokens, "c", [(0, 1), (1, 0)])

    cut = grad_out.reshape(count, Y, part).transpose(1, 0, 2)
    all_grad_out = exchange(cut, "y").reshape(Y * count, part)

    ordered = jnp.dot(basis, rank_order(0, ranks, ranks), preferred_element_type=f32).astype(bf16)
    y_basis = gather(ordered, "y", Y).reshape(Y * rows, ranks)
    moments = jnp.concatenate([first_moment, second_moment], 0).reshape(2 * share, Y, part).transpose(1, 0, 2)
    moments = exchange(moments, "y").reshape(Y, 2, share, part)
    first_part = moments[:, 0].reshape(Y * share, part)
    second_part = moments[:, 1].reshape(Y * share, part)

    mine = lax.dynamic_index_in_dim(chip_basis, core, 0, keepdims=False)
    theirs = lax.dynamic_index_in_dim(chip_basis, 1 - core, 0, keepdims=False)
    summed = jnp.dot(tokens, mine, preferred_element_type=f32) + jnp.dot(other, theirs, preferred_element_type=f32)
    summed = exchange(summed.reshape(X, count // X, half), "x").sum(0)
    projected = gather(summed.astype(bf16), ("c", "y", "x"), C * Y * X).reshape(C, Y * count, half)

    partial = jnp.concatenate(
        [
            lax.dot_general(projected[c], all_grad_out, (((0,), (0,)), ((), ())), preferred_element_type=f32)
            for c in range(C)
        ],
        0,
    )
    partial = partial.astype(bf16).reshape(Z, Y * share, part)
    gradient = exchange(partial, "z").astype(f32).sum(0)

    first_scale = 1.0 - 0.9**STEP
    second_scale = 1.0 - 0.999**STEP
    new_first, new_second = adam(first_part, second_part, gradient)
    direction = new_first / first_scale / (jnp.sqrt(new_second / second_scale) + 1e-08)
    all_direction = gather(direction.astype(bf16), "z", Z).reshape(ranks, part)
    update = jnp.dot(y_basis, all_direction, preferred_element_type=f32).astype(bf16)
    update = exchange(update.reshape(Y, rows, part), "y").transpose(1, 0, 2).reshape(rows, columns).astype(f32)

    own = exchange(gradient.reshape(Y, share, part), "y").transpose(1, 0, 2).reshape(share, columns)
    new_first, new_second = adam(first_moment, second_moment, own)
    return (new_first, new_second, update)


def solution(mesh):
    grid = Mesh(mesh.devices.reshape(Y, Z, X, C), ("y", "z", "x", "c"))
    dp, col = ("y", "z"), ("x", "c")
    return jax.shard_map(
        on_device,
        mesh=grid,
        in_specs=(P(dp, col), P(dp, None), P(dp, col), P(dp, col), P(dp, col)),
        out_specs=(P(dp, col), P(dp, col), P(dp, col)),
        check_vma=False,
    )
```

time: 650 us -> 217 us (0.33)
  the two profiles are of different devices: /device:TPU:1 before, /device:TPU:64 now
where the time goes in v1:
time: 217 us; the launch traced here: 216 us
  waiting for transfers between devices  126 us (58%)
  starting transfers between devices  71.1 us (33%)
  local copies, waits for them, and re-layouts  12.5 us (6%)
  matrix products  3.39 us (2%)
  other arithmetic  2.54 us (1%)
    all_to_all x10, waiting for transfers between devices, exchange(): return lax.all_to_all(x, axes, 0, 0, tiled=True)  126 us
    all_to_all x10, starting transfers between devices, exchange(): return lax.all_to_all(x, axes, 0, 0, tiled=True)  68.5 us
  transfers between devices with their start and end apart: 12, of which 10 were waited for; matrix products, arithmetic and copies ran while one was open for 5% of the time, Pallas kernels for 0%

profile of v1, /device:TPU:64, one launch (start us, length us, event | category | flops | bytes accessed | tf_op | source)
XLA Modules:
  0.0 216.1 jit_solution(2837021415704168694)
XLA Ops:
  0.7 0.7 copy-done
  2.5 0.9 broadcast_in_dim.8
  3.4 14.9 %all-to-all-start = ((bf16[16,128,128]{2,1,0:T(8,128)(2,1)}), bf16[16,128,128]{2,1,0:T(8,128)(2,1)S(1)}, u32[]{:S(2)}, u32[]{:S(2)}) async-start(bf16[16,128,128]{2,1,0:T(8,128)(2,1)} %broadcast_in_dim.8), calls=%async_computation | async-start | bytes 1048576 | tf_op jit(solution)/shard_map/all_to_all | solution.py:12
  18.3 1.9 collective-permute-start.1
  20.2 25.5 %all-to-all-done = bf16[16,128,128]{2,1,0:T(8,128)(2,1)S(1)} async-done(((bf16[16,128,128]{2,1,0:T(8,128)(2,1)}), bf16[16,128,128]{2,1,0:T(8,128)(2,1)S(1)}, u32[]{:S(2)}, u32[]{:S(2)}) %all-to-all-start) | async-done | bytes 524320 | tf_op jit(solution)/shard_map/all_to_all | solution.py:12
  46.3 0.8 copy.18
  47.1 12.9 %all-to-all-start.1 = ((f32[4,64,128]{2,1,0:T(8,128)}), f32[4,64,128]{2,1,0:T(8,128)S(1)}, u32[]{:S(2)}, u32[]{:S(2)}) async-start(f32[4,64,128]{2,1,0:T(8,128)} %bitcast.5), calls=%async_computation.1 | async-start | bytes 262144 | tf_op jit(solution)/shard_map/all_to_all | solution.py:12
  60.0 2.2 %copy.19 = bf16[256,3584]{0,1:T(8,128)(2,1)} copy(bf16[256,3584]{1,0:T(8,128)(2,1)S(1)} %copy-done.2) | data formatting | bytes 3670016 | tf_op args[2]
  62.2 3.7 %all-to-all-done.1 = f32[4,64,128]{2,1,0:T(8,128)S(1)} async-done(((f32[4,64,128]{2,1,0:T(8,128)}), f32[4,64,128]{2,1,0:T(8,128)S(1)}, u32[]{:S(2)}, u32[]{:S(2)}) %all-to-all-start.1) | async-done | bytes 131104 | tf_op jit(solution)/shard_map/all_to_all | solution.py:12
  66.0 3.7 %all-to-all-start.3 = ((bf16[4,256,896]{1,2,0:T(8,128)(2,1)}), bf16[4,256,896]{1,2,0:T(8,128)(2,1)S(1)}, u32[]{:S(2)}, u32[]{:S(2)}) async-start(bf16[4,256,896]{1,2,0:T(8,128)(2,1)} %bitcast.58), calls=%async_computation.3 | async-start | bytes 3670016 | tf_op jit(solution)/shard_map/all_to_all | solution.py:12
  69.7 16.0 %all-to-all-done.3 = bf16[4,256,896]{1,2,0:T(8,128)(2,1)S(1)} async-done(((bf16[4,256,896]{1,2,0:T(8,128)(2,1)}), bf16[4,256,896]{1,2,0:T(8,128)(2,1)S(1)}, u32[]{:S(2)}, u32[]{:S(2)}) %all-to-all-start.3) | async-done | bytes 1835040 | tf_op jit(solution)/shard_map/all_to_all | solution.py:12
  85.7 1.0 broadcast_in_dim.9
  86.7 3.9 %all-to-all-start.2 = ((bf16[32,64,128]{2,1,0:T(8,128)(2,1)}), bf16[32,64,128]{2,1,0:T(8,128)(2,1)S(1)}, u32[]{:S(2)}, u32[]{:S(2)}) async-start(bf16[32,64,128]{2,1,0:T(8,128)(2,1)} %broadcast_in_dim.9), calls=%async_computation.2 | async-start | bytes 1048576 | tf_op jit(solution)/shard_map/all_to_all | solution.py:12
  91.3 2.9 %copy.20 = bf16[4,256,896]{2,1,0:T(8,128)(2,1)S(1)} copy(bf16[4,256,896]{1,2,0:T(8,128)(2,1)} %copy-done.1) | data formatting | bytes 3670016 | tf_op jit(solution)/shard_map/all_to_all | solution.py:12
  94.2 8.4 %all-to-all-done.2 = bf16[32,64,128]{2,1,0:T(8,128)(2,1)S(1)} async-done(((bf16[32,64,128]{2,1,0:T(8,128)(2,1)}), bf16[32,64,128]{2,1,0:T(8,128)(2,1)S(1)}, u32[]{:S(2)}, u32[]{:S(2)}) %all-to-all-start.2) | async-done | bytes 524320 | tf_op jit(solution)/shard_map/all_to_all | solution.py:12
  102.6 3.3 %all-to-all-start.7 = ((f32[4,8,896]{2,1,0:T(8,128)}), f32[4,8,896]{2,1,0:T(8,128)S(1)}, u32[]{:S(2)}, u32[]{:S(2)}) async-start(f32[4,8,896]{2,1,0:T(8,128)} %bitcast.18), calls=%async_computation.7 | async-start | bytes 229376 | tf_op jit(solution)/shard_map/all_to_all | solution.py:12
  106.9 0.8 pad_maximum_fusion
  107.7 4.0 %all-to-all-done.7 = f32[4,8,896]{2,1,0:T(8,128)S(1)} async-done(((f32[4,8,896]{2,1,0:T(8,128)}), f32[4,8,896]{2,1,0:T(8,128)S(1)}, u32[]{:S(2)}, u32[]{:S(2)}) %all-to-all-start.7) | async-done | bytes 114720 | tf_op jit(solution)/shard_map/all_to_all | solution.py:12
  111.8 13.3 %all-to-all-start.4 = ((bf16[16,16,896]{2,1,0:T(8,128)(2,1)}), bf16[16,16,896]{2,1,0:T(8,128)(2,1)S(1)}, u32[]{:S(2)}, u32[]{:S(2)}) async-start(bf16[16,16,896]{2,1,0:T(8,128)(2,1)} %bitcast.11), calls=%async_computation.4 | async-start | bytes 917504 | tf_op jit(solution)/shard_map/all_to_all | solution.py:12
  125.6 24.1 %all-to-all-done.4 = bf16[16,16,896]{2,1,0:T(8,128)(2,1)S(1)} async-done(((bf16[16,16,896]{2,1,0:T(8,128)(2,1)}), bf16[16,16,896]{2,1,0:T(8,128)(2,1)S(1)}, u32[]{:S(2)}, u32[]{:S(2)}) %all-to-all-start.4) | async-done | bytes 458784 | tf_op jit(solution)/shard_map/all_to_all | solution.py:12
  149.7 0.7 broadcast_in_dim.10
  150.4 3.4 %all-to-all-start.6 = ((bf16[4,128,256]{2,1,0:T(8,128)(2,1)}), bf16[4,128,256]{2,1,0:T(8,128)(2,1)S(1)}, u32[]{:S(2)}, u32[]{:S(2)}) async-start(bf16[4,128,256]{2,1,0:T(8,128)(2,1)} %broadcast_in_dim.10), calls=%async_computation.6 | async-start | bytes 524288 | tf_op jit(solution)/shard_map/all_to_all | solution.py:12
  153.9 6.5 %all-to-all-done.6 = bf16[4,128,256]{2,1,0:T(8,128)(2,1)S(1)} async-done(((bf16[4,128,256]{2,1,0:T(8,128)(2,1)}), bf16[4,128,256]{2,1,0:T(8,128)(2,1)S(1)}, u32[]{:S(2)}, u32[]{:S(2)}) %all-to-all-start.6) | async-done | bytes 262176 | tf_op jit(solution)/shard_map/all_to_all | solution.py:12
  160.4 0.8 broadcast_in_dim.11
  161.2 6.4 %all-to-all-start.8 = ((bf16[16,16,896]{2,1,0:T(8,128)(2,1)}), bf16[16,16,896]{2,1,0:T(8,128)(2,1)S(1)}, u32[]{:S(2)}, u32[]{:S(2)}) async-start(bf16[16,16,896]{2,1,0:T(8,128)(2,1)} %broadcast_in_dim.11), calls=%async_computation.8 | async-start | bytes 917504 | tf_op jit(solution)/shard_map/all_to_all | solution.py:12
  168.3 23.5 %all-to-all-done.8 = bf16[16,16,896]{2,1,0:T(8,128)(2,1)S(1)} async-done(((bf16[16,16,896]{2,1,0:T(8,128)(2,1)}), bf16[16,16,896]{2,1,0:T(8,128)(2,1)S(1)}, u32[]{:S(2)}, u32[]{:S(2)}) %all-to-all-start.8) | async-done | bytes 458784 | tf_op jit(solution)/shard_map/all_to_all | solution.py:12
  191.7 3.3 %all-to-all-start.5 = ((f32[4,4,896]{2,1,0:T(4,128)}), f32[4,4,896]{2,1,0:T(4,128)S(1)}, u32[]{:S(2)}, u32[]{:S(2)}) async-start(f32[4,4,896]{2,1,0:T(4,128)} %reshape.86), calls=%async_computation.5 | async-start | bytes 114688 | tf_op jit(solution)/shard_map/all_to_all | solution.py:12
  195.0 1.4 convolution_convert_fusion
  196.4 4.4 %all-to-all-done.5 = f32[4,4,896]{2,1,0:T(4,128)S(1)} async-done(((f32[4,4,896]{2,1,0:T(4,128)}), f32[4,4,896]{2,1,0:T(4,128)S(1)}, u32[]{:S(2)}, u32[]{:S(2)}) %all-to-all-start.5) | async-done | bytes 57376 | tf_op jit(solution)/shard_map/all_to_all | solution.py:12
  200.8 3.5 %all-to-all-start.9 = ((bf16[4,128,896]{2,1,0:T(8,128)(2,1)}), bf16[4,128,896]{2,1,0:T(8,128)(2,1)S(1)}, u32[]{:S(2)}, u32[]{:S(2)}) async-start(bf16[4,128,896]{2,1,0:T(8,128)(2,1)} %bitcast.20), calls=%async_computation.9 | async-start | bytes 1835008 | tf_op jit(solution)/shard_map/all_to_all | solution.py:12
  205.0 9.5 %all-to-all-done.9 = bf16[4,128,896]{2,1,0:T(8,128)(2,1)S(1)} async-done(((bf16[4,128,896]{2,1,0:T(8,128)(2,1)}), bf16[4,128,896]{2,1,0:T(8,128)(2,1)S(1)}, u32[]{:S(2)}, u32[]{:S(2)}) %all-to-all-start.9) | async-done | bytes 917536 | tf_op jit(solution)/shard_map/all_to_all | solution.py:12
  214.6 1.4 copy.27
  (44 shorter events, 5.4 us)
Async XLA Ops:
  0.6 0.8 copy-start
  0.6 17.6 %copy-start.3 = (bf16[256,1024]{1,0:T(8,128)(2,1)S(1)}, bf16[256,1024]{1,0:T(8,128)(2,1)}, u32[]{:S(2)}) copy-start(bf16[256,1024]{1,0:T(8,128)(2,1)} %param.5) | copy-start | bytes 1572868
  1.7 0.7 collective-permute-start
  3.4 56.6 %copy-start.2 = (bf16[256,3584]{1,0:T(8,128)(2,1)S(1)}, bf16[256,3584]{1,0:T(8,128)(2,1)}, u32[]{:S(2)}) copy-start(bf16[256,3584]{1,0:T(8,128)(2,1)} %param.7) | copy-start | bytes 5505028
  3.4 42.3 %all-to-all-start = ((bf16[16,128,128]{2,1,0:T(8,128)(2,1)}), bf16[16,128,128]{2,1,0:T(8,128)(2,1)S(1)}, u32[]{:S(2)}, u32[]{:S(2)}) async-start(bf16[16,128,128]{2,1,0:T(8,128)(2,1)} %broadcast_in_dim.8), calls=%async_computation | async-start | bytes 1048576 | tf_op jit(solution)/shard_map/all_to_all | solution.py:12
  18.3 27.7 %collective-permute-start.1 = (bf16[256,1024]{1,0:T(8,128)(2,1)S(1)}, bf16[256,1024]{1,0:T(8,128)(2,1)S(1)}, u32[]{:S(2)}, u32[]{:S(2)}) collective-permute-start(bf16[256,1024]{1,0:T(8,128)(2,1)S(1)} %copy-done.3), channel_id=1, source_target_pairs={{0,1},{1,0},{2,3},{3,2},{4,5},{5,4},{6,7},{7,6},{8,9},{9,8},{10,11... | collective-permute-start | bytes 1572872 | tf_op jit(solution)/shard_map/ppermute | solution.py:45
  47.1 18.9 %all-to-all-start.1 = ((f32[4,64,128]{2,1,0:T(8,128)}), f32[4,64,128]{2,1,0:T(8,128)S(1)}, u32[]{:S(2)}, u32[]{:S(2)}) async-start(f32[4,64,128]{2,1,0:T(8,128)} %bitcast.5), calls=%async_computation.1 | async-start | bytes 262144 | tf_op jit(solution)/shard_map/all_to_all | solution.py:12
  66.0 24.6 %copy-start.4 = (f32[4,3584]{1,0:T(4,128)S(1)}, f32[4,3584]{1,0:T(4,128)}, u32[]{:S(2)}) copy-start(f32[4,3584]{1,0:T(4,128)} %param.9) | copy-start | bytes 172036
  66.0 24.7 %copy-start.5 = (f32[4,3584]{1,0:T(4,128)S(1)}, f32[4,3584]{1,0:T(4,128)}, u32[]{:S(2)}) copy-start(f32[4,3584]{1,0:T(4,128)} %param.8) | copy-start | bytes 172036
  66.0 19.7 %all-to-all-start.3 = ((bf16[4,256,896]{1,2,0:T(8,128)(2,1)}), bf16[4,256,896]{1,2,0:T(8,128)(2,1)S(1)}, u32[]{:S(2)}, u32[]{:S(2)}) async-start(bf16[4,256,896]{1,2,0:T(8,128)(2,1)} %bitcast.58), calls=%async_computation.3 | async-start | bytes 3670016 | tf_op jit(solution)/shard_map/all_to_all | solution.py:12
  85.7 4.9 %copy-start.1 = (bf16[4,256,896]{1,2,0:T(8,128)(2,1)}, bf16[4,256,896]{1,2,0:T(8,128)(2,1)S(1)}, u32[]{:S(2)}) copy-start(bf16[4,256,896]{1,2,0:T(8,128)(2,1)S(1)} %all-to-all-done.3) | copy-start | bytes 5505028
  86.7 15.9 %all-to-all-start.2 = ((bf16[32,64,128]{2,1,0:T(8,128)(2,1)}), bf16[32,64,128]{2,1,0:T(8,128)(2,1)S(1)}, u32[]{:S(2)}, u32[]{:S(2)}) async-start(bf16[32,64,128]{2,1,0:T(8,128)(2,1)} %broadcast_in_dim.9), calls=%async_computation.2 | async-start | bytes 1048576 | tf_op jit(solution)/shard_map/all_to_all | solution.py:12
  102.6 9.2 %all-to-all-start.7 = ((f32[4,8,896]{2,1,0:T(8,128)}), f32[4,8,896]{2,1,0:T(8,128)S(1)}, u32[]{:S(2)}, u32[]{:S(2)}) async-start(f32[4,8,896]{2,1,0:T(8,128)} %bitcast.18), calls=%async_computation.7 | async-start | bytes 229376 | tf_op jit(solution)/shard_map/all_to_all | solution.py:12
  111.8 37.9 %all-to-all-start.4 = ((bf16[16,16,896]{2,1,0:T(8,128)(2,1)}), bf16[16,16,896]{2,1,0:T(8,128)(2,1)S(1)}, u32[]{:S(2)}, u32[]{:S(2)}) async-start(bf16[16,16,896]{2,1,0:T(8,128)(2,1)} %bitcast.11), calls=%async_computation.4 | async-start | bytes 917504 | tf_op jit(solution)/shard_map/all_to_all | solution.py:12
  150.4 10.1 %all-to-all-start.6 = ((bf16[4,128,256]{2,1,0:T(8,128)(2,1)}), bf16[4,128,256]{2,1,0:T(8,128)(2,1)S(1)}, u32[]{:S(2)}, u32[]{:S(2)}) async-start(bf16[4,128,256]{2,1,0:T(8,128)(2,1)} %broadcast_in_dim.10), calls=%async_computation.6 | async-start | bytes 524288 | tf_op jit(solution)/shard_map/all_to_all | solution.py:12
  161.2 30.5 %all-to-all-start.8 = ((bf16[16,16,896]{2,1,0:T(8,128)(2,1)}), bf16[16,16,896]{2,1,0:T(8,128)(2,1)S(1)}, u32[]{:S(2)}, u32[]{:S(2)}) async-start(bf16[16,16,896]{2,1,0:T(8,128)(2,1)} %broadcast_in_dim.11), calls=%async_computation.8 | async-start | bytes 917504 | tf_op jit(solution)/shard_map/all_to_all | solution.py:12
  191.7 9.1 %all-to-all-start.5 = ((f32[4,4,896]{2,1,0:T(4,128)}), f32[4,4,896]{2,1,0:T(4,128)S(1)}, u32[]{:S(2)}, u32[]{:S(2)}) async-start(f32[4,4,896]{2,1,0:T(4,128)} %reshape.86), calls=%async_computation.5 | async-start | bytes 114688 | tf_op jit(solution)/shard_map/all_to_all | solution.py:12
  200.8 13.7 %all-to-all-start.9 = ((bf16[4,128,896]{2,1,0:T(8,128)(2,1)}), bf16[4,128,896]{2,1,0:T(8,128)(2,1)S(1)}, u32[]{:S(2)}, u32[]{:S(2)}) async-start(bf16[4,128,896]{2,1,0:T(8,128)(2,1)} %bitcast.20), calls=%async_computation.9 | async-start | bytes 1835008 | tf_op jit(solution)/shard_map/all_to_all | solution.py:12

commit v2 on v1

v2 whole, which is shorter than its diff:
```python
import jax
import jax.numpy as jnp
from jax import lax
from jax.experimental import pallas as pl
from jax.experimental.pallas import tpu as pltpu
from jax.sharding import Mesh, PartitionSpec as P

STEP = 10
Y, Z, X, C = 4, 16, 4, 2
bf16, f32 = jnp.bfloat16, jnp.float32
VMEM = pl.BlockSpec(memory_space=pltpu.VMEM)


def exchange(x, axes):
    return lax.all_to_all(x, axes, 0, 0, tiled=True)


def gather(x, axes, n):
    return exchange(jnp.broadcast_to(x[None], (n,) + x.shape), axes)


def send(x, step):
    return lax.ppermute(x, "y", [(y, (y + step) % Y) for y in range(Y)])


def in_order(parts, me):
    twice = jnp.stack(parts[::-1] * 2)
    return lax.dynamic_slice_in_dim(twice, (Y - 1 - me) % Y, Y, 0)


def rank_order(first, count, ranks):
    share = ranks // (Y * Z)
    place = lax.broadcasted_iota(jnp.int32, (ranks, count), 1) + first
    z, y, j = place // (Y * share), place // share % Y, place % share
    rank = (y * Z + z) * share + j
    return (lax.broadcasted_iota(jnp.int32, (ranks, count), 0) == rank).astype(bf16)


def adam(first_moment, second_moment, gradient):
    new_first = 0.9 * first_moment + 0.1 * gradient
    new_second = 0.999 * second_moment + 0.001 * gradient * gradient
    return new_first, new_second


def partial_kernel(me_ref, joined_ref, *refs):
    grads, out_ref = refs[:Y], refs[Y]
    count = grads[0].shape[0]
    half = joined_ref.shape[3]
    for c in range(C):
        total = 0.0
        for d in range(Y):
            source = lax.rem(me_ref[0] + Y - d, Y)
            tokens = joined_ref[c, source, :count, :]
            total += lax.dot_general(tokens, grads[d][...], (((0,), (0,)), ((), ())), preferred_element_type=f32)
        out_ref[c * half : (c + 1) * half, :] = total.astype(bf16)


def adam_kernel(pieces_ref, first_ref, second_ref, gradient_ref, direction_ref):
    gradient = jnp.sum(pieces_ref[...].astype(f32), axis=0)
    gradient_ref[...] = gradient
    first_scale = 1.0 - 0.9**STEP
    second_scale = 1.0 - 0.999**STEP
    new_first, new_second = adam(first_ref[...], second_ref[...], gradient)
    direction = new_first / first_scale / (jnp.sqrt(new_second / second_scale) + 1e-08)
    direction_ref[...] = jnp.broadcast_to(direction.astype(bf16)[None], direction_ref.shape)


def update_kernel(joined_ref, direction_ref, out_ref):
    rows = out_ref.shape[1]
    half = joined_ref.shape[3]
    for y in range(Y):
        total = 0.0
        for c in range(C):
            basis = joined_ref[c, y, joined_ref.shape[2] - rows :, :]
            total += jnp.dot(basis, direction_ref[c * half : (c + 1) * half, :], preferred_element_type=f32)
        out_ref[y] = total.astype(bf16)


def on_device(tokens, basis, grad_out, first_moment, second_moment):
    rows, ranks = basis.shape
    count, features = tokens.shape
    share, columns = first_moment.shape
    part = columns // Y
    half = ranks // C
    core = lax.axis_index("c")
    me = lax.axis_index("y")

    ordered_half = jnp.dot(basis, rank_order(core * half, half, ranks), preferred_element_type=f32).astype(bf16)
    turned = lax.ppermute(ordered_half, ("y", "x"), [(y * X + x, x * X + y) for y in range(Y) for x in range(X)])
    chip_basis = gather(turned, "z", Z).reshape(C, features, half)

    other = lax.ppermute(tokens, "c", [(0, 1), (1, 0)])

    def columns_of(x, step):
        return lax.dynamic_slice_in_dim(x, (me + step) % Y * part, part, 1)

    grads = [columns_of(grad_out, 0)] + [send(columns_of(grad_out, d), d) for d in range(1, Y)]

    moments = jnp.concatenate([first_moment, second_moment], 0)
    moments = [columns_of(moments, 0)] + [send(columns_of(moments, d), d) for d in range(1, Y)]

    mine = lax.dynamic_index_in_dim(chip_basis, core, 0, keepdims=False)
    theirs = lax.dynamic_index_in_dim(chip_basis, 1 - core, 0, keepdims=False)
    summed = jnp.dot(tokens, mine, preferred_element_type=f32) + jnp.dot(other, theirs, preferred_element_type=f32)
    summed = gather(summed, "x", X).sum(0)
    summed, grads, moments = lax.optimization_barrier((summed, grads, moments))
    moments = in_order(moments, me)
    first_part = moments[:, :share].reshape(Y * share, part)
    second_part = moments[:, share:].reshape(Y * share, part)

    joined = jnp.concatenate([summed.astype(bf16), ordered_half], 0)
    joined = gather(joined, ("c", "y"), C * Y).reshape(C, Y, count + rows, half)

    partial = pl.pallas_call(
        partial_kernel,
        out_shape=jax.ShapeDtypeStruct((ranks, part), bf16),
        in_specs=[pl.BlockSpec(memory_space=pltpu.SMEM)] + [VMEM] * (1 + Y),
        out_specs=VMEM,
        compiler_params=pltpu.CompilerParams(vmem_limit_bytes=24 * 2**20),
        name="gradient_partial",
    )(me.reshape(1), joined, *grads)
    pieces = exchange(partial.reshape(Z, Y * share, part), "z")
    gradient, direction = pl.pallas_call(
        adam_kernel,
        out_shape=(
            jax.ShapeDtypeStruct((Y * share, part), f32),
            jax.ShapeDtypeStruct((Z, Y * share, part), bf16),
        ),
        in_specs=[VMEM] * 3,
        out_specs=(VMEM, VMEM),
        compiler_params=pltpu.CompilerParams(vmem_limit_bytes=24 * 2**20),
        name="sum_and_adam",
    )(pieces, first_part, second_part)
    all_direction = exchange(direction, "z").reshape(ranks, part)
    update = pl.pallas_call(
        update_kernel,
        out_shape=jax.ShapeDtypeStruct((Y, rows, part), bf16),
        in_specs=[VMEM] * 2,
        out_specs=VMEM,
        compiler_params=pltpu.CompilerParams(vmem_limit_bytes=24 * 2**20),
        name="update",
    )(joined, all_direction)
    update = exchange(update, "y").transpose(1, 0, 2).reshape(rows, columns).astype(f32)

    def rows_of(x, step):
        return lax.dynamic_slice_in_dim(x, (me + step) % Y * share, share, 0)

    own = in_order([rows_of(gradient, 0)] + [send(rows_of(gradient, d), d) for d in range(1, Y)], me)
    own = own.transpose(1, 0, 2).reshape(share, columns)
    new_first, new_second = adam(first_moment, second_moment, own)
    return (new_first, new_second, update)


def solution(mesh):
    grid = Mesh(mesh.devices.reshape(Y, Z, X, C), ("y", "z", "x", "c"))
    dp, col = ("y", "z"), ("x", "c")
    return jax.shard_map(
        on_device,
        mesh=grid,
        in_specs=(P(dp, col), P(dp, None), P(dp, col), P(dp, col), P(dp, col)),
        out_specs=(P(dp, col), P(dp, col), P(dp, col)),
        check_vma=False,
    )
```

time: 217 us -> 184 us (0.85)
  the two profiles are of different devices: /device:TPU:64 before, /device:TPU:2 now
where the time goes in v2:
time: 184 us; the launch traced here: 183 us
  waiting for transfers between devices  83 us (45%)
  starting transfers between devices  81.6 us (44%)
  local copies, waits for them, and re-layouts  8.4 us (5%)
  Pallas kernels  3.95 us (2%)
  matrix products  2.89 us (2%)
  other arithmetic  2.25 us (1%)
    all_to_all x6, waiting for transfers between devices, exchange(): return lax.all_to_all(x, axes, 0, 0, tiled=True)  72.9 us
    all_to_all x6, starting transfers between devices, exchange(): return lax.all_to_all(x, axes, 0, 0, tiled=True)  43.6 us
    ppermute x9, starting transfers between devices, send(): return lax.ppermute(x, 'y', [(y, (y + step) % Y) for y in range(Y)])  32.6 us
    ppermute x9, waiting for transfers between devices, send(): return lax.ppermute(x, 'y', [(y, (y + step) % Y) for y in range(Y)])  6.84 us
  transfers between devices with their start and end apart: 17, of which 9 were waited for; matrix products, arithmetic and copies ran while one was open for 3% of the time, Pallas kernels for 0%

profile of v2, /device:TPU:2, one launch (start us, length us, event | category | flops | bytes accessed | tf_op | source)
XLA Modules:
  0.0 183.2 jit_solution(4519408482207952778)
XLA Ops:
  1.6 3.5 %collective-permute-start = (bf16[128,128]{1,0:T(8,128)(2,1)S(1)}, bf16[128,128]{1,0:T(8,128)(2,1)S(1)}, u32[]{:S(2)}, u32[]{:S(2)}) collective-permute-start(bf16[128,128]{1,0:T(8,128)(2,1)S(1)} %fusion.1), channel_id=1, source_target_pairs={{0,0},{2,128},{4,256},{6,384},{128,2},{130,130},{132,258},{134,386... | collective-permute-start | bytes 98312 | tf_op jit(solution)/shard_map/ppermute | solution.py:89
  5.1 3.2 %collective-permute-done = bf16[128,128]{1,0:T(8,128)(2,1)S(1)} collective-permute-done((bf16[128,128]{1,0:T(8,128)(2,1)S(1)}, bf16[128,128]{1,0:T(8,128)(2,1)S(1)}, u32[]{:S(2)}, u32[]{:S(2)}) %collective-permute-start) | collective-permute-done | bytes 32800 | tf_op jit(solution)/shard_map/ppermute | solution.py:89
  9.2 15.2 %all-to-all-start = ((bf16[16,128,128]{2,1,0:T(8,128)(2,1)}), bf16[16,128,128]{2,1,0:T(8,128)(2,1)S(1)}, u32[]{:S(2)}, u32[]{:S(2)}) async-start(bf16[16,128,128]{2,1,0:T(8,128)(2,1)} %broadcast_in_dim.6), calls=%async_computation | async-start | bytes 1048576 | tf_op jit(solution)/shard_map/all_to_all | solution.py:15
  24.4 1.9 %collective-permute-start.1 = (bf16[256,1024]{1,0:T(8,128)(2,1)}, bf16[256,1024]{1,0:T(8,128)(2,1)}, u32[]{:S(2)}, u32[]{:S(2)}) collective-permute-start(bf16[256,1024]{1,0:T(8,128)(2,1)} %param.5), channel_id=1, source_target_pairs={{0,1},{1,0},{2,3},{3,2},{4,5},{5,4},{6,7},{7,6},{8,9},{9,8},{10,11... | collective-permute-start | bytes 1572872 | tf_op jit(solution)/shard_map/ppermute | solution.py:92
  27.6 1.9 %collective-permute-start.2 = (bf16[256,896]{1,0:T(8,128)(2,1)}, bf16[256,896]{1,0:T(8,128)(2,1)S(1)}, u32[]{:S(2)}, u32[]{:S(2)}) collective-permute-start(bf16[256,896]{1,0:T(8,128)(2,1)} %get-tuple-element.32), channel_id=1, source_target_pairs={{0,128},{128,256},{256,384},{384,0},{1,129},{129,257},{257,385},{3... | collective-permute-start | bytes 1376264 | tf_op jit(solution)/shard_map/ppermute | solution.py:23
  29.5 9.4 %collective-permute-start.3 = (bf16[256,896]{1,0:T(8,128)(2,1)}, bf16[256,896]{1,0:T(8,128)(2,1)S(1)}, u32[]{:S(2)}, u32[]{:S(2)}) collective-permute-start(bf16[256,896]{1,0:T(8,128)(2,1)} %get-tuple-element.34), channel_id=1, source_target_pairs={{0,256},{128,384},{256,0},{384,128},{1,257},{129,385},{257,1},{385... | collective-permute-start | bytes 1376264 | tf_op jit(solution)/shard_map/ppermute | solution.py:23
  38.9 1.9 %collective-permute-start.4 = (bf16[256,896]{1,0:T(8,128)(2,1)}, bf16[256,896]{1,0:T(8,128)(2,1)S(1)}, u32[]{:S(2)}, u32[]{:S(2)}) collective-permute-start(bf16[256,896]{1,0:T(8,128)(2,1)} %get-tuple-element.31), channel_id=1, source_target_pairs={{0,384},{128,0},{256,128},{384,256},{1,385},{129,1},{257,129},{385... | collective-permute-start | bytes 1376264 | tf_op jit(solution)/shard_map/ppermute | solution.py:23
  40.8 11.0 %all-to-all-done = bf16[16,128,128]{2,1,0:T(8,128)(2,1)S(1)} async-done(((bf16[16,128,128]{2,1,0:T(8,128)(2,1)}), bf16[16,128,128]{2,1,0:T(8,128)(2,1)S(1)}, u32[]{:S(2)}, u32[]{:S(2)}) %all-to-all-start) | async-done | bytes 524320 | tf_op jit(solution)/shard_map/all_to_all | solution.py:15
  51.8 1.4 fusion.3
  53.2 1.4 fusion
  55.5 7.8 %all-to-all-start.1 = ((f32[4,256,128]{2,1,0:T(8,128)}), f32[4,256,128]{2,1,0:T(8,128)S(1)}, u32[]{:S(2)}, u32[]{:S(2)}) async-start(f32[4,256,128]{2,1,0:T(8,128)} %broadcast_in_dim.7), calls=%async_computation.1 | async-start | bytes 1048576 | tf_op jit(solution)/shard_map/all_to_all | solution.py:15
  63.4 3.2 %collective-permute-start.5 = (f32[8,896]{1,0:T(8,128)S(1)}, f32[8,896]{1,0:T(8,128)S(1)}, u32[]{:S(2)}, u32[]{:S(2)}) collective-permute-start(f32[8,896]{1,0:T(8,128)S(1)} %get-tuple-element.39), channel_id=1, source_target_pairs={{0,128},{128,256},{256,384},{384,0},{1,129},{129,257},{257,385},{3... | collective-permute-start | bytes 86024 | tf_op jit(solution)/shard_map/ppermute | solution.py:23
  66.7 3.8 %collective-permute-start.6 = (f32[8,896]{1,0:T(8,128)S(1)}, f32[8,896]{1,0:T(8,128)S(1)}, u32[]{:S(2)}, u32[]{:S(2)}) collective-permute-start(f32[8,896]{1,0:T(8,128)S(1)} %get-tuple-element.40), channel_id=1, source_target_pairs={{0,256},{128,384},{256,0},{384,128},{1,257},{129,385},{257,1},{385... | collective-permute-start | bytes 86024 | tf_op jit(solution)/shard_map/ppermute | solution.py:23
  70.5 3.7 %collective-permute-start.7 = (f32[8,896]{1,0:T(8,128)S(1)}, f32[8,896]{1,0:T(8,128)S(1)}, u32[]{:S(2)}, u32[]{:S(2)}) collective-permute-start(f32[8,896]{1,0:T(8,128)S(1)} %get-tuple-element.37), channel_id=1, source_target_pairs={{0,384},{128,0},{256,128},{384,256},{1,385},{129,1},{257,129},{385... | collective-permute-start | bytes 86024 | tf_op jit(solution)/shard_map/ppermute | solution.py:23
  74.3 2.0 %collective-permute-done.7 = f32[8,896]{1,0:T(8,128)S(1)} collective-permute-done((f32[8,896]{1,0:T(8,128)S(1)}, f32[8,896]{1,0:T(8,128)S(1)}, u32[]{:S(2)}, u32[]{:S(2)}) %collective-permute-start.7) | collective-permute-done | bytes 28704 | tf_op jit(solution)/shard_map/ppermute | solution.py:23
  77.2 4.3 %all-to-all-start.2 = ((bf16[8,384,128]{2,1,0:T(8,128)(2,1)}), bf16[8,384,128]{2,1,0:T(8,128)(2,1)S(1)}, u32[]{:S(2)}, u32[]{:S(2)}) async-start(bf16[8,384,128]{2,1,0:T(8,128)(2,1)} %broadcast_in_dim.8), calls=%async_computation.2 | async-start | bytes 1572864 | tf_op jit(solution)/shard_map/all_to_all | solution.py:15
  81.5 12.5 %all-to-all-done.2 = bf16[8,384,128]{2,1,0:T(8,128)(2,1)S(1)} async-done(((bf16[8,384,128]{2,1,0:T(8,128)(2,1)}), bf16[8,384,128]{2,1,0:T(8,128)(2,1)S(1)}, u32[]{:S(2)}, u32[]{:S(2)}) %all-to-all-start.2) | async-done | bytes 786464 | tf_op jit(solution)/shard_map/all_to_all | solution.py:15
  94.1 1.5 gradient_partial.1
  95.6 6.9 %all-to-all-start.3 = ((bf16[16,16,896]{2,1,0:T(8,128)(2,1)}), bf16[16,16,896]{2,1,0:T(8,128)(2,1)S(1)}, u32[]{:S(2)}, u32[]{:S(2)}) async-start(bf16[16,16,896]{2,1,0:T(8,128)(2,1)} %bitcast.7), calls=%async_computation.3 | async-start | bytes 917504 | tf_op jit(solution)/shard_map/all_to_all | solution.py:15
  102.7 26.8 %all-to-all-done.3.pieces_ref = bf16[16,16,896]{2,1,0:T(8,128)(2,1)S(1)} async-done(((bf16[16,16,896]{2,1,0:T(8,128)(2,1)}), bf16[16,16,896]{2,1,0:T(8,128)(2,1)S(1)}, u32[]{:S(2)}, u32[]{:S(2)}) %all-to-all-start.3) | async-done | bytes 458784 | tf_op jit(solution)/shard_map/all_to_all | solution.py:15
  130.3 5.9 %all-to-all-start.4 = ((bf16[16,16,896]{2,1,0:T(8,128)(2,1)}), bf16[16,16,896]{2,1,0:T(8,128)(2,1)S(1)}, u32[]{:S(2)}, u32[]{:S(2)}) async-start(bf16[16,16,896]{2,1,0:T(8,128)(2,1)} %get-tuple-element.24), calls=%async_computation.4 | async-start | bytes 917504 | tf_op jit(solution)/shard_map/all_to_all | solution.py:15
  136.3 3.2 %collective-permute-start.8 = (f32[4,896]{1,0:T(4,128)S(1)}, f32[4,896]{1,0:T(4,128)S(1)}, u32[]{:S(2)}, u32[]{:S(2)}) collective-permute-start(f32[4,896]{1,0:T(4,128)S(1)} %get-tuple-element.45), channel_id=1, source_target_pairs={{0,384},{128,0},{256,128},{384,256},{1,385},{129,1},{257,129},{385... | collective-permute-start | bytes 43016 | tf_op jit(solution)/shard_map/ppermute | solution.py:23
  139.5 3.6 %collective-permute-start.9 = (f32[4,896]{1,0:T(4,128)S(1)}, f32[4,896]{1,0:T(4,128)S(1)}, u32[]{:S(2)}, u32[]{:S(2)}) collective-permute-start(f32[4,896]{1,0:T(4,128)S(1)} %get-tuple-element.44), channel_id=1, source_target_pairs={{0,256},{128,384},{256,0},{384,128},{1,257},{129,385},{257,1},{385... | collective-permute-start | bytes 43016 | tf_op jit(solution)/shard_map/ppermute | solution.py:23
  143.0 1.9 %collective-permute-start.10 = (f32[4,896]{1,0:T(4,128)S(1)}, f32[4,896]{1,0:T(4,128)S(1)}, u32[]{:S(2)}, u32[]{:S(2)}) collective-permute-start(f32[4,896]{1,0:T(4,128)S(1)} %get-tuple-element.43), channel_id=1, source_target_pairs={{0,128},{128,256},{256,384},{384,0},{1,129},{129,257},{257,385},{3... | collective-permute-start | bytes 43016 | tf_op jit(solution)/shard_map/ppermute | solution.py:23
  145.0 1.6 collective-permute-done.9
  146.6 3.3 %collective-permute-done.10 = f32[4,896]{1,0:T(4,128)S(1)} collective-permute-done((f32[4,896]{1,0:T(4,128)S(1)}, f32[4,896]{1,0:T(4,128)S(1)}, u32[]{:S(2)}, u32[]{:S(2)}) %collective-permute-start.10) | collective-permute-done | bytes 14368 | tf_op jit(solution)/shard_map/ppermute | solution.py:23
  150.0 13.1 %all-to-all-done.4 = bf16[16,16,896]{2,1,0:T(8,128)(2,1)S(1)} async-done(((bf16[16,16,896]{2,1,0:T(8,128)(2,1)}), bf16[16,16,896]{2,1,0:T(8,128)(2,1)S(1)}, u32[]{:S(2)}, u32[]{:S(2)}) %all-to-all-start.4) | async-done | bytes 458784 | tf_op jit(solution)/shard_map/all_to_all | solution.py:15
  163.1 1.5 update.1
  164.7 3.5 %all-to-all-start.5 = ((bf16[4,128,896]{2,1,0:T(8,128)(2,1)}), bf16[4,128,896]{2,1,0:T(8,128)(2,1)S(1)}, u32[]{:S(2)}, u32[]{:S(2)}) async-start(bf16[4,128,896]{2,1,0:T(8,128)(2,1)} %update.1), calls=%async_computation.5 | async-start | bytes 1835008 | tf_op jit(solution)/shard_map/all_to_all | solution.py:15
  168.9 9.5 %all-to-all-done.5 = bf16[4,128,896]{2,1,0:T(8,128)(2,1)S(1)} async-done(((bf16[4,128,896]{2,1,0:T(8,128)(2,1)}), bf16[4,128,896]{2,1,0:T(8,128)(2,1)S(1)}, u32[]{:S(2)}, u32[]{:S(2)}) %all-to-all-start.5) | async-done | bytes 917536 | tf_op jit(solution)/shard_map/all_to_all | solution.py:15
  179.7 1.8 copy.13
  181.5 1.7 copy.14
  (54 shorter events, 8.2 us)
Async XLA Ops:
  0.6 0.8 copy-start
  0.6 25.8 %copy-start.1 = (bf16[256,3584]{1,0:T(8,128)(2,1)S(1)}, bf16[256,3584]{1,0:T(8,128)(2,1)}, u32[]{:S(2)}) copy-start(bf16[256,3584]{1,0:T(8,128)(2,1)} %param.7) | copy-start | bytes 5505028
  1.6 6.7 %collective-permute-start = (bf16[128,128]{1,0:T(8,128)(2,1)S(1)}, bf16[128,128]{1,0:T(8,128)(2,1)S(1)}, u32[]{:S(2)}, u32[]{:S(2)}) collective-permute-start(bf16[128,128]{1,0:T(8,128)(2,1)S(1)} %fusion.1), channel_id=1, source_target_pairs={{0,0},{2,128},{4,256},{6,384},{128,2},{130,130},{132,258},{134,386... | collective-permute-start | bytes 98312 | tf_op jit(solution)/shard_map/ppermute | solution.py:89
  9.2 42.6 %all-to-all-start = ((bf16[16,128,128]{2,1,0:T(8,128)(2,1)}), bf16[16,128,128]{2,1,0:T(8,128)(2,1)S(1)}, u32[]{:S(2)}, u32[]{:S(2)}) async-start(bf16[16,128,128]{2,1,0:T(8,128)(2,1)} %broadcast_in_dim.6), calls=%async_computation | async-start | bytes 1048576 | tf_op jit(solution)/shard_map/all_to_all | solution.py:15
  24.4 28.8 %collective-permute-start.1 = (bf16[256,1024]{1,0:T(8,128)(2,1)}, bf16[256,1024]{1,0:T(8,128)(2,1)}, u32[]{:S(2)}, u32[]{:S(2)}) collective-permute-start(bf16[256,1024]{1,0:T(8,128)(2,1)} %param.5), channel_id=1, source_target_pairs={{0,1},{1,0},{2,3},{3,2},{4,5},{5,4},{6,7},{7,6},{8,9},{9,8},{10,11... | collective-permute-start | bytes 1572872 | tf_op jit(solution)/shard_map/ppermute | solution.py:92
  27.6 48.6 %collective-permute-start.2 = (bf16[256,896]{1,0:T(8,128)(2,1)}, bf16[256,896]{1,0:T(8,128)(2,1)S(1)}, u32[]{:S(2)}, u32[]{:S(2)}) collective-permute-start(bf16[256,896]{1,0:T(8,128)(2,1)} %get-tuple-element.32), channel_id=1, source_target_pairs={{0,128},{128,256},{256,384},{384,0},{1,129},{129,257},{257,385},{3... | collective-permute-start | bytes 1376264 | tf_op jit(solution)/shard_map/ppermute | solution.py:23
  29.5 46.7 %collective-permute-start.3 = (bf16[256,896]{1,0:T(8,128)(2,1)}, bf16[256,896]{1,0:T(8,128)(2,1)S(1)}, u32[]{:S(2)}, u32[]{:S(2)}) collective-permute-start(bf16[256,896]{1,0:T(8,128)(2,1)} %get-tuple-element.34), channel_id=1, source_target_pairs={{0,256},{128,384},{256,0},{384,128},{1,257},{129,385},{257,1},{385... | collective-permute-start | bytes 1376264 | tf_op jit(solution)/shard_map/ppermute | solution.py:23
  38.9 37.3 %collective-permute-start.4 = (bf16[256,896]{1,0:T(8,128)(2,1)}, bf16[256,896]{1,0:T(8,128)(2,1)S(1)}, u32[]{:S(2)}, u32[]{:S(2)}) collective-permute-start(bf16[256,896]{1,0:T(8,128)(2,1)} %get-tuple-element.31), channel_id=1, source_target_pairs={{0,384},{128,0},{256,128},{384,256},{1,385},{129,1},{257,129},{385... | collective-permute-start | bytes 1376264 | tf_op jit(solution)/shard_map/ppermute | solution.py:23
  51.8 11.5 %copy-start.2 = (f32[4,3584]{1,0:T(4,128)S(1)}, f32[4,3584]{1,0:T(4,128)}, u32[]{:S(2)}) copy-start(f32[4,3584]{1,0:T(4,128)} %param.8) | copy-start | bytes 172036
  51.8 11.5 %copy-start.3 = (f32[4,3584]{1,0:T(4,128)S(1)}, f32[4,3584]{1,0:T(4,128)}, u32[]{:S(2)}) copy-start(f32[4,3584]{1,0:T(4,128)} %param.9) | copy-start | bytes 172036
  55.5 18.7 %all-to-all-start.1 = ((f32[4,256,128]{2,1,0:T(8,128)}), f32[4,256,128]{2,1,0:T(8,128)S(1)}, u32[]{:S(2)}, u32[]{:S(2)}) async-start(f32[4,256,128]{2,1,0:T(8,128)} %broadcast_in_dim.7), calls=%async_computation.1 | async-start | bytes 1048576 | tf_op jit(solution)/shard_map/all_to_all | solution.py:15
  63.4 7.0 %collective-permute-start.5 = (f32[8,896]{1,0:T(8,128)S(1)}, f32[8,896]{1,0:T(8,128)S(1)}, u32[]{:S(2)}, u32[]{:S(2)}) collective-permute-start(f32[8,896]{1,0:T(8,128)S(1)} %get-tuple-element.39), channel_id=1, source_target_pairs={{0,128},{128,256},{256,384},{384,0},{1,129},{129,257},{257,385},{3... | collective-permute-start | bytes 86024 | tf_op jit(solution)/shard_map/ppermute | solution.py:23
  66.7 7.6 %collective-permute-start.6 = (f32[8,896]{1,0:T(8,128)S(1)}, f32[8,896]{1,0:T(8,128)S(1)}, u32[]{:S(2)}, u32[]{:S(2)}) collective-permute-start(f32[8,896]{1,0:T(8,128)S(1)} %get-tuple-element.40), channel_id=1, source_target_pairs={{0,256},{128,384},{256,0},{384,128},{1,257},{129,385},{257,1},{385... | collective-permute-start | bytes 86024 | tf_op jit(solution)/shard_map/ppermute | solution.py:23
  70.5 5.8 %collective-permute-start.7 = (f32[8,896]{1,0:T(8,128)S(1)}, f32[8,896]{1,0:T(8,128)S(1)}, u32[]{:S(2)}, u32[]{:S(2)}) collective-permute-start(f32[8,896]{1,0:T(8,128)S(1)} %get-tuple-element.37), channel_id=1, source_target_pairs={{0,384},{128,0},{256,128},{384,256},{1,385},{129,1},{257,129},{385... | collective-permute-start | bytes 86024 | tf_op jit(solution)/shard_map/ppermute | solution.py:23
  77.2 16.9 %all-to-all-start.2 = ((bf16[8,384,128]{2,1,0:T(8,128)(2,1)}), bf16[8,384,128]{2,1,0:T(8,128)(2,1)S(1)}, u32[]{:S(2)}, u32[]{:S(2)}) async-start(bf16[8,384,128]{2,1,0:T(8,128)(2,1)} %broadcast_in_dim.8), calls=%async_computation.2 | async-start | bytes 1572864 | tf_op jit(solution)/shard_map/all_to_all | solution.py:15
  95.6 33.8 %all-to-all-start.3 = ((bf16[16,16,896]{2,1,0:T(8,128)(2,1)}), bf16[16,16,896]{2,1,0:T(8,128)(2,1)S(1)}, u32[]{:S(2)}, u32[]{:S(2)}) async-start(bf16[16,16,896]{2,1,0:T(8,128)(2,1)} %bitcast.7), calls=%async_computation.3 | async-start | bytes 917504 | tf_op jit(solution)/shard_map/all_to_all | solution.py:15
  130.3 32.8 %all-to-all-start.4 = ((bf16[16,16,896]{2,1,0:T(8,128)(2,1)}), bf16[16,16,896]{2,1,0:T(8,128)(2,1)S(1)}, u32[]{:S(2)}, u32[]{:S(2)}) async-start(bf16[16,16,896]{2,1,0:T(8,128)(2,1)} %get-tuple-element.24), calls=%async_computation.4 | async-start | bytes 917504 | tf_op jit(solution)/shard_map/all_to_all | solution.py:15
  136.3 8.7 %collective-permute-start.8 = (f32[4,896]{1,0:T(4,128)S(1)}, f32[4,896]{1,0:T(4,128)S(1)}, u32[]{:S(2)}, u32[]{:S(2)}) collective-permute-start(f32[4,896]{1,0:T(4,128)S(1)} %get-tuple-element.45), channel_id=1, source_target_pairs={{0,384},{128,0},{256,128},{384,256},{1,385},{129,1},{257,129},{385... | collective-permute-start | bytes 43016 | tf_op jit(solution)/shard_map/ppermute | solution.py:23
  139.5 7.1 %collective-permute-start.9 = (f32[4,896]{1,0:T(4,128)S(1)}, f32[4,896]{1,0:T(4,128)S(1)}, u32[]{:S(2)}, u32[]{:S(2)}) collective-permute-start(f32[4,896]{1,0:T(4,128)S(1)} %get-tuple-element.44), channel_id=1, source_target_pairs={{0,256},{128,384},{256,0},{384,128},{1,257},{129,385},{257,1},{385... | collective-permute-start | bytes 43016 | tf_op jit(solution)/shard_map/ppermute | solution.py:23
  143.0 6.8 %collective-permute-start.10 = (f32[4,896]{1,0:T(4,128)S(1)}, f32[4,896]{1,0:T(4,128)S(1)}, u32[]{:S(2)}, u32[]{:S(2)}) collective-permute-start(f32[4,896]{1,0:T(4,128)S(1)} %get-tuple-element.43), channel_id=1, source_target_pairs={{0,128},{128,256},{256,384},{384,0},{1,129},{129,257},{257,385},{3... | collective-permute-start | bytes 43016 | tf_op jit(solution)/shard_map/ppermute | solution.py:23
  164.7 13.7 %all-to-all-start.5 = ((bf16[4,128,896]{2,1,0:T(8,128)(2,1)}), bf16[4,128,896]{2,1,0:T(8,128)(2,1)S(1)}, u32[]{:S(2)}, u32[]{:S(2)}) async-start(bf16[4,128,896]{2,1,0:T(8,128)(2,1)} %update.1), calls=%async_computation.5 | async-start | bytes 1835008 | tf_op jit(solution)/shard_map/all_to_all | solution.py:15

commit v3 on v1

v3 whole, which is shorter than its diff:
```python
import jax
import jax.numpy as jnp
from jax import lax
from jax.experimental import pallas as pl
from jax.experimental.pallas import tpu as pltpu
from jax.sharding import Mesh, PartitionSpec as P

STEP = 10
Y, Z, X, C = 4, 16, 4, 2
PACK = 48
MOMENT_ROWS = 32
bf16, f32 = jnp.bfloat16, jnp.float32
VMEM = pl.BlockSpec(memory_space=pltpu.VMEM)
SMEM = pl.BlockSpec(memory_space=pltpu.SMEM)


def exchange(x, axes):
    return lax.all_to_all(x, axes, 0, 0, tiled=True)


def gather(x, axes, n):
    return exchange(jnp.broadcast_to(x[None], (n,) + x.shape), axes)


def send(x, step):
    return lax.ppermute(x, "y", [(y, (y + step) % Y) for y in range(Y)])


def call(kernel, name, out, *args):
    return pl.pallas_call(
        kernel,
        out_shape=[jax.ShapeDtypeStruct(shape, dtype) for shape, dtype in out],
        in_specs=[SMEM] + [VMEM] * (len(args) - 1),
        out_specs=[VMEM] * len(out),
        compiler_params=pltpu.CompilerParams(vmem_limit_bytes=32 * 2**20),
        name=name,
    )(*args)


def rank_order(first, count, ranks):
    share = ranks // (Y * Z)
    place = lax.broadcasted_iota(jnp.int32, (ranks, count), 1) + first
    z, y, j = place // (Y * share), place // share % Y, place % share
    rank = (y * Z + z) * share + j
    return (lax.broadcasted_iota(jnp.int32, (ranks, count), 0) == rank).astype(bf16)


def three_parts(x):
    high = x.astype(bf16).astype(f32)
    rest = x - high
    middle = rest.astype(bf16).astype(f32)
    return high, middle, rest - middle


def adam(first_moment, second_moment, gradient):
    new_first = 0.9 * first_moment + 0.1 * gradient
    new_second = 0.999 * second_moment + 0.001 * gradient * gradient
    return new_first, new_second


def source(me, d):
    return (me + Y - d) & (Y - 1)


def pack_kernel(at_ref, basis_ref, grad_ref, moments_ref, *outs):
    part = outs[0].shape[1]
    count = grad_ref.shape[0]
    rows, ranks = basis_ref.shape
    for d in range(Y):
        begin = pl.multiple_of(((at_ref[0] + d) & (Y - 1)) * part, 128)
        outs[d][:count, :] = grad_ref[:, pl.ds(begin, part)]
        for k in range(3):
            take = min(PACK, rows - k * PACK)
            outs[d][count : count + take, k * ranks : (k + 1) * ranks] = basis_ref[k * PACK : k * PACK + take, :]
        parts = three_parts(moments_ref[:, pl.ds(begin, part)])
        parts = jnp.concatenate(parts + (jnp.zeros_like(parts[0]),), 0)
        outs[d][count + PACK :, :] = parts.astype(bf16)


def project_kernel(at_ref, tokens_ref, other_ref, basis_ref, out_ref):
    core = at_ref[1]
    total = jnp.dot(tokens_ref[...], basis_ref[core], preferred_element_type=f32)
    total += jnp.dot(other_ref[...], basis_ref[1 - core], preferred_element_type=f32)
    for x in range(out_ref.shape[0]):
        out_ref[x] = total


def round_kernel(at_ref, summands_ref, out_ref):
    total = jnp.sum(summands_ref[...], axis=0).astype(bf16)
    for i in range(out_ref.shape[0]):
        out_ref[i] = total


def partial_kernel(at_ref, projected_ref, *refs):
    messages, out_ref = refs[:Y], refs[Y]
    count, half = projected_ref.shape[2:]
    for c in range(C):
        total = 0.0
        for d in range(Y):
            tokens = projected_ref[c, source(at_ref[0], d)]
            total += lax.dot_general(tokens, messages[d][:count, :], (((0,), (0,)), ((), ())), preferred_element_type=f32)
        out_ref[c * half : (c + 1) * half, :] = total.astype(bf16)


def moments_kernel(at_ref, *refs):
    messages, (first_ref, second_ref) = refs[:Y], refs[Y:]
    ranks = first_ref.shape[0]
    stack = jnp.concatenate([m[m.shape[0] - MOMENT_ROWS :, :] for m in messages], 0)
    shape = (6 * ranks, stack.shape[0])
    row, column = lax.broadcasted_iota(jnp.int32, shape, 0), lax.broadcasted_iota(jnp.int32, shape, 1)
    which, rank = row // ranks, row % ranks
    moment, piece = which // 3, which % 3
    block = (at_ref[0] + Y - rank // 4) & (Y - 1)
    pick = (column == block * MOMENT_ROWS + piece * 8 + moment * 4 + rank % 4).astype(bf16)
    picked = jnp.dot(pick, stack, preferred_element_type=f32)
    for m, out_ref in enumerate((first_ref, second_ref)):
        high, middle, low = (picked[(3 * m + p) * ranks : (3 * m + p + 1) * ranks, :] for p in range(3))
        out_ref[...] = high + middle + low


def adam_kernel(at_ref, pieces_ref, first_ref, second_ref, gradient_ref, direction_ref):
    gradient = jnp.sum(pieces_ref[...].astype(f32), axis=0)
    gradient_ref[...] = gradient
    first_scale = 1.0 - 0.9**STEP
    second_scale = 1.0 - 0.999**STEP
    new_first, new_second = adam(first_ref[...], second_ref[...], gradient)
    direction = new_first / first_scale / (jnp.sqrt(new_second / second_scale) + 1e-08)
    direction = direction.astype(bf16)
    for h in range(direction_ref.shape[0]):
        direction_ref[h] = direction


def update_kernel(at_ref, direction_ref, gradient_ref, *refs):
    messages, out_ref = refs[:Y], refs[Y]
    count = messages[0].shape[0] - PACK - MOMENT_ROWS
    ranks = direction_ref.shape[0]
    rows = out_ref.shape[1] - 16
    direction = direction_ref[...]
    for d in range(Y):
        pieces = []
        for k in range(3):
            take = min(PACK, rows - k * PACK)
            pieces.append(messages[d][count : count + take, k * ranks : (k + 1) * ranks])
        basis = jnp.concatenate(pieces, 0)
        out_ref[source(at_ref[0], d), :rows, :] = jnp.dot(basis, direction, preferred_element_type=f32).astype(bf16)
    parts = jnp.concatenate(three_parts(gradient_ref[...]), 0).astype(bf16)
    shape = (Y * 16, parts.shape[0])
    row, column = lax.broadcasted_iota(jnp.int32, shape, 0), lax.broadcasted_iota(jnp.int32, shape, 1)
    place = row % 16
    wanted = place // 4 * gradient_ref.shape[0] + row // 16 * 4 + place % 4
    pick = ((column == wanted) & (place < 12)).astype(bf16)
    picked = jnp.dot(pick, parts, preferred_element_type=f32).astype(bf16)
    for y in range(Y):
        out_ref[y, rows:, :] = picked[16 * y : 16 * (y + 1), :]


def finish_kernel(at_ref, arrived_ref, first_ref, second_ref, new_first_ref, new_second_ref, update_ref):
    rows = update_ref.shape[0]
    part = arrived_ref.shape[2]
    for y in range(Y):
        columns = slice(y * part, (y + 1) * part)
        update_ref[:, columns] = arrived_ref[y, :rows, :].astype(f32)
        parts = arrived_ref[y, rows:, :].astype(f32)
        gradient = parts[0:4] + parts[4:8] + parts[8:12]
        new_first, new_second = adam(first_ref[:, columns], second_ref[:, columns], gradient)
        new_first_ref[:, columns] = new_first
        new_second_ref[:, columns] = new_second


def on_device(tokens, basis, grad_out, first_moment, second_moment):
    rows, ranks = basis.shape
    count, features = tokens.shape
    share, columns = first_moment.shape
    part = columns // Y
    half = ranks // C
    core = lax.axis_index("c")
    at = jnp.stack([lax.axis_index("y"), core])

    ordered_half = jnp.dot(basis, rank_order(core * half, half, ranks), preferred_element_type=f32).astype(bf16)
    turned = lax.ppermute(ordered_half, ("y", "x"), [(y * X + x, x * X + y) for y in range(Y) for x in range(X)])
    chip_basis = gather(turned, "z", Z).reshape(C, features, half)

    other = lax.ppermute(tokens, "c", [(0, 1), (1, 0)])

    ordered = jnp.dot(basis, rank_order(0, ranks, ranks), preferred_element_type=f32).astype(bf16)
    moments = jnp.concatenate([first_moment, second_moment], 0)
    message = (count + PACK + MOMENT_ROWS, part)
    messages = call(pack_kernel, "pack", [(message, bf16)] * Y, at, ordered, grad_out, moments)
    messages = [messages[0]] + [send(messages[d], d) for d in range(1, Y)]

    (summands,) = call(project_kernel, "project", [((X, count, half), f32)], at, tokens, other, chip_basis)
    summands = exchange(summands, "x")
    (projected,) = call(round_kernel, "round", [((C * Y, count, half), bf16)], at, summands)
    projected, messages = lax.optimization_barrier((projected, messages))
    projected = exchange(projected, ("c", "y")).reshape(C, Y, count, half)

    (partial,) = call(partial_kernel, "partial", [((ranks, part), bf16)], at, projected, *messages)
    pieces = exchange(partial.reshape(Z, ranks // Z, part), "z")
    first, second = call(moments_kernel, "moments", [((ranks // Z, part), f32)] * 2, at, *messages)
    gradient, direction = call(
        adam_kernel,
        "sum_and_adam",
        [((ranks // Z, part), f32), ((Z, ranks // Z, part), bf16)],
        at,
        pieces,
        first,
        second,
    )
    direction = exchange(direction, "z").reshape(ranks, part)
    (update,) = call(update_kernel, "update", [((Y, rows + 16, part), bf16)], at, direction, gradient, *messages)
    arrived = exchange(update, "y")
    return tuple(
        call(
            finish_kernel,
            "finish",
            [((share, columns), f32), ((share, columns), f32), ((rows, columns), f32)],
            at,
            arrived,
            first_moment,
            second_moment,
        )
    )


def solution(mesh):
    grid = Mesh(mesh.devices.reshape(Y, Z, X, C), ("y", "z", "x", "c"))
    dp, col = ("y", "z"), ("x", "c")
    return jax.shard_map(
        on_device,
        mesh=grid,
        in_specs=(P(dp, col), P(dp, None), P(dp, col), P(dp, col), P(dp, col)),
        out_specs=(P(dp, col), P(dp, col), P(dp, col)),
        check_vma=False,
    )
```

time: 217 us -> 174 us (0.80)
  the two profiles are of different devices: /device:TPU:64 before, /device:TPU:32 now
where the time goes in v3:
time: 174 us; the launch traced here: 173 us
  blocking collectives  82.5 us (47%)
  starting transfers between devices  50.4 us (29%)
  waiting for transfers between devices  25.3 us (15%)
  Pallas kernels  10.3 us (6%)
  local copies, waits for them, and re-layouts  3.26 us (2%)
    all_to_all x4, blocking collectives, exchange(): return lax.all_to_all(x, axes, 0, 0, tiled=True)  82.5 us
    all_to_all x2, starting transfers between devices, exchange(): return lax.all_to_all(x, axes, 0, 0, tiled=True)  27.2 us
    all_to_all x2, waiting for transfers between devices, exchange(): return lax.all_to_all(x, axes, 0, 0, tiled=True)  25.3 us
    ppermute x3, starting transfers between devices, send(): return lax.ppermute(x, 'y', [(y, (y + step) % Y) for y in range(Y)])  20.6 us
    pallas_call x8, Pallas kernels, call(): pl.pallas_call(kernel, out_shape=[jax.ShapeDtypeStruct(shape, dtype) for...  10.3 us
  transfers between devices with their start and end apart: 7, of which 2 were waited for; matrix products, arithmetic and copies ran while one was open for 0% of the time, Pallas kernels for 3%

profile of v3, /device:TPU:32, one launch (start us, length us, event | category | flops | bytes accessed | tf_op | source)
XLA Modules:
  0.0 173.2 jit_solution(7528988314862243869)
XLA Ops:
  0.6 0.0 copy-start
  0.7 0.0 copy-start.3
  0.7 0.0 copy-start.5
  0.8 0.7 copy-done
  1.5 0.2 fusion.1
  1.7 0.7 collective-permute-start.1
  2.4 0.1 copy.8
  2.5 0.9 broadcast_in_dim.2
  3.4 15.2 %all-to-all-start = ((bf16[16,128,128]{2,1,0:T(8,128)(2,1)}), bf16[16,128,128]{2,1,0:T(8,128)(2,1)S(1)}, u32[]{:S(2)}, u32[]{:S(2)}) async-start(bf16[16,128,128]{2,1,0:T(8,128)(2,1)} %broadcast_in_dim.2), calls=%async_computation | async-start | bytes 1048576 | tf_op jit(solution)/shard_map/all_to_all | solution.py:18
  18.6 1.9 %collective-permute-start = (bf16[256,1024]{1,0:T(8,128)(2,1)S(1)}, bf16[256,1024]{1,0:T(8,128)(2,1)}, u32[]{:S(2)}, u32[]{:S(2)}) collective-permute-start(bf16[256,1024]{1,0:T(8,128)(2,1)S(1)} %copy-done.2), channel_id=1, source_target_pairs={{0,1},{1,0},{2,3},{3,2},{4,5},{5,4},{6,7},{7,6},{8,9},{9,8},{10,11... | collective-permute-start | bytes 1572872 | tf_op jit(solution)/shard_map/ppermute | solution.py:183
  20.6 0.1 pad_add_fusion.at_ref
  20.7 0.2 fusion.basis_ref
  20.9 0.0 copy-start.1
  20.9 1.5 copy-done.1
  22.4 1.9 %pack.1 = (bf16[336,896]{1,0:T(8,128)(2,1)S(1)}, bf16[336,896]{1,0:T(8,128)(2,1)}, bf16[336,896]{1,0:T(8,128)(2,1)}, bf16[336,896]{1,0:T(8,128)(2,1)}) custom-call(s32[2]{0:T(128)S(1)} %pad_add_fusion.at_ref, bf16[128,256]{1,0:T(8,128)(2,1)S(1)} %fusion.basis_ref, bf16[256,3584]{1,0:T(8,128)(2,1)S(1)} %copy-done.1, f32[8,3584]{1,0:T(8,128)S(1)} %pad_maximum_fusion.moments_ref), custom_call_target="tpu_custom_call" | custom-call | tf_op jit(solution)/shard_map/pack/pallas_call | solution.py:30
  24.3 9.5 %collective-permute-start.2 = (bf16[336,896]{1,0:T(8,128)(2,1)}, bf16[336,896]{1,0:T(8,128)(2,1)S(1)}, u32[]{:S(2)}, u32[]{:S(2)}) collective-permute-start(bf16[336,896]{1,0:T(8,128)(2,1)} %get-tuple-element.17), channel_id=1, source_target_pairs={{0,128},{128,256},{256,384},{384,0},{1,129},{129,257},{257,385},{3... | collective-permute-start | bytes 1806344 | tf_op jit(solution)/shard_map/ppermute | solution.py:26
  33.8 7.2 %collective-permute-start.3 = (bf16[336,896]{1,0:T(8,128)(2,1)}, bf16[336,896]{1,0:T(8,128)(2,1)S(1)}, u32[]{:S(2)}, u32[]{:S(2)}) collective-permute-start(bf16[336,896]{1,0:T(8,128)(2,1)} %get-tuple-element.18), channel_id=1, source_target_pairs={{0,256},{128,384},{256,0},{384,128},{1,257},{129,385},{257,1},{385... | collective-permute-start | bytes 1806344 | tf_op jit(solution)/shard_map/ppermute | solution.py:26
  41.1 3.8 %collective-permute-start.4 = (bf16[336,896]{1,0:T(8,128)(2,1)}, bf16[336,896]{1,0:T(8,128)(2,1)S(1)}, u32[]{:S(2)}, u32[]{:S(2)}) collective-permute-start(bf16[336,896]{1,0:T(8,128)(2,1)} %get-tuple-element.19), channel_id=1, source_target_pairs={{0,384},{128,0},{256,128},{384,256},{1,385},{129,1},{257,129},{385... | collective-permute-start | bytes 1806344 | tf_op jit(solution)/shard_map/ppermute | solution.py:26
  44.9 1.9 %all-to-all-done = bf16[16,128,128]{2,1,0:T(8,128)(2,1)S(1)} async-done(((bf16[16,128,128]{2,1,0:T(8,128)(2,1)}), bf16[16,128,128]{2,1,0:T(8,128)(2,1)S(1)}, u32[]{:S(2)}, u32[]{:S(2)}) %all-to-all-start) | async-done | bytes 524320 | tf_op jit(solution)/shard_map/all_to_all | solution.py:18
  46.8 1.5 project.1
  48.3 20.5 %all_to_all.30.summands_ref = f32[4,256,128]{2,1,0:T(8,128)S(1)} all-to-all(f32[4,256,128]{2,1,0:T(8,128)S(1)} %project.1), channel_id=1, replica_groups=mesh['y'=4,'z'=16,'x'=4,'c'=2] {'x'}, dimensions={0} | all-to-all | bytes 1048576 | tf_op jit(solution)/shard_map/all_to_all | solution.py:18
  68.8 0.6 round.1
  69.4 12.6 %all_to_all.31 = bf16[8,256,128]{2,1,0:T(8,128)(2,1)S(1)} all-to-all(bf16[8,256,128]{2,1,0:T(8,128)(2,1)S(1)} %round.1), channel_id=1, replica_groups=mesh['y'=4,'z'=16,'x'=4,'c'=2] {'c','y'}, dimensions={0} | all-to-all | bytes 1048576 | tf_op jit(solution)/shard_map/all_to_all | solution.py:18
  82.1 2.1 %partial.1 = bf16[256,896]{1,0:T(8,128)(2,1)} custom-call(s32[2]{0:T(128)S(1)} %pad_add_fusion.at_ref, bf16[2,4,256,128]{3,2,1,0:T(8,128)(2,1)S(1)} %bitcast.13, bf16[336,896]{1,0:T(8,128)(2,1)S(1)} %get-tuple-element.21.refs_0_, bf16[336,896]{1,0:T(8,128)(2,1)S(1)} %collective-permute-done.2.refs_1_, bf16[336,896]{1,0:T(8,128)(2,1)S(1)} %collective-permute-done.3.refs_2_, ...), custom_call_target="tpu_custom_call" | custom-call | tf_op jit(solution)/shard_map/partial/pallas_call | solution.py:30
  84.1 12.0 %all-to-all-start.3 = ((bf16[16,16,896]{2,1,0:T(8,128)(2,1)}), bf16[16,16,896]{2,1,0:T(8,128)(2,1)S(1)}, u32[]{:S(2)}, u32[]{:S(2)}) async-start(bf16[16,16,896]{2,1,0:T(8,128)(2,1)} %bitcast.6), calls=%async_computation.3 | async-start | bytes 917504 | tf_op jit(solution)/shard_map/all_to_all | solution.py:18
  96.2 0.7 moments.1
  96.9 23.4 %all-to-all-done.3.pieces_ref = bf16[16,16,896]{2,1,0:T(8,128)(2,1)S(1)} async-done(((bf16[16,16,896]{2,1,0:T(8,128)(2,1)}), bf16[16,16,896]{2,1,0:T(8,128)(2,1)S(1)}, u32[]{:S(2)}, u32[]{:S(2)}) %all-to-all-start.3) | async-done | bytes 458784 | tf_op jit(solution)/shard_map/all_to_all | solution.py:18
  120.3 0.7 sum_and_adam.1
  120.9 32.7 %all_to_all.32 = bf16[16,16,896]{2,1,0:T(8,128)(2,1)S(1)} all-to-all(bf16[16,16,896]{2,1,0:T(8,128)(2,1)S(1)} %get-tuple-element.27), channel_id=1, replica_groups=mesh['y'=4,'z'=16,'x'=4,'c'=2] {'z'}, dimensions={0} | all-to-all | bytes 917504 | tf_op jit(solution)/shard_map/all_to_all | solution.py:18
  153.6 1.0 update.1
  154.7 16.6 %all_to_all.33.arrived_ref = bf16[4,144,896]{2,1,0:T(8,128)(2,1)S(1)} all-to-all(bf16[4,144,896]{2,1,0:T(8,128)(2,1)S(1)} %update.1), channel_id=1, replica_groups=mesh['y'=4,'z'=16,'x'=4,'c'=2] {'y'}, dimensions={0} | all-to-all | bytes 2064384 | tf_op jit(solution)/shard_map/all_to_all | solution.py:18
  171.3 1.9 %finish.1 = (f32[4,3584]{1,0:T(4,128)}, f32[4,3584]{1,0:T(4,128)}, f32[128,3584]{1,0:T(8,128)}) custom-call(s32[2]{0:T(128)S(1)} %pad_add_fusion.at_ref, bf16[4,144,896]{2,1,0:T(8,128)(2,1)S(1)} %all_to_all.33.arrived_ref, f32[4,3584]{1,0:T(4,128)S(1)} %copy-done.6, f32[4,3584]{1,0:T(4,128)S(1)} %copy-done.4), custom_call_target="tpu_custom_call" | custom-call | tf_op jit(solution)/shard_map/finish/pallas_call | solution.py:30
  (24 shorter events, 0.1 us)
Async XLA Ops:
  0.6 0.8 copy-start
  0.6 18.0 %copy-start.2 = (bf16[256,1024]{1,0:T(8,128)(2,1)S(1)}, bf16[256,1024]{1,0:T(8,128)(2,1)}, u32[]{:S(2)}) copy-start(bf16[256,1024]{1,0:T(8,128)(2,1)} %tokens_ref.1) | copy-start | bytes 1572868
  0.7 19.9 %copy-start.3 = (f32[4,3584]{1,0:T(4,128)S(1)}, f32[4,3584]{1,0:T(4,128)}, u32[]{:S(2)}) copy-start(f32[4,3584]{1,0:T(4,128)} %second_ref.1) | copy-start | bytes 172036
  0.7 19.9 %copy-start.5 = (f32[4,3584]{1,0:T(4,128)S(1)}, f32[4,3584]{1,0:T(4,128)}, u32[]{:S(2)}) copy-start(f32[4,3584]{1,0:T(4,128)} %first_ref.1) | copy-start | bytes 172036
  1.7 0.7 collective-permute-start.1
  3.4 43.4 %all-to-all-start = ((bf16[16,128,128]{2,1,0:T(8,128)(2,1)}), bf16[16,128,128]{2,1,0:T(8,128)(2,1)S(1)}, u32[]{:S(2)}, u32[]{:S(2)}) async-start(bf16[16,128,128]{2,1,0:T(8,128)(2,1)} %broadcast_in_dim.2), calls=%async_computation | async-start | bytes 1048576 | tf_op jit(solution)/shard_map/all_to_all | solution.py:18
  18.6 26.3 %collective-permute-start = (bf16[256,1024]{1,0:T(8,128)(2,1)S(1)}, bf16[256,1024]{1,0:T(8,128)(2,1)}, u32[]{:S(2)}, u32[]{:S(2)}) collective-permute-start(bf16[256,1024]{1,0:T(8,128)(2,1)S(1)} %copy-done.2), channel_id=1, source_target_pairs={{0,1},{1,0},{2,3},{3,2},{4,5},{5,4},{6,7},{7,6},{8,9},{9,8},{10,11... | collective-permute-start | bytes 1572872 | tf_op jit(solution)/shard_map/ppermute | solution.py:183
  20.9 1.5 copy-start.1
  24.3 45.1 %collective-permute-start.2 = (bf16[336,896]{1,0:T(8,128)(2,1)}, bf16[336,896]{1,0:T(8,128)(2,1)S(1)}, u32[]{:S(2)}, u32[]{:S(2)}) collective-permute-start(bf16[336,896]{1,0:T(8,128)(2,1)} %get-tuple-element.17), channel_id=1, source_target_pairs={{0,128},{128,256},{256,384},{384,0},{1,129},{129,257},{257,385},{3... | collective-permute-start | bytes 1806344 | tf_op jit(solution)/shard_map/ppermute | solution.py:26
  33.8 35.6 %collective-permute-start.3 = (bf16[336,896]{1,0:T(8,128)(2,1)}, bf16[336,896]{1,0:T(8,128)(2,1)S(1)}, u32[]{:S(2)}, u32[]{:S(2)}) collective-permute-start(bf16[336,896]{1,0:T(8,128)(2,1)} %get-tuple-element.18), channel_id=1, source_target_pairs={{0,256},{128,384},{256,0},{384,128},{1,257},{129,385},{257,1},{385... | collective-permute-start | bytes 1806344 | tf_op jit(solution)/shard_map/ppermute | solution.py:26
  41.1 28.4 %collective-permute-start.4 = (bf16[336,896]{1,0:T(8,128)(2,1)}, bf16[336,896]{1,0:T(8,128)(2,1)S(1)}, u32[]{:S(2)}, u32[]{:S(2)}) collective-permute-start(bf16[336,896]{1,0:T(8,128)(2,1)} %get-tuple-element.19), channel_id=1, source_target_pairs={{0,384},{128,0},{256,128},{384,256},{1,385},{129,1},{257,129},{385... | collective-permute-start | bytes 1806344 | tf_op jit(solution)/shard_map/ppermute | solution.py:26
  84.1 36.1 %all-to-all-start.3 = ((bf16[16,16,896]{2,1,0:T(8,128)(2,1)}), bf16[16,16,896]{2,1,0:T(8,128)(2,1)S(1)}, u32[]{:S(2)}, u32[]{:S(2)}) async-start(bf16[16,16,896]{2,1,0:T(8,128)(2,1)} %bitcast.6), calls=%async_computation.3 | async-start | bytes 917504 | tf_op jit(solution)/shard_map/all_to_all | solution.py:18
  154.7 16.7 %copy-start.4 = (f32[4,3584]{1,0:T(4,128)S(1)}, f32[4,3584]{1,0:T(4,128)}, u32[]{:S(2)}) copy-start(f32[4,3584]{1,0:T(4,128)} %second_ref.1) | copy-start | bytes 172036
  154.7 16.6 %copy-start.6 = (f32[4,3584]{1,0:T(4,128)S(1)}, f32[4,3584]{1,0:T(4,128)}, u32[]{:S(2)}) copy-start(f32[4,3584]{1,0:T(4,128)} %first_ref.1) | copy-start | bytes 172036

commit v4 on v3

--- a/solution.py
+++ b/solution.py
@@ -186,17 +186,19 @@
     moments = jnp.concatenate([first_moment, second_moment], 0)
     message = (count + PACK + MOMENT_ROWS, part)
     messages = call(pack_kernel, "pack", [(message, bf16)] * Y, at, ordered, grad_out, moments)
-    messages = [messages[0]] + [send(messages[d], d) for d in range(1, Y)]
+    sent = {d: send(messages[d], d) for d in (2, 3, 1)}
 
     (summands,) = call(project_kernel, "project", [((X, count, half), f32)], at, tokens, other, chip_basis)
     summands = exchange(summands, "x")
     (projected,) = call(round_kernel, "round", [((C * Y, count, half), bf16)], at, summands)
-    projected, messages = lax.optimization_barrier((projected, messages))
+    projected, sent[2], sent[3], sent[1] = lax.optimization_barrier((projected, sent[2], sent[3], sent[1]))
+    messages = [messages[0], sent[1], sent[2], sent[3]]
+    first, second = call(moments_kernel, "moments", [((ranks // Z, part), f32)] * 2, at, *messages)
+    projected, first, second = lax.optimization_barrier((projected, first, second))
     projected = exchange(projected, ("c", "y")).reshape(C, Y, count, half)
 
     (partial,) = call(partial_kernel, "partial", [((ranks, part), bf16)], at, projected, *messages)
     pieces = exchange(partial.reshape(Z, ranks // Z, part), "z")
-    first, second = call(moments_kernel, "moments", [((ranks // Z, part), f32)] * 2, at, *messages)
     gradient, direction = call(
         adam_kernel,
         "sum_and_adam",

time: 174 us -> 171 us (0.983)
  blocking collectives: 82.5 us -> 116 us
  waiting for transfers between devices: 25.3 us -> 2.53 us
  starting transfers between devices: 50.4 us -> 37.8 us
    all_to_all x4 -> x5, blocking collectives: 82.5 us -> 116 us  [exchange(): return lax.all_to_all(x, axes, 0, 0, tiled=True)]
    all_to_all x2 -> x1, waiting for transfers between devices: 25.3 us -> 2.52 us  [exchange(): return lax.all_to_all(x, axes, 0, 0, tiled=True)]
    all_to_all x2 -> x1, starting transfers between devices: 27.2 us -> 15.2 us  [exchange(): return lax.all_to_all(x, axes, 0, 0, tiled=True)]
  transfers between devices with their start and end apart: 7 -> 6, of which waited for: 2 -> 1; matrix products, arithmetic and copies ran while one was open for 0% -> 0% of each run, Pallas kernels for 3% -> 2%
where the time goes in v4:
time: 171 us
  blocking collectives  116 us (68%)
  starting transfers between devices  37.8 us (22%)
  Pallas kernels  9.58 us (6%)
  local copies, waits for them, and re-layouts  3.26 us (2%)
  waiting for transfers between devices  2.53 us (1%)
    all_to_all x5, blocking collectives, exchange(): return lax.all_to_all(x, axes, 0, 0, tiled=True)  116 us
    ppermute x3, starting transfers between devices, send(): return lax.ppermute(x, 'y', [(y, (y + step) % Y) for y in range(Y)])  20 us
    all_to_all x1, starting transfers between devices, exchange(): return lax.all_to_all(x, axes, 0, 0, tiled=True)  15.2 us
    pallas_call x8, Pallas kernels, call(): pl.pallas_call(kernel, out_shape=[jax.ShapeDtypeStruct(shape, dtype) for...  9.58 us
  transfers between devices with their start and end apart: 6, of which 1 were waited for; matrix products, arithmetic and copies ran while one was open for 0% of the time, Pallas kernels for 2%

profile of v4, /device:TPU:32, one launch (start us, length us, event | category | flops | bytes accessed | tf_op | source)
XLA Modules:
  0.0 170.8 jit_solution(7727170934750573924)
XLA Ops:
  0.6 0.0 copy-start
  0.7 0.0 copy-start.3
  0.7 0.0 copy-start.5
  0.8 0.7 copy-done
  1.5 0.2 fusion.1
  1.7 0.7 collective-permute-start.1
  2.4 0.1 copy.8
  2.5 0.9 broadcast_in_dim.2
  3.4 15.2 %all-to-all-start = ((bf16[16,128,128]{2,1,0:T(8,128)(2,1)}), bf16[16,128,128]{2,1,0:T(8,128)(2,1)S(1)}, u32[]{:S(2)}, u32[]{:S(2)}) async-start(bf16[16,128,128]{2,1,0:T(8,128)(2,1)} %broadcast_in_dim.2), calls=%async_computation | async-start | bytes 1048576 | tf_op jit(solution)/shard_map/all_to_all | solution.py:18
  18.6 1.9 %collective-permute-start = (bf16[256,1024]{1,0:T(8,128)(2,1)S(1)}, bf16[256,1024]{1,0:T(8,128)(2,1)}, u32[]{:S(2)}, u32[]{:S(2)}) collective-permute-start(bf16[256,1024]{1,0:T(8,128)(2,1)S(1)} %copy-done.2), channel_id=1, source_target_pairs={{0,1},{1,0},{2,3},{3,2},{4,5},{5,4},{6,7},{7,6},{8,9},{9,8},{10,11... | collective-permute-start | bytes 1572872 | tf_op jit(solution)/shard_map/ppermute | solution.py:183
  20.6 0.1 pad_add_fusion.at_ref
  20.7 0.2 fusion.basis_ref
  20.9 1.5 copy-done.1
  22.4 1.9 %pack.1 = (bf16[336,896]{1,0:T(8,128)(2,1)S(1)}, bf16[336,896]{1,0:T(8,128)(2,1)}, bf16[336,896]{1,0:T(8,128)(2,1)}, bf16[336,896]{1,0:T(8,128)(2,1)}) custom-call(s32[2]{0:T(128)S(1)} %pad_add_fusion.at_ref, bf16[128,256]{1,0:T(8,128)(2,1)S(1)} %fusion.basis_ref, bf16[256,3584]{1,0:T(8,128)(2,1)S(1)} %copy-done.1, f32[8,3584]{1,0:T(8,128)S(1)} %pad_maximum_fusion.moments_ref), custom_call_target="tpu_custom_call" | custom-call | tf_op jit(solution)/shard_map/pack/pallas_call | solution.py:30
  24.3 14.1 %collective-permute-start.2 = (bf16[336,896]{1,0:T(8,128)(2,1)}, bf16[336,896]{1,0:T(8,128)(2,1)S(1)}, u32[]{:S(2)}, u32[]{:S(2)}) collective-permute-start(bf16[336,896]{1,0:T(8,128)(2,1)} %get-tuple-element.18), channel_id=1, source_target_pairs={{0,256},{128,384},{256,0},{384,128},{1,257},{129,385},{257,1},{385... | collective-permute-start | bytes 1806344 | tf_op jit(solution)/shard_map/ppermute | solution.py:26
  38.4 1.9 %collective-permute-start.3 = (bf16[336,896]{1,0:T(8,128)(2,1)}, bf16[336,896]{1,0:T(8,128)(2,1)S(1)}, u32[]{:S(2)}, u32[]{:S(2)}) collective-permute-start(bf16[336,896]{1,0:T(8,128)(2,1)} %get-tuple-element.19), channel_id=1, source_target_pairs={{0,384},{128,0},{256,128},{384,256},{1,385},{129,1},{257,129},{385... | collective-permute-start | bytes 1806344 | tf_op jit(solution)/shard_map/ppermute | solution.py:26
  40.4 3.9 %collective-permute-start.4 = (bf16[336,896]{1,0:T(8,128)(2,1)}, bf16[336,896]{1,0:T(8,128)(2,1)S(1)}, u32[]{:S(2)}, u32[]{:S(2)}) collective-permute-start(bf16[336,896]{1,0:T(8,128)(2,1)} %get-tuple-element.20), channel_id=1, source_target_pairs={{0,128},{128,256},{256,384},{384,0},{1,129},{129,257},{257,385},{3... | collective-permute-start | bytes 1806344 | tf_op jit(solution)/shard_map/ppermute | solution.py:26
  44.3 2.5 %all-to-all-done = bf16[16,128,128]{2,1,0:T(8,128)(2,1)S(1)} async-done(((bf16[16,128,128]{2,1,0:T(8,128)(2,1)}), bf16[16,128,128]{2,1,0:T(8,128)(2,1)S(1)}, u32[]{:S(2)}, u32[]{:S(2)}) %all-to-all-start) | async-done | bytes 524320 | tf_op jit(solution)/shard_map/all_to_all | solution.py:18
  46.8 1.5 project.1
  48.3 20.5 %all_to_all.30.summands_ref = f32[4,256,128]{2,1,0:T(8,128)S(1)} all-to-all(f32[4,256,128]{2,1,0:T(8,128)S(1)} %project.1), channel_id=1, replica_groups=mesh['y'=4,'z'=16,'x'=4,'c'=2] {'x'}, dimensions={0} | all-to-all | bytes 1048576 | tf_op jit(solution)/shard_map/all_to_all | solution.py:18
  68.8 0.6 round.1
  69.4 0.8 moments.1
  70.2 12.2 %all_to_all.31 = bf16[8,256,128]{2,1,0:T(8,128)(2,1)S(1)} all-to-all(bf16[8,256,128]{2,1,0:T(8,128)(2,1)S(1)} %round.1), channel_id=1, replica_groups=mesh['y'=4,'z'=16,'x'=4,'c'=2] {'c','y'}, dimensions={0} | all-to-all | bytes 1048576 | tf_op jit(solution)/shard_map/all_to_all | solution.py:18
  82.4 1.3 partial.1
  83.7 34.1 %all_to_all.32.pieces_ref = bf16[16,16,896]{2,1,0:T(8,128)(2,1)S(1)} all-to-all(bf16[16,16,896]{2,1,0:T(8,128)(2,1)S(1)} %bitcast.15), channel_id=1, replica_groups=mesh['y'=4,'z'=16,'x'=4,'c'=2] {'z'}, dimensions={0} | all-to-all | bytes 917504 | tf_op jit(solution)/shard_map/all_to_all | solution.py:18
  117.8 0.7 sum_and_adam.1
  118.5 32.7 %all_to_all.33 = bf16[16,16,896]{2,1,0:T(8,128)(2,1)S(1)} all-to-all(bf16[16,16,896]{2,1,0:T(8,128)(2,1)S(1)} %get-tuple-element.31), channel_id=1, replica_groups=mesh['y'=4,'z'=16,'x'=4,'c'=2] {'z'}, dimensions={0} | all-to-all | bytes 917504 | tf_op jit(solution)/shard_map/all_to_all | solution.py:18
  151.2 1.0 update.1
  152.2 0.0 copy-start.4
  152.2 0.0 copy-start.6
  152.2 16.6 %all_to_all.34.arrived_ref = bf16[4,144,896]{2,1,0:T(8,128)(2,1)S(1)} all-to-all(bf16[4,144,896]{2,1,0:T(8,128)(2,1)S(1)} %update.1), channel_id=1, replica_groups=mesh['y'=4,'z'=16,'x'=4,'c'=2] {'y'}, dimensions={0} | all-to-all | bytes 2064384 | tf_op jit(solution)/shard_map/all_to_all | solution.py:18
  168.9 1.9 %finish.1 = (f32[4,3584]{1,0:T(4,128)}, f32[4,3584]{1,0:T(4,128)}, f32[128,3584]{1,0:T(8,128)}) custom-call(s32[2]{0:T(128)S(1)} %pad_add_fusion.at_ref, bf16[4,144,896]{2,1,0:T(8,128)(2,1)S(1)} %all_to_all.34.arrived_ref, f32[4,3584]{1,0:T(4,128)S(1)} %copy-done.6, f32[4,3584]{1,0:T(4,128)S(1)} %copy-done.4), custom_call_target="tpu_custom_call" | custom-call | tf_op jit(solution)/shard_map/finish/pallas_call | solution.py:30
  (23 shorter events, 0.1 us)
Async XLA Ops:
  0.6 0.8 copy-start
  0.6 17.9 %copy-start.2 = (bf16[256,1024]{1,0:T(8,128)(2,1)S(1)}, bf16[256,1024]{1,0:T(8,128)(2,1)}, u32[]{:S(2)}) copy-start(bf16[256,1024]{1,0:T(8,128)(2,1)} %tokens_ref.1) | copy-start | bytes 1572868
  0.7 19.9 %copy-start.3 = (f32[4,3584]{1,0:T(4,128)S(1)}, f32[4,3584]{1,0:T(4,128)}, u32[]{:S(2)}) copy-start(f32[4,3584]{1,0:T(4,128)} %second_ref.1) | copy-start | bytes 172036
  0.7 19.9 %copy-start.5 = (f32[4,3584]{1,0:T(4,128)S(1)}, f32[4,3584]{1,0:T(4,128)}, u32[]{:S(2)}) copy-start(f32[4,3584]{1,0:T(4,128)} %first_ref.1) | copy-start | bytes 172036
  1.7 0.7 collective-permute-start.1
  3.4 43.4 %all-to-all-start = ((bf16[16,128,128]{2,1,0:T(8,128)(2,1)}), bf16[16,128,128]{2,1,0:T(8,128)(2,1)S(1)}, u32[]{:S(2)}, u32[]{:S(2)}) async-start(bf16[16,128,128]{2,1,0:T(8,128)(2,1)} %broadcast_in_dim.2), calls=%async_computation | async-start | bytes 1048576 | tf_op jit(solution)/shard_map/all_to_all | solution.py:18
  18.6 25.7 %collective-permute-start = (bf16[256,1024]{1,0:T(8,128)(2,1)S(1)}, bf16[256,1024]{1,0:T(8,128)(2,1)}, u32[]{:S(2)}, u32[]{:S(2)}) collective-permute-start(bf16[256,1024]{1,0:T(8,128)(2,1)S(1)} %copy-done.2), channel_id=1, source_target_pairs={{0,1},{1,0},{2,3},{3,2},{4,5},{5,4},{6,7},{7,6},{8,9},{9,8},{10,11... | collective-permute-start | bytes 1572872 | tf_op jit(solution)/shard_map/ppermute | solution.py:183
  20.9 1.5 copy-start.1
  24.3 45.1 %collective-permute-start.2 = (bf16[336,896]{1,0:T(8,128)(2,1)}, bf16[336,896]{1,0:T(8,128)(2,1)S(1)}, u32[]{:S(2)}, u32[]{:S(2)}) collective-permute-start(bf16[336,896]{1,0:T(8,128)(2,1)} %get-tuple-element.18), channel_id=1, source_target_pairs={{0,256},{128,384},{256,0},{384,128},{1,257},{129,385},{257,1},{385... | collective-permute-start | bytes 1806344 | tf_op jit(solution)/shard_map/ppermute | solution.py:26
  38.4 31.0 %collective-permute-start.3 = (bf16[336,896]{1,0:T(8,128)(2,1)}, bf16[336,896]{1,0:T(8,128)(2,1)S(1)}, u32[]{:S(2)}, u32[]{:S(2)}) collective-permute-start(bf16[336,896]{1,0:T(8,128)(2,1)} %get-tuple-element.19), channel_id=1, source_target_pairs={{0,384},{128,0},{256,128},{384,256},{1,385},{129,1},{257,129},{385... | collective-permute-start | bytes 1806344 | tf_op jit(solution)/shard_map/ppermute | solution.py:26
  40.4 29.1 %collective-permute-start.4 = (bf16[336,896]{1,0:T(8,128)(2,1)}, bf16[336,896]{1,0:T(8,128)(2,1)S(1)}, u32[]{:S(2)}, u32[]{:S(2)}) collective-permute-start(bf16[336,896]{1,0:T(8,128)(2,1)} %get-tuple-element.20), channel_id=1, source_target_pairs={{0,128},{128,256},{256,384},{384,0},{1,129},{129,257},{257,385},{3... | collective-permute-start | bytes 1806344 | tf_op jit(solution)/shard_map/ppermute | solution.py:26
  152.2 16.7 %copy-start.4 = (f32[4,3584]{1,0:T(4,128)S(1)}, f32[4,3584]{1,0:T(4,128)}, u32[]{:S(2)}) copy-start(f32[4,3584]{1,0:T(4,128)} %second_ref.1) | copy-start | bytes 172036
  152.2 16.6 %copy-start.6 = (f32[4,3584]{1,0:T(4,128)S(1)}, f32[4,3584]{1,0:T(4,128)}, u32[]{:S(2)}) copy-start(f32[4,3584]{1,0:T(4,128)} %first_ref.1) | copy-start | bytes 172036

commit v5 on v4

--- a/solution.py
+++ b/solution.py
@@ -6,10 +6,12 @@
 from jax.sharding import Mesh, PartitionSpec as P
 
 STEP = 10
-Y, Z, X, C = 4, 16, 4, 2
+Y, H, L, X, C = 4, 8, 2, 4, 2
+Z = H * L
 PACK = 48
 MOMENT_ROWS = 32
 bf16, f32 = jnp.bfloat16, jnp.float32
+TURN = [(x * X + (y + 2) % X, y * X + x) for y in range(Y) for x in range(X)]
 VMEM = pl.BlockSpec(memory_space=pltpu.VMEM)
 SMEM = pl.BlockSpec(memory_space=pltpu.SMEM)
 
@@ -62,25 +64,44 @@
     return (me + Y - d) & (Y - 1)
 
 
-def pack_kernel(at_ref, basis_ref, grad_ref, moments_ref, *outs):
+def pack_kernel(at_ref, basis_ref, moments_ref, grad_ref, *refs):
+    outs, (rest_ref, done_ref) = refs[:Y], refs[Y:]
     part = outs[0].shape[1]
     count = grad_ref.shape[0]
     rows, ranks = basis_ref.shape
-    for d in range(Y):
-        begin = pl.multiple_of(((at_ref[0] + d) & (Y - 1)) * part, 128)
-        outs[d][:count, :] = grad_ref[:, pl.ds(begin, part)]
+    begins = [pl.multiple_of(((at_ref[0] + d) & (Y - 1)) * part, 128) for d in range(Y)]
+    order = (2, 3, 1, 0)
+    copies = []
+    for d in order:
+        block = grad_ref.at[:, pl.ds(begins[d], part)]
+        copies.append(pltpu.make_async_copy(block, outs[d].at[pl.ds(0, count), :], done_ref.at[d]))
+        copies[-1].start()
+    for d in order:
         for k in range(3):
             take = min(PACK, rows - k * PACK)
-            outs[d][count : count + take, k * ranks : (k + 1) * ranks] = basis_ref[k * PACK : k * PACK + take, :]
-        parts = three_parts(moments_ref[:, pl.ds(begin, part)])
+            rest_ref[d, :take, k * ranks : (k + 1) * ranks] = basis_ref[k * PACK : k * PACK + take, :]
+        parts = three_parts(moments_ref[:, pl.ds(begins[d], part)])
         parts = jnp.concatenate(parts + (jnp.zeros_like(parts[0]),), 0)
-        outs[d][count + PACK :, :] = parts.astype(bf16)
-
-
-def project_kernel(at_ref, tokens_ref, other_ref, basis_ref, out_ref):
-    core = at_ref[1]
-    total = jnp.dot(tokens_ref[...], basis_ref[core], preferred_element_type=f32)
-    total += jnp.dot(other_ref[...], basis_ref[1 - core], preferred_element_type=f32)
+        rest_ref[d, PACK:, :] = parts.astype(bf16)
+        rest = outs[d].at[pl.ds(count, PACK + MOMENT_ROWS), :]
+        copies.append(pltpu.make_async_copy(rest_ref.at[d], rest, done_ref.at[Y + d]))
+        copies[-1].start()
+    for copy in copies:
+        copy.wait()
+
+
+def project_kernel(at_ref, tokens_ref, other_ref, own_ref, got_ref, out_ref):
+    core, l = at_ref[1], at_ref[2]
+    shards, block, half = own_ref.shape
+    total = 0.0
+    for c, part_ref in ((core, tokens_ref), (1 - core, other_ref)):
+        for parity, basis_ref in ((l, own_ref), (1 - l, got_ref)):
+            pieces = []
+            for b in range(shards // C):
+                begin = pl.multiple_of((L * b + parity) * block, block)
+                pieces.append(part_ref[:, pl.ds(begin, block)])
+            rows = jnp.concatenate([basis_ref[c * (shards // C) + b] for b in range(shards // C)], 0)
+            total += jnp.dot(jnp.concatenate(pieces, 1), rows, preferred_element_type=f32)
     for x in range(out_ref.shape[0]):
         out_ref[x] = total
 
@@ -102,9 +123,7 @@
         out_ref[c * half : (c + 1) * half, :] = total.astype(bf16)
 
 
-def moments_kernel(at_ref, *refs):
-    messages, (first_ref, second_ref) = refs[:Y], refs[Y:]
-    ranks = first_ref.shape[0]
+def moments_of(at_ref, messages, ranks):
     stack = jnp.concatenate([m[m.shape[0] - MOMENT_ROWS :, :] for m in messages], 0)
     shape = (6 * ranks, stack.shape[0])
     row, column = lax.broadcasted_iota(jnp.int32, shape, 0), lax.broadcasted_iota(jnp.int32, shape, 1)
@@ -113,17 +132,18 @@
     block = (at_ref[0] + Y - rank // 4) & (Y - 1)
     pick = (column == block * MOMENT_ROWS + piece * 8 + moment * 4 + rank % 4).astype(bf16)
     picked = jnp.dot(pick, stack, preferred_element_type=f32)
-    for m, out_ref in enumerate((first_ref, second_ref)):
+    for m in range(2):
         high, middle, low = (picked[(3 * m + p) * ranks : (3 * m + p + 1) * ranks, :] for p in range(3))
-        out_ref[...] = high + middle + low
-
-
-def adam_kernel(at_ref, pieces_ref, first_ref, second_ref, gradient_ref, direction_ref):
+        yield high + middle + low
+
+
+def adam_kernel(at_ref, pieces_ref, *refs):
+    messages, (gradient_ref, direction_ref) = refs[:Y], refs[Y:]
     gradient = jnp.sum(pieces_ref[...].astype(f32), axis=0)
     gradient_ref[...] = gradient
     first_scale = 1.0 - 0.9**STEP
     second_scale = 1.0 - 0.999**STEP
-    new_first, new_second = adam(first_ref[...], second_ref[...], gradient)
+    new_first, new_second = adam(*moments_of(at_ref, messages, gradient.shape[0]), gradient)
     direction = new_first / first_scale / (jnp.sqrt(new_second / second_scale) + 1e-08)
     direction = direction.astype(bf16)
     for h in range(direction_ref.shape[0]):
@@ -174,41 +194,50 @@
     part = columns // Y
     half = ranks // C
     core = lax.axis_index("c")
-    at = jnp.stack([lax.axis_index("y"), core])
+    at = jnp.stack([lax.axis_index("y"), core, lax.axis_index("l")])
 
     ordered_half = jnp.dot(basis, rank_order(core * half, half, ranks), preferred_element_type=f32).astype(bf16)
-    turned = lax.ppermute(ordered_half, ("y", "x"), [(y * X + x, x * X + y) for y in range(Y) for x in range(X)])
-    chip_basis = gather(turned, "z", Z).reshape(C, features, half)
-
-    other = lax.ppermute(tokens, "c", [(0, 1), (1, 0)])
+    turned = lax.ppermute(ordered_half, ("y", "x"), TURN)
+    own_basis = gather(turned, "h", H)
+    got_basis = lax.ppermute(own_basis, "l", [(0, 1), (1, 0)])
 
     ordered = jnp.dot(basis, rank_order(0, ranks, ranks), preferred_element_type=f32).astype(bf16)
     moments = jnp.concatenate([first_moment, second_moment], 0)
     message = (count + PACK + MOMENT_ROWS, part)
-    messages = call(pack_kernel, "pack", [(message, bf16)] * Y, at, ordered, grad_out, moments)
+    anywhere = pl.BlockSpec(memory_space=pl.ANY)
+    messages = pl.pallas_call(
+        pack_kernel,
+        out_shape=[jax.ShapeDtypeStruct(message, bf16)] * Y,
+        in_specs=[SMEM, VMEM, VMEM, anywhere],
+        out_specs=[anywhere] * Y,
+        scratch_shapes=[pltpu.VMEM((Y, PACK + MOMENT_ROWS, part), bf16), pltpu.SemaphoreType.DMA((2 * Y,))],
+        compiler_params=pltpu.CompilerParams(vmem_limit_bytes=32 * 2**20),
+        name="pack",
+    )(at, ordered, moments, grad_out)
     sent = {d: send(messages[d], d) for d in (2, 3, 1)}
 
-    (summands,) = call(project_kernel, "project", [((X, count, half), f32)], at, tokens, other, chip_basis)
+    tokens, first_message = lax.optimization_barrier((tokens, messages[0]))
+    other = lax.ppermute(tokens, "c", [(0, 1), (1, 0)])
+
+    (summands,) = call(project_kernel, "project", [((X, count, half), f32)], at, tokens, other, own_basis, got_basis)
+    summands, sent[2] = lax.optimization_barrier((summands, sent[2]))
     summands = exchange(summands, "x")
     (projected,) = call(round_kernel, "round", [((C * Y, count, half), bf16)], at, summands)
-    projected, sent[2], sent[3], sent[1] = lax.optimization_barrier((projected, sent[2], sent[3], sent[1]))
-    messages = [messages[0], sent[1], sent[2], sent[3]]
-    first, second = call(moments_kernel, "moments", [((ranks // Z, part), f32)] * 2, at, *messages)
-    projected, first, second = lax.optimization_barrier((projected, first, second))
+    projected, sent[3], sent[1] = lax.optimization_barrier((projected, sent[3], sent[1]))
+    messages = [first_message, sent[1], sent[2], sent[3]]
     projected = exchange(projected, ("c", "y")).reshape(C, Y, count, half)
 
     (partial,) = call(partial_kernel, "partial", [((ranks, part), bf16)], at, projected, *messages)
-    pieces = exchange(partial.reshape(Z, ranks // Z, part), "z")
+    pieces = exchange(partial.reshape(Z, ranks // Z, part), ("h", "l"))
     gradient, direction = call(
         adam_kernel,
         "sum_and_adam",
         [((ranks // Z, part), f32), ((Z, ranks // Z, part), bf16)],
         at,
         pieces,
-        first,
-        second,
+        *messages,
     )
-    direction = exchange(direction, "z").reshape(ranks, part)
+    direction = exchange(direction, ("h", "l")).reshape(ranks, part)
     (update,) = call(update_kernel, "update", [((Y, rows + 16, part), bf16)], at, direction, gradient, *messages)
     arrived = exchange(update, "y")
     return tuple(
@@ -225,8 +254,8 @@
 
 
 def solution(mesh):
-    grid = Mesh(mesh.devices.reshape(Y, Z, X, C), ("y", "z", "x", "c"))
-    dp, col = ("y", "z"), ("x", "c")
+    grid = Mesh(mesh.devices.reshape(Y, H, L, X, C), ("y", "h", "l", "x", "c"))
+    dp, col = ("y", "h", "l"), ("x", "c")
     return jax.shard_map(
         on_device,
         mesh=grid,

time: 171 us -> 165 us (0.965)
  the two profiles are of different devices: /device:TPU:32 before, /device:TPU:34 now
where the time goes in v5:
time: 165 us
  blocking collectives  104 us (63%)
  starting transfers between devices  37.9 us (23%)
  waiting for transfers between devices  12 us (7%)
  Pallas kernels  8.01 us (5%)
    all_to_all x5, blocking collectives, exchange(): return lax.all_to_all(x, axes, 0, 0, tiled=True)  104 us
    all_to_all x1, starting transfers between devices, exchange(): return lax.all_to_all(x, axes, 0, 0, tiled=True)  14.2 us
    ppermute x3, starting transfers between devices, send(): return lax.ppermute(x, 'y', [(y, (y + step) % Y) for y in range(Y)])  12.7 us
    all_to_all x1, waiting for transfers between devices, exchange(): return lax.all_to_all(x, axes, 0, 0, tiled=True)  10.2 us
    pallas_call x6, Pallas kernels, call(): pl.pallas_call(kernel, out_shape=[jax.ShapeDtypeStruct(shape, dtype) for...  6.58 us
    ppermute x1, starting transfers between devices, on_device(): turned = lax.ppermute(ordered_half, ('y', 'x'), TURN)  4.89 us
    ppermute x1, starting transfers between devices, on_device(): got_basis = lax.ppermute(own_basis, 'l', [(0, 1), (1, 0)])  4.15 us
  transfers between devices with their start and end apart: 7, of which 2 were waited for; matrix products, arithmetic and copies ran while one was open for 0% of the time, Pallas kernels for 2%

profile of v5, /device:TPU:34, one launch (start us, length us, event | category | flops | bytes accessed | tf_op | source)
XLA Modules:
  0.0 164.8 jit_solution(14114308133187208154)
XLA Ops:
  0.6 0.0 copy-start
  0.8 0.7 copy-done
  1.5 0.2 fusion.1
  1.7 4.9 %collective-permute-start.1 = (bf16[128,128]{0,1:T(8,128)(2,1)S(1)}, bf16[128,128]{0,1:T(8,128)(2,1)S(1)}, u32[]{:S(2)}, u32[]{:S(2)}) collective-permute-start(bf16[128,128]{0,1:T(8,128)(2,1)S(1)} %fusion.1), channel_id=1, source_target_pairs={{4,0},{132,2},{260,4},{388,6},{6,128},{134,130},{262,132},{390,134... | collective-permute-start | bytes 98312 | tf_op jit(solution)/shard_map/ppermute | solution.py:200
  6.6 1.8 %collective-permute-done.1 = bf16[128,128]{0,1:T(8,128)(2,1)S(1)} collective-permute-done((bf16[128,128]{0,1:T(8,128)(2,1)S(1)}, bf16[128,128]{0,1:T(8,128)(2,1)S(1)}, u32[]{:S(2)}, u32[]{:S(2)}) %collective-permute-start.1) | collective-permute-done | bytes 32800 | tf_op jit(solution)/shard_map/ppermute | solution.py:200
  8.5 0.1 copy.9
  8.6 0.8 broadcast_in_dim.2
  9.4 14.2 %all-to-all-start = ((bf16[8,128,128]{2,1,0:T(8,128)(2,1)}), bf16[8,128,128]{2,1,0:T(8,128)(2,1)S(1)}, u32[]{:S(2)}, u32[]{:S(2)}) async-start(bf16[8,128,128]{2,1,0:T(8,128)(2,1)} %broadcast_in_dim.2), calls=%async_computation | async-start | bytes 524288 | tf_op jit(solution)/shard_map/all_to_all | solution.py:20
  23.6 0.2 fusion.basis_ref
  23.8 0.1 pad_add_fusion.at_ref
  23.9 1.4 pack.1
  25.3 5.0 %collective-permute-start.3 = (bf16[336,896]{1,0:T(8,128)(2,1)}, bf16[336,896]{1,0:T(8,128)(2,1)S(1)}, u32[]{:S(2)}, u32[]{:S(2)}) collective-permute-start(bf16[336,896]{1,0:T(8,128)(2,1)} %get-tuple-element.18), channel_id=1, source_target_pairs={{0,256},{128,384},{256,0},{384,128},{1,257},{129,385},{257,1},{385... | collective-permute-start | bytes 1806344 | tf_op jit(solution)/shard_map/ppermute | solution.py:28
  30.4 1.9 %collective-permute-start = (bf16[256,1024]{1,0:T(8,128)(2,1)S(1)}, bf16[256,1024]{1,0:T(8,128)(2,1)S(1)}, u32[]{:S(2)}, u32[]{:S(2)}) collective-permute-start(bf16[256,1024]{1,0:T(8,128)(2,1)S(1)} %copy-done.2), channel_id=1, source_target_pairs={{0,1},{1,0},{2,3},{3,2},{4,5},{5,4},{6,7},{7,6},{8,9},{9,8},{10,11... | collective-permute-start | bytes 1572872 | tf_op jit(solution)/shard_map/ppermute | solution.py:220
  32.3 10.2 %all-to-all-done.own_ref = bf16[8,128,128]{2,1,0:T(8,128)(2,1)S(1)} async-done(((bf16[8,128,128]{2,1,0:T(8,128)(2,1)}), bf16[8,128,128]{2,1,0:T(8,128)(2,1)S(1)}, u32[]{:S(2)}, u32[]{:S(2)}) %all-to-all-start) | async-done | bytes 262176 | tf_op jit(solution)/shard_map/all_to_all | solution.py:20
  42.5 4.2 %collective-permute-start.2 = (bf16[8,128,128]{2,1,0:T(8,128)(2,1)S(1)}, bf16[8,128,128]{2,1,0:T(8,128)(2,1)S(1)}, u32[]{:S(2)}, u32[]{:S(2)}) collective-permute-start(bf16[8,128,128]{2,1,0:T(8,128)(2,1)S(1)} %all-to-all-done.own_ref), channel_id=1, source_target_pairs={{0,8},{8,0},{1,9},{9,1},{2,10},{10,2},{3,11},{11,3},{4,12},{12,4},... | collective-permute-start | bytes 786440 | tf_op jit(solution)/shard_map/ppermute | solution.py:202
  46.7 5.8 %collective-permute-start.4 = (bf16[336,896]{1,0:T(8,128)(2,1)}, bf16[336,896]{1,0:T(8,128)(2,1)S(1)}, u32[]{:S(2)}, u32[]{:S(2)}) collective-permute-start(bf16[336,896]{1,0:T(8,128)(2,1)} %copy-done.6), channel_id=1, source_target_pairs={{0,384},{128,0},{256,128},{384,256},{1,385},{129,1},{257,129},{385... | collective-permute-start | bytes 1806344 | tf_op jit(solution)/shard_map/ppermute | solution.py:28
  52.5 1.9 %collective-permute-start.5 = (bf16[336,896]{1,0:T(8,128)(2,1)}, bf16[336,896]{1,0:T(8,128)(2,1)S(1)}, u32[]{:S(2)}, u32[]{:S(2)}) collective-permute-start(bf16[336,896]{1,0:T(8,128)(2,1)} %copy-done.5), channel_id=1, source_target_pairs={{0,128},{128,256},{256,384},{384,0},{1,129},{129,257},{257,385},{3... | collective-permute-start | bytes 1806344 | tf_op jit(solution)/shard_map/ppermute | solution.py:28
  54.4 0.0 collective-permute-done.other_ref
  54.4 0.0 collective-permute-done.2.got_ref
  54.4 1.0 project.1
  55.4 0.0 collective-permute-done.3.refs_2_
  55.4 10.7 %all_to_all.30.summands_ref = f32[4,256,128]{2,1,0:T(8,128)S(1)} all-to-all(f32[4,256,128]{2,1,0:T(8,128)S(1)} %project.1), channel_id=1, replica_groups=mesh['y'=4,'h'=8,'l'=2,'x'=4,'c'=2] {'x'}, dimensions={0} | all-to-all | bytes 1048576 | tf_op jit(solution)/shard_map/all_to_all | solution.py:20
  66.2 0.6 round.1
  66.8 0.0 collective-permute-done.5.refs_1_
  66.8 14.0 %all_to_all.31 = bf16[8,256,128]{2,1,0:T(8,128)(2,1)S(1)} all-to-all(bf16[8,256,128]{2,1,0:T(8,128)(2,1)S(1)} %round.1), channel_id=1, replica_groups=mesh['y'=4,'h'=8,'l'=2,'x'=4,'c'=2] {'c','y'}, dimensions={0} | all-to-all | bytes 1048576 | tf_op jit(solution)/shard_map/all_to_all | solution.py:20
  80.8 1.3 partial.1
  82.1 29.8 %all_to_all.32.pieces_ref = bf16[16,16,896]{2,1,0:T(8,128)(2,1)S(1)} all-to-all(bf16[16,16,896]{2,1,0:T(8,128)(2,1)S(1)} %bitcast.14), channel_id=1, replica_groups=mesh['y'=4,'h'=8,'l'=2,'x'=4,'c'=2] {'h','l'}, dimensions={0} | all-to-all | bytes 917504 | tf_op jit(solution)/shard_map/all_to_all | solution.py:20
  111.8 0.8 sum_and_adam.1
  112.6 32.7 %all_to_all.33 = bf16[16,16,896]{2,1,0:T(8,128)(2,1)S(1)} all-to-all(bf16[16,16,896]{2,1,0:T(8,128)(2,1)S(1)} %get-tuple-element.27), channel_id=1, replica_groups=mesh['y'=4,'h'=8,'l'=2,'x'=4,'c'=2] {'h','l'}, dimensions={0} | all-to-all | bytes 917504 | tf_op jit(solution)/shard_map/all_to_all | solution.py:20
  145.3 1.0 update.1
  146.3 16.5 %all_to_all.34.arrived_ref = bf16[4,144,896]{2,1,0:T(8,128)(2,1)S(1)} all-to-all(bf16[4,144,896]{2,1,0:T(8,128)(2,1)S(1)} %update.1), channel_id=1, replica_groups=mesh['y'=4,'h'=8,'l'=2,'x'=4,'c'=2] {'y'}, dimensions={0} | all-to-all | bytes 2064384 | tf_op jit(solution)/shard_map/all_to_all | solution.py:20
  162.9 1.9 %finish.1 = (f32[4,3584]{1,0:T(4,128)}, f32[4,3584]{1,0:T(4,128)}, f32[128,3584]{1,0:T(8,128)}) custom-call(s32[3]{0:T(128)S(1)} %pad_add_fusion.at_ref, bf16[4,144,896]{2,1,0:T(8,128)(2,1)S(1)} %all_to_all.34.arrived_ref, f32[4,3584]{1,0:T(4,128)S(1)} %copy-done.4, f32[4,3584]{1,0:T(4,128)S(1)} %copy-done.3), custom_call_target="tpu_custom_call" | custom-call | tf_op jit(solution)/shard_map/finish/pallas_call | solution.py:32
  (24 shorter events, 0.1 us)
Async XLA Ops:
  0.6 0.8 copy-start
  0.6 23.2 %copy-start.3 = (f32[4,3584]{1,0:T(4,128)S(1)}, f32[4,3584]{1,0:T(4,128)}, u32[]{:S(2)}) copy-start(f32[4,3584]{1,0:T(4,128)} %second_ref.1) | copy-start | bytes 172036
  0.7 23.2 %copy-start.4 = (f32[4,3584]{1,0:T(4,128)S(1)}, f32[4,3584]{1,0:T(4,128)}, u32[]{:S(2)}) copy-start(f32[4,3584]{1,0:T(4,128)} %first_ref.1) | copy-start | bytes 172036
  0.7 23.2 %copy-start.1 = (bf16[256,3584]{1,0:T(8,128)(2,1)S(1)}, bf16[256,3584]{1,0:T(8,128)(2,1)}, u32[]{:S(2)}) copy-start(bf16[256,3584]{1,0:T(8,128)(2,1)} %grad_ref.1) | copy-start | bytes 5505028
  1.7 6.8 %collective-permute-start.1 = (bf16[128,128]{0,1:T(8,128)(2,1)S(1)}, bf16[128,128]{0,1:T(8,128)(2,1)S(1)}, u32[]{:S(2)}, u32[]{:S(2)}) collective-permute-start(bf16[128,128]{0,1:T(8,128)(2,1)S(1)} %fusion.1), channel_id=1, source_target_pairs={{4,0},{132,2},{260,4},{388,6},{6,128},{134,130},{262,132},{390,134... | collective-permute-start | bytes 98312 | tf_op jit(solution)/shard_map/ppermute | solution.py:200
  9.4 33.1 %all-to-all-start = ((bf16[8,128,128]{2,1,0:T(8,128)(2,1)}), bf16[8,128,128]{2,1,0:T(8,128)(2,1)S(1)}, u32[]{:S(2)}, u32[]{:S(2)}) async-start(bf16[8,128,128]{2,1,0:T(8,128)(2,1)} %broadcast_in_dim.2), calls=%async_computation | async-start | bytes 524288 | tf_op jit(solution)/shard_map/all_to_all | solution.py:20
  23.6 6.8 %copy-start.2 = (bf16[256,1024]{1,0:T(8,128)(2,1)S(1)}, bf16[256,1024]{1,0:T(8,128)(2,1)}, u32[]{:S(2)}) copy-start(bf16[256,1024]{1,0:T(8,128)(2,1)} %tokens_ref) | copy-start | bytes 1572868
  25.3 5.0 %copy-start.5 = (bf16[336,896]{1,0:T(8,128)(2,1)}, bf16[336,896]{1,0:T(8,128)(2,1)S(1)}, u32[]{:S(2)}) copy-start(bf16[336,896]{1,0:T(8,128)(2,1)S(1)} %get-tuple-element.21) | copy-start | bytes 1806340
  25.3 5.0 %copy-start.6 = (bf16[336,896]{1,0:T(8,128)(2,1)}, bf16[336,896]{1,0:T(8,128)(2,1)S(1)}, u32[]{:S(2)}) copy-start(bf16[336,896]{1,0:T(8,128)(2,1)S(1)} %get-tuple-element.20) | copy-start | bytes 1806340
  25.3 30.1 %collective-permute-start.3 = (bf16[336,896]{1,0:T(8,128)(2,1)}, bf16[336,896]{1,0:T(8,128)(2,1)S(1)}, u32[]{:S(2)}, u32[]{:S(2)}) collective-permute-start(bf16[336,896]{1,0:T(8,128)(2,1)} %get-tuple-element.18), channel_id=1, source_target_pairs={{0,256},{128,384},{256,0},{384,128},{1,257},{129,385},{257,1},{385... | collective-permute-start | bytes 1806344 | tf_op jit(solution)/shard_map/ppermute | solution.py:28
  30.4 24.0 %collective-permute-start = (bf16[256,1024]{1,0:T(8,128)(2,1)S(1)}, bf16[256,1024]{1,0:T(8,128)(2,1)S(1)}, u32[]{:S(2)}, u32[]{:S(2)}) collective-permute-start(bf16[256,1024]{1,0:T(8,128)(2,1)S(1)} %copy-done.2), channel_id=1, source_target_pairs={{0,1},{1,0},{2,3},{3,2},{4,5},{5,4},{6,7},{7,6},{8,9},{9,8},{10,11... | collective-permute-start | bytes 1572872 | tf_op jit(solution)/shard_map/ppermute | solution.py:220
  42.5 11.9 %collective-permute-start.2 = (bf16[8,128,128]{2,1,0:T(8,128)(2,1)S(1)}, bf16[8,128,128]{2,1,0:T(8,128)(2,1)S(1)}, u32[]{:S(2)}, u32[]{:S(2)}) collective-permute-start(bf16[8,128,128]{2,1,0:T(8,128)(2,1)S(1)} %all-to-all-done.own_ref), channel_id=1, source_target_pairs={{0,8},{8,0},{1,9},{9,1},{2,10},{10,2},{3,11},{11,3},{4,12},{12,4},... | collective-permute-start | bytes 786440 | tf_op jit(solution)/shard_map/ppermute | solution.py:202
  46.7 20.1 %collective-permute-start.4 = (bf16[336,896]{1,0:T(8,128)(2,1)}, bf16[336,896]{1,0:T(8,128)(2,1)S(1)}, u32[]{:S(2)}, u32[]{:S(2)}) collective-permute-start(bf16[336,896]{1,0:T(8,128)(2,1)} %copy-done.6), channel_id=1, source_target_pairs={{0,384},{128,0},{256,128},{384,256},{1,385},{129,1},{257,129},{385... | collective-permute-start | bytes 1806344 | tf_op jit(solution)/shard_map/ppermute | solution.py:28
  52.5 14.3 %collective-permute-start.5 = (bf16[336,896]{1,0:T(8,128)(2,1)}, bf16[336,896]{1,0:T(8,128)(2,1)S(1)}, u32[]{:S(2)}, u32[]{:S(2)}) collective-permute-start(bf16[336,896]{1,0:T(8,128)(2,1)} %copy-done.5), channel_id=1, source_target_pairs={{0,128},{128,256},{256,384},{384,0},{1,129},{129,257},{257,385},{3... | collective-permute-start | bytes 1806344 | tf_op jit(solution)/shard_map/ppermute | solution.py:28

commit v6 on v5

--- a/solution.py
+++ b/solution.py
@@ -145,9 +145,7 @@
     second_scale = 1.0 - 0.999**STEP
     new_first, new_second = adam(*moments_of(at_ref, messages, gradient.shape[0]), gradient)
     direction = new_first / first_scale / (jnp.sqrt(new_second / second_scale) + 1e-08)
-    direction = direction.astype(bf16)
-    for h in range(direction_ref.shape[0]):
-        direction_ref[h] = direction
+    direction_ref[...] = direction.astype(bf16)
 
 
 def update_kernel(at_ref, direction_ref, gradient_ref, *refs):
@@ -232,12 +230,12 @@
     gradient, direction = call(
         adam_kernel,
         "sum_and_adam",
-        [((ranks // Z, part), f32), ((Z, ranks // Z, part), bf16)],
+        [((ranks // Z, part), f32), ((ranks // Z, part), bf16)],
         at,
         pieces,
         *messages,
     )
-    direction = exchange(direction, ("h", "l")).reshape(ranks, part)
+    direction = lax.all_gather(direction, ("h", "l"), axis=0, tiled=True)
     (update,) = call(update_kernel, "update", [((Y, rows + 16, part), bf16)], at, direction, gradient, *messages)
     arrived = exchange(update, "y")
     return tuple(

time: 165 us -> 165 us (level)
  the two profiles are of different devices: /device:TPU:34 before, /device:TPU:2 now
where the time goes in v6:
time: 165 us; the launch traced here: 164 us
  blocking collectives  103 us (62%)
  starting transfers between devices  36.9 us (22%)
  waiting for transfers between devices  13.3 us (8%)
  Pallas kernels  8.01 us (5%)
    all_to_all x4, blocking collectives, exchange(): return lax.all_to_all(x, axes, 0, 0, tiled=True)  70.3 us
    all_gather x1, blocking collectives, on_device(): direction = lax.all_gather(direction, ('h', 'l'), axis=0, tiled=True)  32.7 us
    all_to_all x1, starting transfers between devices, exchange(): return lax.all_to_all(x, axes, 0, 0, tiled=True)  15.1 us
    ppermute x3, starting transfers between devices, send(): return lax.ppermute(x, 'y', [(y, (y + step) % Y) for y in range(Y)])  13.1 us
    all_to_all x1, waiting for transfers between devices, exchange(): return lax.all_to_all(x, axes, 0, 0, tiled=True)  11.4 us
    pallas_call x6, Pallas kernels, call(): pl.pallas_call(kernel, out_shape=[jax.ShapeDtypeStruct(shape, dtype) for...  6.57 us
    ppermute x1, starting transfers between devices, on_device(): turned = lax.ppermute(ordered_half, ('y', 'x'), TURN)  4.89 us
  transfers between devices with their start and end apart: 7, of which 2 were waited for; matrix products, arithmetic and copies ran while one was open for 0% of the time, Pallas kernels for 2%

profile of v6, /device:TPU:2, one launch (start us, length us, event | category | flops | bytes accessed | tf_op | source)
XLA Modules:
  0.0 164.4 jit_solution(11773464566222717985)
XLA Ops:
  0.6 0.0 copy-start
  0.8 0.7 copy-done
  1.5 0.2 fusion.1
  1.7 4.9 %collective-permute-start.1 = (bf16[128,128]{0,1:T(8,128)(2,1)S(1)}, bf16[128,128]{0,1:T(8,128)(2,1)S(1)}, u32[]{:S(2)}, u32[]{:S(2)}) collective-permute-start(bf16[128,128]{0,1:T(8,128)(2,1)S(1)} %fusion.1), channel_id=1, source_target_pairs={{4,0},{132,2},{260,4},{388,6},{6,128},{134,130},{262,132},{390,134... | collective-permute-start | bytes 98312 | tf_op jit(solution)/shard_map/ppermute | solution.py:198
  6.6 1.8 %collective-permute-done.1 = bf16[128,128]{0,1:T(8,128)(2,1)S(1)} collective-permute-done((bf16[128,128]{0,1:T(8,128)(2,1)S(1)}, bf16[128,128]{0,1:T(8,128)(2,1)S(1)}, u32[]{:S(2)}, u32[]{:S(2)}) %collective-permute-start.1) | collective-permute-done | bytes 32800 | tf_op jit(solution)/shard_map/ppermute | solution.py:198
  8.5 0.1 copy.9
  8.6 0.8 broadcast_in_dim.2
  9.4 15.1 %all-to-all-start = ((bf16[8,128,128]{2,1,0:T(8,128)(2,1)}), bf16[8,128,128]{2,1,0:T(8,128)(2,1)S(1)}, u32[]{:S(2)}, u32[]{:S(2)}) async-start(bf16[8,128,128]{2,1,0:T(8,128)(2,1)} %broadcast_in_dim.2), calls=%async_computation | async-start | bytes 524288 | tf_op jit(solution)/shard_map/all_to_all | solution.py:20
  24.5 0.2 fusion.basis_ref
  24.7 0.1 pad_add_fusion.at_ref
  24.8 1.4 pack.1
  26.2 5.0 %collective-permute-start.3 = (bf16[336,896]{1,0:T(8,128)(2,1)}, bf16[336,896]{1,0:T(8,128)(2,1)S(1)}, u32[]{:S(2)}, u32[]{:S(2)}) collective-permute-start(bf16[336,896]{1,0:T(8,128)(2,1)} %get-tuple-element.18), channel_id=1, source_target_pairs={{0,256},{128,384},{256,0},{384,128},{1,257},{129,385},{257,1},{385... | collective-permute-start | bytes 1806344 | tf_op jit(solution)/shard_map/ppermute | solution.py:28
  31.3 1.9 %collective-permute-start = (bf16[256,1024]{1,0:T(8,128)(2,1)S(1)}, bf16[256,1024]{1,0:T(8,128)(2,1)S(1)}, u32[]{:S(2)}, u32[]{:S(2)}) collective-permute-start(bf16[256,1024]{1,0:T(8,128)(2,1)S(1)} %copy-done.2), channel_id=1, source_target_pairs={{0,1},{1,0},{2,3},{3,2},{4,5},{5,4},{6,7},{7,6},{8,9},{9,8},{10,11... | collective-permute-start | bytes 1572872 | tf_op jit(solution)/shard_map/ppermute | solution.py:218
  33.2 11.4 %all-to-all-done.own_ref = bf16[8,128,128]{2,1,0:T(8,128)(2,1)S(1)} async-done(((bf16[8,128,128]{2,1,0:T(8,128)(2,1)}), bf16[8,128,128]{2,1,0:T(8,128)(2,1)S(1)}, u32[]{:S(2)}, u32[]{:S(2)}) %all-to-all-start) | async-done | bytes 262176 | tf_op jit(solution)/shard_map/all_to_all | solution.py:20
  44.6 1.9 %collective-permute-start.2 = (bf16[8,128,128]{2,1,0:T(8,128)(2,1)S(1)}, bf16[8,128,128]{2,1,0:T(8,128)(2,1)S(1)}, u32[]{:S(2)}, u32[]{:S(2)}) collective-permute-start(bf16[8,128,128]{2,1,0:T(8,128)(2,1)S(1)} %all-to-all-done.own_ref), channel_id=1, source_target_pairs={{0,8},{8,0},{1,9},{9,1},{2,10},{10,2},{3,11},{11,3},{4,12},{12,4},... | collective-permute-start | bytes 786440 | tf_op jit(solution)/shard_map/ppermute | solution.py:200
  46.6 6.2 %collective-permute-start.4 = (bf16[336,896]{1,0:T(8,128)(2,1)}, bf16[336,896]{1,0:T(8,128)(2,1)S(1)}, u32[]{:S(2)}, u32[]{:S(2)}) collective-permute-start(bf16[336,896]{1,0:T(8,128)(2,1)} %copy-done.6), channel_id=1, source_target_pairs={{0,384},{128,0},{256,128},{384,256},{1,385},{129,1},{257,129},{385... | collective-permute-start | bytes 1806344 | tf_op jit(solution)/shard_map/ppermute | solution.py:28
  52.7 1.9 %collective-permute-start.5 = (bf16[336,896]{1,0:T(8,128)(2,1)}, bf16[336,896]{1,0:T(8,128)(2,1)S(1)}, u32[]{:S(2)}, u32[]{:S(2)}) collective-permute-start(bf16[336,896]{1,0:T(8,128)(2,1)} %copy-done.5), channel_id=1, source_target_pairs={{0,128},{128,256},{256,384},{384,0},{1,129},{129,257},{257,385},{3... | collective-permute-start | bytes 1806344 | tf_op jit(solution)/shard_map/ppermute | solution.py:28
  54.6 0.0 collective-permute-done.other_ref
  54.7 0.0 collective-permute-done.2.got_ref
  54.7 1.0 project.1
  55.7 0.0 collective-permute-done.3.refs_2_
  55.7 10.4 %all_to_all.25.summands_ref = f32[4,256,128]{2,1,0:T(8,128)S(1)} all-to-all(f32[4,256,128]{2,1,0:T(8,128)S(1)} %project.1), channel_id=1, replica_groups=mesh['y'=4,'h'=8,'l'=2,'x'=4,'c'=2] {'x'}, dimensions={0} | all-to-all | bytes 1048576 | tf_op jit(solution)/shard_map/all_to_all | solution.py:20
  66.1 0.6 round.1
  66.7 0.0 collective-permute-done.4.refs_3_
  66.7 14.3 %all_to_all.26 = bf16[8,256,128]{2,1,0:T(8,128)(2,1)S(1)} all-to-all(bf16[8,256,128]{2,1,0:T(8,128)(2,1)S(1)} %round.1), channel_id=1, replica_groups=mesh['y'=4,'h'=8,'l'=2,'x'=4,'c'=2] {'c','y'}, dimensions={0} | all-to-all | bytes 1048576 | tf_op jit(solution)/shard_map/all_to_all | solution.py:20
  81.0 1.3 partial.1
  82.3 32.4 %all_to_all.27.pieces_ref = bf16[16,16,896]{2,1,0:T(8,128)(2,1)S(1)} all-to-all(bf16[16,16,896]{2,1,0:T(8,128)(2,1)S(1)} %bitcast.12), channel_id=1, replica_groups=mesh['y'=4,'h'=8,'l'=2,'x'=4,'c'=2] {'h','l'}, dimensions={0} | all-to-all | bytes 917504 | tf_op jit(solution)/shard_map/all_to_all | solution.py:20
  114.7 0.8 sum_and_adam.1
  115.5 32.7 %all_gather.3.direction_ref = bf16[256,896]{1,0:T(8,128)(2,1)S(1)} all-gather(bf16[16,896]{1,0:T(8,128)(2,1)S(1)} %get-tuple-element.27), channel_id=1, replica_groups=mesh['y'=4,'h'=8,'l'=2,'x'=4,'c'=2] {'h','l'}, dimensions={0}, use_global_device_ids=true | all-gather | bytes 487424 | tf_op jit(solution)/shard_map/all_gather | solution.py:238
  148.2 1.0 update.1
  149.2 13.2 %all_to_all.28.arrived_ref = bf16[4,144,896]{2,1,0:T(8,128)(2,1)S(1)} all-to-all(bf16[4,144,896]{2,1,0:T(8,128)(2,1)S(1)} %update.1), channel_id=1, replica_groups=mesh['y'=4,'h'=8,'l'=2,'x'=4,'c'=2] {'y'}, dimensions={0} | all-to-all | bytes 2064384 | tf_op jit(solution)/shard_map/all_to_all | solution.py:20
  162.5 1.9 %finish.1 = (f32[4,3584]{1,0:T(4,128)}, f32[4,3584]{1,0:T(4,128)}, f32[128,3584]{1,0:T(8,128)}) custom-call(s32[3]{0:T(128)S(1)} %pad_add_fusion.at_ref, bf16[4,144,896]{2,1,0:T(8,128)(2,1)S(1)} %all_to_all.28.arrived_ref, f32[4,3584]{1,0:T(4,128)S(1)} %copy-done.4, f32[4,3584]{1,0:T(4,128)S(1)} %copy-done.3), custom_call_target="tpu_custom_call" | custom-call | tf_op jit(solution)/shard_map/finish/pallas_call | solution.py:32
  (24 shorter events, 0.1 us)
Async XLA Ops:
  0.6 0.8 copy-start
  0.6 24.1 %copy-start.3 = (f32[4,3584]{1,0:T(4,128)S(1)}, f32[4,3584]{1,0:T(4,128)}, u32[]{:S(2)}) copy-start(f32[4,3584]{1,0:T(4,128)} %second_ref.1) | copy-start | bytes 172036
  0.7 24.1 %copy-start.4 = (f32[4,3584]{1,0:T(4,128)S(1)}, f32[4,3584]{1,0:T(4,128)}, u32[]{:S(2)}) copy-start(f32[4,3584]{1,0:T(4,128)} %first_ref.1) | copy-start | bytes 172036
  0.7 24.1 %copy-start.1 = (bf16[256,3584]{1,0:T(8,128)(2,1)S(1)}, bf16[256,3584]{1,0:T(8,128)(2,1)}, u32[]{:S(2)}) copy-start(bf16[256,3584]{1,0:T(8,128)(2,1)} %grad_ref.1) | copy-start | bytes 5505028
  1.7 6.8 %collective-permute-start.1 = (bf16[128,128]{0,1:T(8,128)(2,1)S(1)}, bf16[128,128]{0,1:T(8,128)(2,1)S(1)}, u32[]{:S(2)}, u32[]{:S(2)}) collective-permute-start(bf16[128,128]{0,1:T(8,128)(2,1)S(1)} %fusion.1), channel_id=1, source_target_pairs={{4,0},{132,2},{260,4},{388,6},{6,128},{134,130},{262,132},{390,134... | collective-permute-start | bytes 98312 | tf_op jit(solution)/shard_map/ppermute | solution.py:198
  9.4 35.3 %all-to-all-start = ((bf16[8,128,128]{2,1,0:T(8,128)(2,1)}), bf16[8,128,128]{2,1,0:T(8,128)(2,1)S(1)}, u32[]{:S(2)}, u32[]{:S(2)}) async-start(bf16[8,128,128]{2,1,0:T(8,128)(2,1)} %broadcast_in_dim.2), calls=%async_computation | async-start | bytes 524288 | tf_op jit(solution)/shard_map/all_to_all | solution.py:20
  24.5 6.8 %copy-start.2 = (bf16[256,1024]{1,0:T(8,128)(2,1)S(1)}, bf16[256,1024]{1,0:T(8,128)(2,1)}, u32[]{:S(2)}) copy-start(bf16[256,1024]{1,0:T(8,128)(2,1)} %tokens_ref) | copy-start | bytes 1572868
  26.2 5.0 %copy-start.5 = (bf16[336,896]{1,0:T(8,128)(2,1)}, bf16[336,896]{1,0:T(8,128)(2,1)S(1)}, u32[]{:S(2)}) copy-start(bf16[336,896]{1,0:T(8,128)(2,1)S(1)} %get-tuple-element.21) | copy-start | bytes 1806340
  26.2 5.0 %copy-start.6 = (bf16[336,896]{1,0:T(8,128)(2,1)}, bf16[336,896]{1,0:T(8,128)(2,1)S(1)}, u32[]{:S(2)}) copy-start(bf16[336,896]{1,0:T(8,128)(2,1)S(1)} %get-tuple-element.20) | copy-start | bytes 1806340
  26.2 29.4 %collective-permute-start.3 = (bf16[336,896]{1,0:T(8,128)(2,1)}, bf16[336,896]{1,0:T(8,128)(2,1)S(1)}, u32[]{:S(2)}, u32[]{:S(2)}) collective-permute-start(bf16[336,896]{1,0:T(8,128)(2,1)} %get-tuple-element.18), channel_id=1, source_target_pairs={{0,256},{128,384},{256,0},{384,128},{1,257},{129,385},{257,1},{385... | collective-permute-start | bytes 1806344 | tf_op jit(solution)/shard_map/ppermute | solution.py:28
  31.3 23.4 %collective-permute-start = (bf16[256,1024]{1,0:T(8,128)(2,1)S(1)}, bf16[256,1024]{1,0:T(8,128)(2,1)S(1)}, u32[]{:S(2)}, u32[]{:S(2)}) collective-permute-start(bf16[256,1024]{1,0:T(8,128)(2,1)S(1)} %copy-done.2), channel_id=1, source_target_pairs={{0,1},{1,0},{2,3},{3,2},{4,5},{5,4},{6,7},{7,6},{8,9},{9,8},{10,11... | collective-permute-start | bytes 1572872 | tf_op jit(solution)/shard_map/ppermute | solution.py:218
  44.6 10.0 %collective-permute-start.2 = (bf16[8,128,128]{2,1,0:T(8,128)(2,1)S(1)}, bf16[8,128,128]{2,1,0:T(8,128)(2,1)S(1)}, u32[]{:S(2)}, u32[]{:S(2)}) collective-permute-start(bf16[8,128,128]{2,1,0:T(8,128)(2,1)S(1)} %all-to-all-done.own_ref), channel_id=1, source_target_pairs={{0,8},{8,0},{1,9},{9,1},{2,10},{10,2},{3,11},{11,3},{4,12},{12,4},... | collective-permute-start | bytes 786440 | tf_op jit(solution)/shard_map/ppermute | solution.py:200
  46.6 20.1 %collective-permute-start.4 = (bf16[336,896]{1,0:T(8,128)(2,1)}, bf16[336,896]{1,0:T(8,128)(2,1)S(1)}, u32[]{:S(2)}, u32[]{:S(2)}) collective-permute-start(bf16[336,896]{1,0:T(8,128)(2,1)} %copy-done.6), channel_id=1, source_target_pairs={{0,384},{128,0},{256,128},{384,256},{1,385},{129,1},{257,129},{385... | collective-permute-start | bytes 1806344 | tf_op jit(solution)/shard_map/ppermute | solution.py:28
  52.7 14.0 %collective-permute-start.5 = (bf16[336,896]{1,0:T(8,128)(2,1)}, bf16[336,896]{1,0:T(8,128)(2,1)S(1)}, u32[]{:S(2)}, u32[]{:S(2)}) collective-permute-start(bf16[336,896]{1,0:T(8,128)(2,1)} %copy-done.5), channel_id=1, source_target_pairs={{0,128},{128,256},{256,384},{384,0},{1,129},{129,257},{257,385},{3... | collective-permute-start | bytes 1806344 | tf_op jit(solution)/shard_map/ppermute | solution.py:28

commit v7 on v6

--- a/solution.py
+++ b/solution.py
@@ -28,6 +28,10 @@
     return lax.ppermute(x, "y", [(y, (y + step) % Y) for y in range(Y)])
 
 
+def send_one_core(x, step, c):
+    return lax.ppermute(x, ("y", "c"), [(y * C + c, (y + step) % Y * C + c) for y in range(Y)])
+
+
 def call(kernel, name, out, *args):
     return pl.pallas_call(
         kernel,
@@ -58,6 +62,11 @@
     new_first = 0.9 * first_moment + 0.1 * gradient
     new_second = 0.999 * second_moment + 0.001 * gradient * gradient
     return new_first, new_second
+
+
+def block_of(messages, d, rows, columns=slice(None)):
+    block = messages[d][rows, columns]
+    return block + messages[Y][rows, columns] if d == 1 else block
 
 
 def source(me, d):
@@ -113,18 +122,19 @@
 
 
 def partial_kernel(at_ref, projected_ref, *refs):
-    messages, out_ref = refs[:Y], refs[Y]
+    messages, out_ref = refs[: Y + 1], refs[Y + 1]
     count, half = projected_ref.shape[2:]
     for c in range(C):
         total = 0.0
         for d in range(Y):
             tokens = projected_ref[c, source(at_ref[0], d)]
-            total += lax.dot_general(tokens, messages[d][:count, :], (((0,), (0,)), ((), ())), preferred_element_type=f32)
+            total += lax.dot_general(tokens, block_of(messages, d, slice(0, count)), (((0,), (0,)), ((), ())), preferred_element_type=f32)
         out_ref[c * half : (c + 1) * half, :] = total.astype(bf16)
 
 
 def moments_of(at_ref, messages, ranks):
-    stack = jnp.concatenate([m[m.shape[0] - MOMENT_ROWS :, :] for m in messages], 0)
+    total = messages[0].shape[0]
+    stack = jnp.concatenate([block_of(messages, d, slice(total - MOMENT_ROWS, total)) for d in range(Y)], 0)
     shape = (6 * ranks, stack.shape[0])
     row, column = lax.broadcasted_iota(jnp.int32, shape, 0), lax.broadcasted_iota(jnp.int32, shape, 1)
     which, rank = row // ranks, row % ranks
@@ -138,7 +148,7 @@
 
 
 def adam_kernel(at_ref, pieces_ref, *refs):
-    messages, (gradient_ref, direction_ref) = refs[:Y], refs[Y:]
+    messages, (gradient_ref, direction_ref) = refs[: Y + 1], refs[Y + 1 :]
     gradient = jnp.sum(pieces_ref[...].astype(f32), axis=0)
     gradient_ref[...] = gradient
     first_scale = 1.0 - 0.9**STEP
@@ -149,7 +159,7 @@
 
 
 def update_kernel(at_ref, direction_ref, gradient_ref, *refs):
-    messages, out_ref = refs[:Y], refs[Y]
+    messages, out_ref = refs[: Y + 1], refs[Y + 1]
     count = messages[0].shape[0] - PACK - MOMENT_ROWS
     ranks = direction_ref.shape[0]
     rows = out_ref.shape[1] - 16
@@ -158,7 +168,7 @@
         pieces = []
         for k in range(3):
             take = min(PACK, rows - k * PACK)
-            pieces.append(messages[d][count : count + take, k * ranks : (k + 1) * ranks])
+            pieces.append(block_of(messages, d, slice(count, count + take), slice(k * ranks, (k + 1) * ranks)))
         basis = jnp.concatenate(pieces, 0)
         out_ref[source(at_ref[0], d), :rows, :] = jnp.dot(basis, direction, preferred_element_type=f32).astype(bf16)
     parts = jnp.concatenate(three_parts(gradient_ref[...]), 0).astype(bf16)
@@ -212,7 +222,8 @@
         compiler_params=pltpu.CompilerParams(vmem_limit_bytes=32 * 2**20),
         name="pack",
     )(at, ordered, moments, grad_out)
-    sent = {d: send(messages[d], d) for d in (2, 3, 1)}
+    sent = {2: send(messages[2], 2), 3: send(messages[3], 3), 1: send_one_core(messages[1], 1, 0)}
+    late = messages[1]
 
     tokens, first_message = lax.optimization_barrier((tokens, messages[0]))
     other = lax.ppermute(tokens, "c", [(0, 1), (1, 0)])
@@ -224,6 +235,9 @@
     projected, sent[3], sent[1] = lax.optimization_barrier((projected, sent[3], sent[1]))
     messages = [first_message, sent[1], sent[2], sent[3]]
     projected = exchange(projected, ("c", "y")).reshape(C, Y, count, half)
+    projected, late = lax.optimization_barrier((projected, late))
+    messages = messages + [send_one_core(late, 1, 1)]
+
 
     (partial,) = call(partial_kernel, "partial", [((ranks, part), bf16)], at, projected, *messages)
     pieces = exchange(partial.reshape(Z, ranks // Z, part), ("h", "l"))

time: 165 us -> 162 us (0.982)
  the two profiles are of different devices: /device:TPU:2 before, /device:TPU:1 now
where the time goes in v7:
time: 162 us
  blocking collectives  92.7 us (57%)
  starting transfers between devices  40.9 us (25%)
  waiting for transfers between devices  17.1 us (11%)
  Pallas kernels  8.02 us (5%)
  local copies, waits for them, and re-layouts  1.63 us (1%)
    all_to_all x4, blocking collectives, exchange(): return lax.all_to_all(x, axes, 0, 0, tiled=True)  67.9 us
    all_gather x1, blocking collectives, on_device(): direction = lax.all_gather(direction, ('h', 'l'), axis=0, tiled=True)  24.8 us
    all_to_all x1, starting transfers between devices, exchange(): return lax.all_to_all(x, axes, 0, 0, tiled=True)  15 us
    ppermute x2, starting transfers between devices, send(): return lax.ppermute(x, 'y', [(y, (y + step) % Y) for y in range(Y)])  10.1 us
    ppermute x2, waiting for transfers between devices, send_one_core(): lax.ppermute(x, ('y', 'c'), [(y * C + c, (y + step) % Y * C + c) for y in...  9.78 us
    pallas_call x6, Pallas kernels, call(): pl.pallas_call(kernel, out_shape=[jax.ShapeDtypeStruct(shape, dtype) for...  6.59 us
    all_to_all x1, waiting for transfers between devices, exchange(): return lax.all_to_all(x, axes, 0, 0, tiled=True)  6.22 us
    ppermute x1, starting transfers between devices, on_device(): turned = lax.ppermute(ordered_half, ('y', 'x'), TURN)  5.65 us
  transfers between devices with their start and end apart: 8, of which 3 were waited for; matrix products, arithmetic and copies ran while one was open for 0% of the time, Pallas kernels for 2%

profile of v7, /device:TPU:1, one launch (start us, length us, event | category | flops | bytes accessed | tf_op | source)
XLA Modules:
  0.0 161.8 jit_solution(14371755613671304572)
XLA Ops:
  0.6 0.0 copy-start
  0.8 0.7 copy-done
  1.5 0.2 fusion.1
  1.7 5.7 %collective-permute-start.1 = (bf16[128,128]{0,1:T(8,128)(2,1)S(1)}, bf16[128,128]{0,1:T(8,128)(2,1)S(1)}, u32[]{:S(2)}, u32[]{:S(2)}) collective-permute-start(bf16[128,128]{0,1:T(8,128)(2,1)S(1)} %fusion.1), channel_id=1, source_target_pairs={{4,0},{132,2},{260,4},{388,6},{6,128},{134,130},{262,132},{390,134... | collective-permute-start | bytes 98312 | tf_op jit(solution)/shard_map/ppermute | solution.py:208
  7.4 1.1 collective-permute-done.1
  8.5 0.1 copy.9
  8.6 0.8 broadcast_in_dim.2
  9.3 15.0 %all-to-all-start = ((bf16[8,128,128]{2,1,0:T(8,128)(2,1)}), bf16[8,128,128]{2,1,0:T(8,128)(2,1)S(1)}, u32[]{:S(2)}, u32[]{:S(2)}) async-start(bf16[8,128,128]{2,1,0:T(8,128)(2,1)} %broadcast_in_dim.2), calls=%async_computation | async-start | bytes 524288 | tf_op jit(solution)/shard_map/all_to_all | solution.py:20
  24.4 0.2 fusion.basis_ref
  24.6 0.1 pad_add_fusion.at_ref
  24.7 1.4 pack.1
  26.2 4.8 %collective-permute-start.3 = (bf16[336,896]{1,0:T(8,128)(2,1)}, bf16[336,896]{1,0:T(8,128)(2,1)S(1)}, u32[]{:S(2)}, u32[]{:S(2)}) collective-permute-start(bf16[336,896]{1,0:T(8,128)(2,1)} %get-tuple-element.20), channel_id=1, source_target_pairs={{0,256},{128,384},{256,0},{384,128},{1,257},{129,385},{257,1},{385... | collective-permute-start | bytes 1806344 | tf_op jit(solution)/shard_map/ppermute | solution.py:28
  31.0 4.3 %collective-permute-start = (bf16[256,1024]{1,0:T(8,128)(2,1)S(1)}, bf16[256,1024]{1,0:T(8,128)(2,1)S(1)}, u32[]{:S(2)}, u32[]{:S(2)}) collective-permute-start(bf16[256,1024]{1,0:T(8,128)(2,1)S(1)} %copy-done.2), channel_id=1, source_target_pairs={{0,1},{1,0},{2,3},{3,2},{4,5},{5,4},{6,7},{7,6},{8,9},{9,8},{10,11... | collective-permute-start | bytes 1572872 | tf_op jit(solution)/shard_map/ppermute | solution.py:229
  35.3 6.2 %all-to-all-done.own_ref = bf16[8,128,128]{2,1,0:T(8,128)(2,1)S(1)} async-done(((bf16[8,128,128]{2,1,0:T(8,128)(2,1)}), bf16[8,128,128]{2,1,0:T(8,128)(2,1)S(1)}, u32[]{:S(2)}, u32[]{:S(2)}) %all-to-all-start) | async-done | bytes 262176 | tf_op jit(solution)/shard_map/all_to_all | solution.py:20
  41.5 2.7 %collective-permute-start.2 = (bf16[8,128,128]{2,1,0:T(8,128)(2,1)S(1)}, bf16[8,128,128]{2,1,0:T(8,128)(2,1)S(1)}, u32[]{:S(2)}, u32[]{:S(2)}) collective-permute-start(bf16[8,128,128]{2,1,0:T(8,128)(2,1)S(1)} %all-to-all-done.own_ref), channel_id=1, source_target_pairs={{0,8},{8,0},{1,9},{9,1},{2,10},{10,2},{3,11},{11,3},{4,12},{12,4},... | collective-permute-start | bytes 786440 | tf_op jit(solution)/shard_map/ppermute | solution.py:210
  44.2 5.2 %collective-permute-start.4 = (bf16[336,896]{1,0:T(8,128)(2,1)}, bf16[336,896]{1,0:T(8,128)(2,1)S(1)}, u32[]{:S(2)}, u32[]{:S(2)}) collective-permute-start(bf16[336,896]{1,0:T(8,128)(2,1)} %copy-done.7), channel_id=1, source_target_pairs={{0,384},{128,0},{256,128},{384,256},{1,385},{129,1},{257,129},{385... | collective-permute-start | bytes 1806344 | tf_op jit(solution)/shard_map/ppermute | solution.py:28
  49.5 0.7 collective-permute-start.5
  50.2 0.0 collective-permute-done.other_ref
  50.2 0.0 collective-permute-done.2.got_ref
  50.2 1.0 project.1
  51.2 10.1 %all_to_all.25.summands_ref = f32[4,256,128]{2,1,0:T(8,128)S(1)} all-to-all(f32[4,256,128]{2,1,0:T(8,128)S(1)} %project.1), channel_id=1, replica_groups=mesh['y'=4,'h'=8,'l'=2,'x'=4,'c'=2] {'x'}, dimensions={0} | all-to-all | bytes 1048576 | tf_op jit(solution)/shard_map/all_to_all | solution.py:20
  61.3 0.6 round.1
  61.9 21.3 %all_to_all.26 = bf16[8,256,128]{2,1,0:T(8,128)(2,1)S(1)} all-to-all(bf16[8,256,128]{2,1,0:T(8,128)(2,1)S(1)} %round.1), channel_id=1, replica_groups=mesh['y'=4,'h'=8,'l'=2,'x'=4,'c'=2] {'c','y'}, dimensions={0} | all-to-all | bytes 1048576 | tf_op jit(solution)/shard_map/all_to_all | solution.py:20
  83.2 2.5 %collective-permute-start.6 = (bf16[336,896]{1,0:T(8,128)(2,1)S(1)}, bf16[336,896]{1,0:T(8,128)(2,1)S(1)}, u32[]{:S(2)}, u32[]{:S(2)}) collective-permute-start(bf16[336,896]{1,0:T(8,128)(2,1)S(1)} %copy-done.6), channel_id=1, source_target_pairs={{1,129},{129,257},{257,385},{385,1},{3,131},{131,259},{259,387},{3... | collective-permute-start | bytes 1806344 | tf_op jit(solution)/shard_map/ppermute | solution.py:32
  85.7 9.8 %collective-permute-done.6.refs_4_ = bf16[336,896]{1,0:T(8,128)(2,1)S(1)} collective-permute-done((bf16[336,896]{1,0:T(8,128)(2,1)S(1)}, bf16[336,896]{1,0:T(8,128)(2,1)S(1)}, u32[]{:S(2)}, u32[]{:S(2)}) %collective-permute-start.6) | collective-permute-done | bytes 602144 | tf_op jit(solution)/shard_map/ppermute | solution.py:32
  95.5 1.3 partial.1
  96.8 20.6 %all_to_all.27.pieces_ref = bf16[16,16,896]{2,1,0:T(8,128)(2,1)S(1)} all-to-all(bf16[16,16,896]{2,1,0:T(8,128)(2,1)S(1)} %bitcast.12), channel_id=1, replica_groups=mesh['y'=4,'h'=8,'l'=2,'x'=4,'c'=2] {'h','l'}, dimensions={0} | all-to-all | bytes 917504 | tf_op jit(solution)/shard_map/all_to_all | solution.py:20
  117.4 0.8 sum_and_adam.1
  118.2 24.8 %all_gather.3.direction_ref = bf16[256,896]{1,0:T(8,128)(2,1)S(1)} all-gather(bf16[16,896]{1,0:T(8,128)(2,1)S(1)} %get-tuple-element.31), channel_id=1, replica_groups=mesh['y'=4,'h'=8,'l'=2,'x'=4,'c'=2] {'h','l'}, dimensions={0}, use_global_device_ids=true | all-gather | bytes 487424 | tf_op jit(solution)/shard_map/all_gather | solution.py:252
  142.9 1.0 update.1
  144.0 16.0 %all_to_all.28.arrived_ref = bf16[4,144,896]{2,1,0:T(8,128)(2,1)S(1)} all-to-all(bf16[4,144,896]{2,1,0:T(8,128)(2,1)S(1)} %update.1), channel_id=1, replica_groups=mesh['y'=4,'h'=8,'l'=2,'x'=4,'c'=2] {'y'}, dimensions={0} | all-to-all | bytes 2064384 | tf_op jit(solution)/shard_map/all_to_all | solution.py:20
  159.9 1.9 %finish.1 = (f32[4,3584]{1,0:T(4,128)}, f32[4,3584]{1,0:T(4,128)}, f32[128,3584]{1,0:T(8,128)}) custom-call(s32[3]{0:T(128)S(1)} %pad_add_fusion.at_ref, bf16[4,144,896]{2,1,0:T(8,128)(2,1)S(1)} %all_to_all.28.arrived_ref, f32[4,3584]{1,0:T(4,128)S(1)} %copy-done.4, f32[4,3584]{1,0:T(4,128)S(1)} %copy-done.3), custom_call_target="tpu_custom_call" | custom-call | tf_op jit(solution)/shard_map/finish/pallas_call | solution.py:36
  (28 shorter events, 0.1 us)
Async XLA Ops:
  0.6 0.8 copy-start
  0.6 24.0 %copy-start.3 = (f32[4,3584]{1,0:T(4,128)S(1)}, f32[4,3584]{1,0:T(4,128)}, u32[]{:S(2)}) copy-start(f32[4,3584]{1,0:T(4,128)} %second_ref.1) | copy-start | bytes 172036
  0.7 24.0 %copy-start.4 = (f32[4,3584]{1,0:T(4,128)S(1)}, f32[4,3584]{1,0:T(4,128)}, u32[]{:S(2)}) copy-start(f32[4,3584]{1,0:T(4,128)} %first_ref.1) | copy-start | bytes 172036
  0.7 24.0 %copy-start.1 = (bf16[256,3584]{1,0:T(8,128)(2,1)S(1)}, bf16[256,3584]{1,0:T(8,128)(2,1)}, u32[]{:S(2)}) copy-start(bf16[256,3584]{1,0:T(8,128)(2,1)} %grad_ref.1) | copy-start | bytes 5505028
  1.7 6.8 %collective-permute-start.1 = (bf16[128,128]{0,1:T(8,128)(2,1)S(1)}, bf16[128,128]{0,1:T(8,128)(2,1)S(1)}, u32[]{:S(2)}, u32[]{:S(2)}) collective-permute-start(bf16[128,128]{0,1:T(8,128)(2,1)S(1)} %fusion.1), channel_id=1, source_target_pairs={{4,0},{132,2},{260,4},{388,6},{6,128},{134,130},{262,132},{390,134... | collective-permute-start | bytes 98312 | tf_op jit(solution)/shard_map/ppermute | solution.py:208
  9.3 32.2 %all-to-all-start = ((bf16[8,128,128]{2,1,0:T(8,128)(2,1)}), bf16[8,128,128]{2,1,0:T(8,128)(2,1)S(1)}, u32[]{:S(2)}, u32[]{:S(2)}) async-start(bf16[8,128,128]{2,1,0:T(8,128)(2,1)} %broadcast_in_dim.2), calls=%async_computation | async-start | bytes 524288 | tf_op jit(solution)/shard_map/all_to_all | solution.py:20
  24.4 6.6 %copy-start.2 = (bf16[256,1024]{1,0:T(8,128)(2,1)S(1)}, bf16[256,1024]{1,0:T(8,128)(2,1)}, u32[]{:S(2)}) copy-start(bf16[256,1024]{1,0:T(8,128)(2,1)} %tokens_ref) | copy-start | bytes 1572868
  26.1 4.9 %copy-start.5 = (bf16[336,896]{1,0:T(8,128)(2,1)}, bf16[336,896]{1,0:T(8,128)(2,1)S(1)}, u32[]{:S(2)}) copy-start(bf16[336,896]{1,0:T(8,128)(2,1)S(1)} %get-tuple-element.30) | copy-start | bytes 1806340
  26.1 4.9 %copy-start.7 = (bf16[336,896]{1,0:T(8,128)(2,1)}, bf16[336,896]{1,0:T(8,128)(2,1)S(1)}, u32[]{:S(2)}) copy-start(bf16[336,896]{1,0:T(8,128)(2,1)S(1)} %get-tuple-element.22) | copy-start | bytes 1806340
  26.2 25.0 %collective-permute-start.3 = (bf16[336,896]{1,0:T(8,128)(2,1)}, bf16[336,896]{1,0:T(8,128)(2,1)S(1)}, u32[]{:S(2)}, u32[]{:S(2)}) collective-permute-start(bf16[336,896]{1,0:T(8,128)(2,1)} %get-tuple-element.20), channel_id=1, source_target_pairs={{0,256},{128,384},{256,0},{384,128},{1,257},{129,385},{257,1},{385... | collective-permute-start | bytes 1806344 | tf_op jit(solution)/shard_map/ppermute | solution.py:28
  31.0 19.2 %collective-permute-start = (bf16[256,1024]{1,0:T(8,128)(2,1)S(1)}, bf16[256,1024]{1,0:T(8,128)(2,1)S(1)}, u32[]{:S(2)}, u32[]{:S(2)}) collective-permute-start(bf16[256,1024]{1,0:T(8,128)(2,1)S(1)} %copy-done.2), channel_id=1, source_target_pairs={{0,1},{1,0},{2,3},{3,2},{4,5},{5,4},{6,7},{7,6},{8,9},{9,8},{10,11... | collective-permute-start | bytes 1572872 | tf_op jit(solution)/shard_map/ppermute | solution.py:229
  41.5 8.6 %collective-permute-start.2 = (bf16[8,128,128]{2,1,0:T(8,128)(2,1)S(1)}, bf16[8,128,128]{2,1,0:T(8,128)(2,1)S(1)}, u32[]{:S(2)}, u32[]{:S(2)}) collective-permute-start(bf16[8,128,128]{2,1,0:T(8,128)(2,1)S(1)} %all-to-all-done.own_ref), channel_id=1, source_target_pairs={{0,8},{8,0},{1,9},{9,1},{2,10},{10,2},{3,11},{11,3},{4,12},{12,4},... | collective-permute-start | bytes 786440 | tf_op jit(solution)/shard_map/ppermute | solution.py:210
  44.2 17.6 %collective-permute-start.4 = (bf16[336,896]{1,0:T(8,128)(2,1)}, bf16[336,896]{1,0:T(8,128)(2,1)S(1)}, u32[]{:S(2)}, u32[]{:S(2)}) collective-permute-start(bf16[336,896]{1,0:T(8,128)(2,1)} %copy-done.7), channel_id=1, source_target_pairs={{0,384},{128,0},{256,128},{384,256},{1,385},{129,1},{257,129},{385... | collective-permute-start | bytes 1806344 | tf_op jit(solution)/shard_map/ppermute | solution.py:28
  49.5 12.4 %collective-permute-start.5 = (bf16[336,896]{1,0:T(8,128)(2,1)}, bf16[336,896]{1,0:T(8,128)(2,1)S(1)}, u32[]{:S(2)}, u32[]{:S(2)}) collective-permute-start(bf16[336,896]{1,0:T(8,128)(2,1)} %copy-done.5), channel_id=1, source_target_pairs={{0,128},{128,256},{256,384},{384,0},{2,130},{130,258},{258,386},{3... | collective-permute-start | bytes 1806344 | tf_op jit(solution)/shard_map/ppermute | solution.py:32
  51.2 32.0 %copy-start.6 = (bf16[336,896]{1,0:T(8,128)(2,1)S(1)}, bf16[336,896]{1,0:T(8,128)(2,1)}, u32[]{:S(2)}) copy-start(bf16[336,896]{1,0:T(8,128)(2,1)} %copy-done.5) | copy-start | bytes 1806340
  83.2 12.3 %collective-permute-start.6 = (bf16[336,896]{1,0:T(8,128)(2,1)S(1)}, bf16[336,896]{1,0:T(8,128)(2,1)S(1)}, u32[]{:S(2)}, u32[]{:S(2)}) collective-permute-start(bf16[336,896]{1,0:T(8,128)(2,1)S(1)} %copy-done.6), channel_id=1, source_target_pairs={{1,129},{129,257},{257,385},{385,1},{3,131},{131,259},{259,387},{3... | collective-permute-start | bytes 1806344 | tf_op jit(solution)/shard_map/ppermute | solution.py:32

commit v8 on v7

--- a/solution.py
+++ b/solution.py
@@ -66,7 +66,7 @@
 
 def block_of(messages, d, rows, columns=slice(None)):
     block = messages[d][rows, columns]
-    return block + messages[Y][rows, columns] if d == 1 else block
+    return block + messages[Y][rows, columns] if d == 3 else block
 
 
 def source(me, d):
@@ -222,8 +222,8 @@
         compiler_params=pltpu.CompilerParams(vmem_limit_bytes=32 * 2**20),
         name="pack",
     )(at, ordered, moments, grad_out)
-    sent = {2: send(messages[2], 2), 3: send(messages[3], 3), 1: send_one_core(messages[1], 1, 0)}
-    late = messages[1]
+    sent = {2: send(messages[2], 2), 1: send(messages[1], 1), 3: send_one_core(messages[3], 3, 0)}
+    late = messages[3]
 
     tokens, first_message = lax.optimization_barrier((tokens, messages[0]))
     other = lax.ppermute(tokens, "c", [(0, 1), (1, 0)])
@@ -232,11 +232,11 @@
     summands, sent[2] = lax.optimization_barrier((summands, sent[2]))
     summands = exchange(summands, "x")
     (projected,) = call(round_kernel, "round", [((C * Y, count, half), bf16)], at, summands)
-    projected, sent[3], sent[1] = lax.optimization_barrier((projected, sent[3], sent[1]))
+    projected, sent[1], sent[3] = lax.optimization_barrier((projected, sent[1], sent[3]))
     messages = [first_message, sent[1], sent[2], sent[3]]
     projected = exchange(projected, ("c", "y")).reshape(C, Y, count, half)
     projected, late = lax.optimization_barrier((projected, late))
-    messages = messages + [send_one_core(late, 1, 1)]
+    messages = messages + [send_one_core(late, 3, 1)]
 
 
     (partial,) = call(partial_kernel, "partial", [((ranks, part), bf16)], at, projected, *messages)

time: 162 us -> 162 us (level)
  blocking collectives: 92.7 us -> 95.7 us
  waiting for transfers between devices: 17.1 us -> 15.3 us
    all_to_all x4, blocking collectives: 67.9 us -> 72.7 us  [exchange(): return lax.all_to_all(x, axes, 0, 0, tiled=True)]
    all_gather x1, blocking collectives: 24.8 us -> 22.9 us  [on_device(): direction = lax.all_gather(direction, ('h', 'l'), axis=0, tiled=True)]
    ppermute x2, waiting for transfers between devices: 9.78 us -> 8.02 us  [send_one_core(): lax.ppermute(x, ('y', 'c'), [(y * C + c, (y + step) % Y * C + c) for y in...]
where the time goes in v8:
time: 162 us
  blocking collectives  95.7 us (59%)
  starting transfers between devices  39.7 us (25%)
  waiting for transfers between devices  15.3 us (9%)
  Pallas kernels  8.02 us (5%)
  local copies, waits for them, and re-layouts  1.63 us (1%)
    all_to_all x4, blocking collectives, exchange(): return lax.all_to_all(x, axes, 0, 0, tiled=True)  72.7 us
    all_gather x1, blocking collectives, on_device(): direction = lax.all_gather(direction, ('h', 'l'), axis=0, tiled=True)  22.9 us
    all_to_all x1, starting transfers between devices, exchange(): return lax.all_to_all(x, axes, 0, 0, tiled=True)  15 us
    ppermute x2, starting transfers between devices, send(): return lax.ppermute(x, 'y', [(y, (y + step) % Y) for y in range(Y)])  8.63 us
    ppermute x2, waiting for transfers between devices, send_one_core(): lax.ppermute(x, ('y', 'c'), [(y * C + c, (y + step) % Y * C + c) for y in...  8.02 us
    pallas_call x6, Pallas kernels, call(): pl.pallas_call(kernel, out_shape=[jax.ShapeDtypeStruct(shape, dtype) for...  6.58 us
    all_to_all x1, waiting for transfers between devices, exchange(): return lax.all_to_all(x, axes, 0, 0, tiled=True)  6.22 us
    ppermute x1, starting transfers between devices, on_device(): turned = lax.ppermute(ordered_half, ('y', 'x'), TURN)  5.65 us
  transfers between devices with their start and end apart: 8, of which 3 were waited for; matrix products, arithmetic and copies ran while one was open for 0% of the time, Pallas kernels for 2%

profile of v8, /device:TPU:1, one launch (start us, length us, event | category | flops | bytes accessed | tf_op | source)
XLA Modules:
  0.0 161.9 jit_solution(2000196811947067358)
XLA Ops:
  0.6 0.0 copy-start
  0.8 0.7 copy-done
  1.5 0.2 fusion.1
  1.7 5.7 %collective-permute-start.1 = (bf16[128,128]{0,1:T(8,128)(2,1)S(1)}, bf16[128,128]{0,1:T(8,128)(2,1)S(1)}, u32[]{:S(2)}, u32[]{:S(2)}) collective-permute-start(bf16[128,128]{0,1:T(8,128)(2,1)S(1)} %fusion.1), channel_id=1, source_target_pairs={{4,0},{132,2},{260,4},{388,6},{6,128},{134,130},{262,132},{390,134... | collective-permute-start | bytes 98312 | tf_op jit(solution)/shard_map/ppermute | solution.py:208
  7.4 1.1 collective-permute-done.1
  8.5 0.1 copy.9
  8.6 0.8 broadcast_in_dim.2
  9.3 15.0 %all-to-all-start = ((bf16[8,128,128]{2,1,0:T(8,128)(2,1)}), bf16[8,128,128]{2,1,0:T(8,128)(2,1)S(1)}, u32[]{:S(2)}, u32[]{:S(2)}) async-start(bf16[8,128,128]{2,1,0:T(8,128)(2,1)} %broadcast_in_dim.2), calls=%async_computation | async-start | bytes 524288 | tf_op jit(solution)/shard_map/all_to_all | solution.py:20
  24.4 0.2 fusion.basis_ref
  24.6 0.1 pad_add_fusion.at_ref
  24.7 1.4 pack.1
  26.2 4.8 %collective-permute-start.3 = (bf16[336,896]{1,0:T(8,128)(2,1)}, bf16[336,896]{1,0:T(8,128)(2,1)S(1)}, u32[]{:S(2)}, u32[]{:S(2)}) collective-permute-start(bf16[336,896]{1,0:T(8,128)(2,1)} %get-tuple-element.20), channel_id=1, source_target_pairs={{0,256},{128,384},{256,0},{384,128},{1,257},{129,385},{257,1},{385... | collective-permute-start | bytes 1806344 | tf_op jit(solution)/shard_map/ppermute | solution.py:28
  31.0 4.3 %collective-permute-start = (bf16[256,1024]{1,0:T(8,128)(2,1)S(1)}, bf16[256,1024]{1,0:T(8,128)(2,1)S(1)}, u32[]{:S(2)}, u32[]{:S(2)}) collective-permute-start(bf16[256,1024]{1,0:T(8,128)(2,1)S(1)} %copy-done.2), channel_id=1, source_target_pairs={{0,1},{1,0},{2,3},{3,2},{4,5},{5,4},{6,7},{7,6},{8,9},{9,8},{10,11... | collective-permute-start | bytes 1572872 | tf_op jit(solution)/shard_map/ppermute | solution.py:229
  35.3 6.2 %all-to-all-done.own_ref = bf16[8,128,128]{2,1,0:T(8,128)(2,1)S(1)} async-done(((bf16[8,128,128]{2,1,0:T(8,128)(2,1)}), bf16[8,128,128]{2,1,0:T(8,128)(2,1)S(1)}, u32[]{:S(2)}, u32[]{:S(2)}) %all-to-all-start) | async-done | bytes 262176 | tf_op jit(solution)/shard_map/all_to_all | solution.py:20
  41.5 2.7 %collective-permute-start.2 = (bf16[8,128,128]{2,1,0:T(8,128)(2,1)S(1)}, bf16[8,128,128]{2,1,0:T(8,128)(2,1)S(1)}, u32[]{:S(2)}, u32[]{:S(2)}) collective-permute-start(bf16[8,128,128]{2,1,0:T(8,128)(2,1)S(1)} %all-to-all-done.own_ref), channel_id=1, source_target_pairs={{0,8},{8,0},{1,9},{9,1},{2,10},{10,2},{3,11},{11,3},{4,12},{12,4},... | collective-permute-start | bytes 786440 | tf_op jit(solution)/shard_map/ppermute | solution.py:210
  44.2 3.8 %collective-permute-start.4 = (bf16[336,896]{1,0:T(8,128)(2,1)}, bf16[336,896]{1,0:T(8,128)(2,1)S(1)}, u32[]{:S(2)}, u32[]{:S(2)}) collective-permute-start(bf16[336,896]{1,0:T(8,128)(2,1)} %copy-done.7), channel_id=1, source_target_pairs={{0,128},{128,256},{256,384},{384,0},{1,129},{129,257},{257,385},{3... | collective-permute-start | bytes 1806344 | tf_op jit(solution)/shard_map/ppermute | solution.py:28
  48.0 0.7 collective-permute-start.5
  48.7 0.0 collective-permute-done.other_ref
  48.8 1.0 project.1
  49.8 0.0 collective-permute-done.3.refs_2_
  49.8 11.1 %all_to_all.25.summands_ref = f32[4,256,128]{2,1,0:T(8,128)S(1)} all-to-all(f32[4,256,128]{2,1,0:T(8,128)S(1)} %project.1), channel_id=1, replica_groups=mesh['y'=4,'h'=8,'l'=2,'x'=4,'c'=2] {'x'}, dimensions={0} | all-to-all | bytes 1048576 | tf_op jit(solution)/shard_map/all_to_all | solution.py:20
  60.9 0.6 round.1
  61.5 21.7 %all_to_all.26 = bf16[8,256,128]{2,1,0:T(8,128)(2,1)S(1)} all-to-all(bf16[8,256,128]{2,1,0:T(8,128)(2,1)S(1)} %round.1), channel_id=1, replica_groups=mesh['y'=4,'h'=8,'l'=2,'x'=4,'c'=2] {'c','y'}, dimensions={0} | all-to-all | bytes 1048576 | tf_op jit(solution)/shard_map/all_to_all | solution.py:20
  83.2 2.7 %collective-permute-start.6 = (bf16[336,896]{1,0:T(8,128)(2,1)S(1)}, bf16[336,896]{1,0:T(8,128)(2,1)S(1)}, u32[]{:S(2)}, u32[]{:S(2)}) collective-permute-start(bf16[336,896]{1,0:T(8,128)(2,1)S(1)} %copy-done.6), channel_id=1, source_target_pairs={{1,385},{129,1},{257,129},{385,257},{3,387},{131,3},{259,131},{387... | collective-permute-start | bytes 1806344 | tf_op jit(solution)/shard_map/ppermute | solution.py:32
  85.9 8.0 %collective-permute-done.6.refs_4_ = bf16[336,896]{1,0:T(8,128)(2,1)S(1)} collective-permute-done((bf16[336,896]{1,0:T(8,128)(2,1)S(1)}, bf16[336,896]{1,0:T(8,128)(2,1)S(1)}, u32[]{:S(2)}, u32[]{:S(2)}) %collective-permute-start.6) | collective-permute-done | bytes 602144 | tf_op jit(solution)/shard_map/ppermute | solution.py:32
  94.0 1.3 partial.1
  95.3 22.6 %all_to_all.27.pieces_ref = bf16[16,16,896]{2,1,0:T(8,128)(2,1)S(1)} all-to-all(bf16[16,16,896]{2,1,0:T(8,128)(2,1)S(1)} %bitcast.12), channel_id=1, replica_groups=mesh['y'=4,'h'=8,'l'=2,'x'=4,'c'=2] {'h','l'}, dimensions={0} | all-to-all | bytes 917504 | tf_op jit(solution)/shard_map/all_to_all | solution.py:20
  117.8 0.8 sum_and_adam.1
  118.6 22.9 %all_gather.3.direction_ref = bf16[256,896]{1,0:T(8,128)(2,1)S(1)} all-gather(bf16[16,896]{1,0:T(8,128)(2,1)S(1)} %get-tuple-element.31), channel_id=1, replica_groups=mesh['y'=4,'h'=8,'l'=2,'x'=4,'c'=2] {'h','l'}, dimensions={0}, use_global_device_ids=true | all-gather | bytes 487424 | tf_op jit(solution)/shard_map/all_gather | solution.py:252
  141.6 1.0 update.1
  142.6 17.3 %all_to_all.28.arrived_ref = bf16[4,144,896]{2,1,0:T(8,128)(2,1)S(1)} all-to-all(bf16[4,144,896]{2,1,0:T(8,128)(2,1)S(1)} %update.1), channel_id=1, replica_groups=mesh['y'=4,'h'=8,'l'=2,'x'=4,'c'=2] {'y'}, dimensions={0} | all-to-all | bytes 2064384 | tf_op jit(solution)/shard_map/all_to_all | solution.py:20
  159.9 1.9 %finish.1 = (f32[4,3584]{1,0:T(4,128)}, f32[4,3584]{1,0:T(4,128)}, f32[128,3584]{1,0:T(8,128)}) custom-call(s32[3]{0:T(128)S(1)} %pad_add_fusion.at_ref, bf16[4,144,896]{2,1,0:T(8,128)(2,1)S(1)} %all_to_all.28.arrived_ref, f32[4,3584]{1,0:T(4,128)S(1)} %copy-done.4, f32[4,3584]{1,0:T(4,128)S(1)} %copy-done.3), custom_call_target="tpu_custom_call" | custom-call | tf_op jit(solution)/shard_map/finish/pallas_call | solution.py:36
  (28 shorter events, 0.1 us)
Async XLA Ops:
  0.6 0.8 copy-start
  0.6 24.0 %copy-start.3 = (f32[4,3584]{1,0:T(4,128)S(1)}, f32[4,3584]{1,0:T(4,128)}, u32[]{:S(2)}) copy-start(f32[4,3584]{1,0:T(4,128)} %second_ref.1) | copy-start | bytes 172036
  0.7 24.0 %copy-start.4 = (f32[4,3584]{1,0:T(4,128)S(1)}, f32[4,3584]{1,0:T(4,128)}, u32[]{:S(2)}) copy-start(f32[4,3584]{1,0:T(4,128)} %first_ref.1) | copy-start | bytes 172036
  0.7 24.0 %copy-start.1 = (bf16[256,3584]{1,0:T(8,128)(2,1)S(1)}, bf16[256,3584]{1,0:T(8,128)(2,1)}, u32[]{:S(2)}) copy-start(bf16[256,3584]{1,0:T(8,128)(2,1)} %grad_ref.1) | copy-start | bytes 5505028
  1.7 6.8 %collective-permute-start.1 = (bf16[128,128]{0,1:T(8,128)(2,1)S(1)}, bf16[128,128]{0,1:T(8,128)(2,1)S(1)}, u32[]{:S(2)}, u32[]{:S(2)}) collective-permute-start(bf16[128,128]{0,1:T(8,128)(2,1)S(1)} %fusion.1), channel_id=1, source_target_pairs={{4,0},{132,2},{260,4},{388,6},{6,128},{134,130},{262,132},{390,134... | collective-permute-start | bytes 98312 | tf_op jit(solution)/shard_map/ppermute | solution.py:208
  9.3 32.2 %all-to-all-start = ((bf16[8,128,128]{2,1,0:T(8,128)(2,1)}), bf16[8,128,128]{2,1,0:T(8,128)(2,1)S(1)}, u32[]{:S(2)}, u32[]{:S(2)}) async-start(bf16[8,128,128]{2,1,0:T(8,128)(2,1)} %broadcast_in_dim.2), calls=%async_computation | async-start | bytes 524288 | tf_op jit(solution)/shard_map/all_to_all | solution.py:20
  24.4 6.6 %copy-start.2 = (bf16[256,1024]{1,0:T(8,128)(2,1)S(1)}, bf16[256,1024]{1,0:T(8,128)(2,1)}, u32[]{:S(2)}) copy-start(bf16[256,1024]{1,0:T(8,128)(2,1)} %tokens_ref) | copy-start | bytes 1572868
  26.1 4.9 %copy-start.5 = (bf16[336,896]{1,0:T(8,128)(2,1)}, bf16[336,896]{1,0:T(8,128)(2,1)S(1)}, u32[]{:S(2)}) copy-start(bf16[336,896]{1,0:T(8,128)(2,1)S(1)} %get-tuple-element.30) | copy-start | bytes 1806340
  26.1 4.9 %copy-start.7 = (bf16[336,896]{1,0:T(8,128)(2,1)}, bf16[336,896]{1,0:T(8,128)(2,1)S(1)}, u32[]{:S(2)}) copy-start(bf16[336,896]{1,0:T(8,128)(2,1)S(1)} %get-tuple-element.22) | copy-start | bytes 1806340
  26.2 23.6 %collective-permute-start.3 = (bf16[336,896]{1,0:T(8,128)(2,1)}, bf16[336,896]{1,0:T(8,128)(2,1)S(1)}, u32[]{:S(2)}, u32[]{:S(2)}) collective-permute-start(bf16[336,896]{1,0:T(8,128)(2,1)} %get-tuple-element.20), channel_id=1, source_target_pairs={{0,256},{128,384},{256,0},{384,128},{1,257},{129,385},{257,1},{385... | collective-permute-start | bytes 1806344 | tf_op jit(solution)/shard_map/ppermute | solution.py:28
  31.0 17.7 %collective-permute-start = (bf16[256,1024]{1,0:T(8,128)(2,1)S(1)}, bf16[256,1024]{1,0:T(8,128)(2,1)S(1)}, u32[]{:S(2)}, u32[]{:S(2)}) collective-permute-start(bf16[256,1024]{1,0:T(8,128)(2,1)S(1)} %copy-done.2), channel_id=1, source_target_pairs={{0,1},{1,0},{2,3},{3,2},{4,5},{5,4},{6,7},{7,6},{8,9},{9,8},{10,11... | collective-permute-start | bytes 1572872 | tf_op jit(solution)/shard_map/ppermute | solution.py:229
  41.5 7.2 %collective-permute-start.2 = (bf16[8,128,128]{2,1,0:T(8,128)(2,1)S(1)}, bf16[8,128,128]{2,1,0:T(8,128)(2,1)S(1)}, u32[]{:S(2)}, u32[]{:S(2)}) collective-permute-start(bf16[8,128,128]{2,1,0:T(8,128)(2,1)S(1)} %all-to-all-done.own_ref), channel_id=1, source_target_pairs={{0,8},{8,0},{1,9},{9,1},{2,10},{10,2},{3,11},{11,3},{4,12},{12,4},... | collective-permute-start | bytes 786440 | tf_op jit(solution)/shard_map/ppermute | solution.py:210
  44.2 17.3 %collective-permute-start.4 = (bf16[336,896]{1,0:T(8,128)(2,1)}, bf16[336,896]{1,0:T(8,128)(2,1)S(1)}, u32[]{:S(2)}, u32[]{:S(2)}) collective-permute-start(bf16[336,896]{1,0:T(8,128)(2,1)} %copy-done.7), channel_id=1, source_target_pairs={{0,128},{128,256},{256,384},{384,0},{1,129},{129,257},{257,385},{3... | collective-permute-start | bytes 1806344 | tf_op jit(solution)/shard_map/ppermute | solution.py:28
  48.0 13.5 %collective-permute-start.5 = (bf16[336,896]{1,0:T(8,128)(2,1)}, bf16[336,896]{1,0:T(8,128)(2,1)S(1)}, u32[]{:S(2)}, u32[]{:S(2)}) collective-permute-start(bf16[336,896]{1,0:T(8,128)(2,1)} %copy-done.5), channel_id=1, source_target_pairs={{0,384},{128,0},{256,128},{384,256},{2,386},{130,2},{258,130},{386... | collective-permute-start | bytes 1806344 | tf_op jit(solution)/shard_map/ppermute | solution.py:32
  49.8 33.5 %copy-start.6 = (bf16[336,896]{1,0:T(8,128)(2,1)S(1)}, bf16[336,896]{1,0:T(8,128)(2,1)}, u32[]{:S(2)}) copy-start(bf16[336,896]{1,0:T(8,128)(2,1)} %copy-done.5) | copy-start | bytes 1806340
  83.2 10.7 %collective-permute-start.6 = (bf16[336,896]{1,0:T(8,128)(2,1)S(1)}, bf16[336,896]{1,0:T(8,128)(2,1)S(1)}, u32[]{:S(2)}, u32[]{:S(2)}) collective-permute-start(bf16[336,896]{1,0:T(8,128)(2,1)S(1)} %copy-done.6), channel_id=1, source_target_pairs={{1,385},{129,1},{257,129},{385,257},{3,387},{131,3},{259,131},{387... | collective-permute-start | bytes 1806344 | tf_op jit(solution)/shard_map/ppermute | solution.py:32

commit v9 on v8

--- a/solution.py
+++ b/solution.py
@@ -121,15 +121,25 @@
         out_ref[i] = total
 
 
-def partial_kernel(at_ref, projected_ref, *refs):
-    messages, out_ref = refs[: Y + 1], refs[Y + 1]
+def early_kernel(at_ref, projected_ref, *refs):
+    messages, out_ref = refs[:Y], refs[Y]
     count, half = projected_ref.shape[2:]
     for c in range(C):
         total = 0.0
         for d in range(Y):
             tokens = projected_ref[c, source(at_ref[0], d)]
-            total += lax.dot_general(tokens, block_of(messages, d, slice(0, count)), (((0,), (0,)), ((), ())), preferred_element_type=f32)
-        out_ref[c * half : (c + 1) * half, :] = total.astype(bf16)
+            grads = messages[d][:count, :]
+            total += lax.dot_general(tokens, grads, (((0,), (0,)), ((), ())), preferred_element_type=f32)
+        out_ref[c * half : (c + 1) * half, :] = total
+
+
+def late_kernel(at_ref, early_ref, projected_ref, late_ref, out_ref):
+    count, half = projected_ref.shape[2:]
+    for c in range(C):
+        tokens = projected_ref[c, source(at_ref[0], 3)]
+        total = lax.dot_general(tokens, late_ref[:count, :], (((0,), (0,)), ((), ())), preferred_element_type=f32)
+        rows = slice(c * half, (c + 1) * half)
+        out_ref[rows, :] = (early_ref[rows, :] + total).astype(bf16)
 
 
 def moments_of(at_ref, messages, ranks):
@@ -239,7 +249,8 @@
     messages = messages + [send_one_core(late, 3, 1)]
 
 
-    (partial,) = call(partial_kernel, "partial", [((ranks, part), bf16)], at, projected, *messages)
+    (early,) = call(early_kernel, "early", [((ranks, part), f32)], at, projected, *messages[:Y])
+    (partial,) = call(late_kernel, "partial", [((ranks, part), bf16)], at, early, projected, messages[Y])
     pieces = exchange(partial.reshape(Z, ranks // Z, part), ("h", "l"))
     gradient, direction = call(
         adam_kernel,

time: 162 us -> 163 us (level)
    pallas_call x6 -> x7, Pallas kernels: 6.58 us -> 7.46 us  [call(): pl.pallas_call(kernel, out_shape=[jax.ShapeDtypeStruct(shape, dtype) for...]
  transfers between devices with their start and end apart: 8 -> 8, of which waited for: 3 -> 3; matrix products, arithmetic and copies ran while one was open for 0% -> 0% of each run, Pallas kernels for 2% -> 3%
where the time goes in v9:
time: 163 us; the launch traced here: 162 us
  blocking collectives  96.5 us (59%)
  starting transfers between devices  39.7 us (24%)
  waiting for transfers between devices  14 us (9%)
  Pallas kernels  8.89 us (5%)
    all_to_all x4, blocking collectives, exchange(): return lax.all_to_all(x, axes, 0, 0, tiled=True)  72.1 us
    all_gather x1, blocking collectives, on_device(): direction = lax.all_gather(direction, ('h', 'l'), axis=0, tiled=True)  24.3 us
    all_to_all x1, starting transfers between devices, exchange(): return lax.all_to_all(x, axes, 0, 0, tiled=True)  15 us
    ppermute x2, starting transfers between devices, send(): return lax.ppermute(x, 'y', [(y, (y + step) % Y) for y in range(Y)])  8.63 us
    pallas_call x7, Pallas kernels, call(): pl.pallas_call(kernel, out_shape=[jax.ShapeDtypeStruct(shape, dtype) for...  7.46 us
    ppermute x2, waiting for transfers between devices, send_one_core(): lax.ppermute(x, ('y', 'c'), [(y * C + c, (y + step) % Y * C + c) for y in...  6.72 us
    all_to_all x1, waiting for transfers between devices, exchange(): return lax.all_to_all(x, axes, 0, 0, tiled=True)  6.22 us
    ppermute x1, starting transfers between devices, on_device(): turned = lax.ppermute(ordered_half, ('y', 'x'), TURN)  5.65 us
  transfers between devices with their start and end apart: 8, of which 3 were waited for; matrix products, arithmetic and copies ran while one was open for 0% of the time, Pallas kernels for 3%

profile of v9, /device:TPU:1, one launch (start us, length us, event | category | flops | bytes accessed | tf_op | source)
XLA Modules:
  0.0 162.2 jit_solution(11308149815382205427)
XLA Ops:
  0.6 0.0 copy-start
  0.8 0.7 copy-done
  1.5 0.2 fusion.1
  1.7 5.7 %collective-permute-start.1 = (bf16[128,128]{0,1:T(8,128)(2,1)S(1)}, bf16[128,128]{0,1:T(8,128)(2,1)S(1)}, u32[]{:S(2)}, u32[]{:S(2)}) collective-permute-start(bf16[128,128]{0,1:T(8,128)(2,1)S(1)} %fusion.1), channel_id=1, source_target_pairs={{4,0},{132,2},{260,4},{388,6},{6,128},{134,130},{262,132},{390,134... | collective-permute-start | bytes 98312 | tf_op jit(solution)/shard_map/ppermute | solution.py:218
  7.4 1.1 collective-permute-done.1
  8.5 0.1 copy.9
  8.6 0.8 broadcast_in_dim.2
  9.3 15.0 %all-to-all-start = ((bf16[8,128,128]{2,1,0:T(8,128)(2,1)}), bf16[8,128,128]{2,1,0:T(8,128)(2,1)S(1)}, u32[]{:S(2)}, u32[]{:S(2)}) async-start(bf16[8,128,128]{2,1,0:T(8,128)(2,1)} %broadcast_in_dim.2), calls=%async_computation | async-start | bytes 524288 | tf_op jit(solution)/shard_map/all_to_all | solution.py:20
  24.4 0.2 fusion.basis_ref
  24.6 0.1 pad_add_fusion.at_ref
  24.7 1.4 pack.1
  26.2 4.8 %collective-permute-start.3 = (bf16[336,896]{1,0:T(8,128)(2,1)}, bf16[336,896]{1,0:T(8,128)(2,1)S(1)}, u32[]{:S(2)}, u32[]{:S(2)}) collective-permute-start(bf16[336,896]{1,0:T(8,128)(2,1)} %get-tuple-element.20), channel_id=1, source_target_pairs={{0,256},{128,384},{256,0},{384,128},{1,257},{129,385},{257,1},{385... | collective-permute-start | bytes 1806344 | tf_op jit(solution)/shard_map/ppermute | solution.py:28
  31.0 4.3 %collective-permute-start = (bf16[256,1024]{1,0:T(8,128)(2,1)S(1)}, bf16[256,1024]{1,0:T(8,128)(2,1)S(1)}, u32[]{:S(2)}, u32[]{:S(2)}) collective-permute-start(bf16[256,1024]{1,0:T(8,128)(2,1)S(1)} %copy-done.2), channel_id=1, source_target_pairs={{0,1},{1,0},{2,3},{3,2},{4,5},{5,4},{6,7},{7,6},{8,9},{9,8},{10,11... | collective-permute-start | bytes 1572872 | tf_op jit(solution)/shard_map/ppermute | solution.py:239
  35.3 6.2 %all-to-all-done.own_ref = bf16[8,128,128]{2,1,0:T(8,128)(2,1)S(1)} async-done(((bf16[8,128,128]{2,1,0:T(8,128)(2,1)}), bf16[8,128,128]{2,1,0:T(8,128)(2,1)S(1)}, u32[]{:S(2)}, u32[]{:S(2)}) %all-to-all-start) | async-done | bytes 262176 | tf_op jit(solution)/shard_map/all_to_all | solution.py:20
  41.5 2.7 %collective-permute-start.2 = (bf16[8,128,128]{2,1,0:T(8,128)(2,1)S(1)}, bf16[8,128,128]{2,1,0:T(8,128)(2,1)S(1)}, u32[]{:S(2)}, u32[]{:S(2)}) collective-permute-start(bf16[8,128,128]{2,1,0:T(8,128)(2,1)S(1)} %all-to-all-done.own_ref), channel_id=1, source_target_pairs={{0,8},{8,0},{1,9},{9,1},{2,10},{10,2},{3,11},{11,3},{4,12},{12,4},... | collective-permute-start | bytes 786440 | tf_op jit(solution)/shard_map/ppermute | solution.py:220
  44.2 3.8 %collective-permute-start.4 = (bf16[336,896]{1,0:T(8,128)(2,1)}, bf16[336,896]{1,0:T(8,128)(2,1)S(1)}, u32[]{:S(2)}, u32[]{:S(2)}) collective-permute-start(bf16[336,896]{1,0:T(8,128)(2,1)} %copy-done.7), channel_id=1, source_target_pairs={{0,128},{128,256},{256,384},{384,0},{1,129},{129,257},{257,385},{3... | collective-permute-start | bytes 1806344 | tf_op jit(solution)/shard_map/ppermute | solution.py:28
  48.0 0.7 collective-permute-start.5
  48.7 0.0 collective-permute-done.other_ref
  48.8 1.0 project.1
  49.8 11.1 %all_to_all.25.summands_ref = f32[4,256,128]{2,1,0:T(8,128)S(1)} all-to-all(f32[4,256,128]{2,1,0:T(8,128)S(1)} %project.1), channel_id=1, replica_groups=mesh['y'=4,'h'=8,'l'=2,'x'=4,'c'=2] {'x'}, dimensions={0} | all-to-all | bytes 1048576 | tf_op jit(solution)/shard_map/all_to_all | solution.py:20
  60.9 0.6 round.1
  61.5 21.7 %all_to_all.26 = bf16[8,256,128]{2,1,0:T(8,128)(2,1)S(1)} all-to-all(bf16[8,256,128]{2,1,0:T(8,128)(2,1)S(1)} %round.1), channel_id=1, replica_groups=mesh['y'=4,'h'=8,'l'=2,'x'=4,'c'=2] {'c','y'}, dimensions={0} | all-to-all | bytes 1048576 | tf_op jit(solution)/shard_map/all_to_all | solution.py:20
  83.2 2.7 %collective-permute-start.6 = (bf16[336,896]{1,0:T(8,128)(2,1)S(1)}, bf16[336,896]{1,0:T(8,128)(2,1)S(1)}, u32[]{:S(2)}, u32[]{:S(2)}) collective-permute-start(bf16[336,896]{1,0:T(8,128)(2,1)S(1)} %copy-done.6), channel_id=1, source_target_pairs={{1,385},{129,1},{257,129},{385,257},{3,387},{131,3},{259,131},{387... | collective-permute-start | bytes 1806344 | tf_op jit(solution)/shard_map/ppermute | solution.py:32
  85.9 1.3 early.1.early_ref
  87.2 6.7 %collective-permute-done.6.late_ref.refs_4_ = bf16[336,896]{1,0:T(8,128)(2,1)S(1)} collective-permute-done((bf16[336,896]{1,0:T(8,128)(2,1)S(1)}, bf16[336,896]{1,0:T(8,128)(2,1)S(1)}, u32[]{:S(2)}, u32[]{:S(2)}) %collective-permute-start.6) | collective-permute-done | bytes 602144 | tf_op jit(solution)/shard_map/ppermute | solution.py:32
  94.0 0.9 partial.1
  94.8 22.2 %all_to_all.27.pieces_ref = bf16[16,16,896]{2,1,0:T(8,128)(2,1)S(1)} all-to-all(bf16[16,16,896]{2,1,0:T(8,128)(2,1)S(1)} %bitcast.13), channel_id=1, replica_groups=mesh['y'=4,'h'=8,'l'=2,'x'=4,'c'=2] {'h','l'}, dimensions={0} | all-to-all | bytes 917504 | tf_op jit(solution)/shard_map/all_to_all | solution.py:20
  117.0 0.8 sum_and_adam.1
  117.8 24.3 %all_gather.3.direction_ref = bf16[256,896]{1,0:T(8,128)(2,1)S(1)} all-gather(bf16[16,896]{1,0:T(8,128)(2,1)S(1)} %get-tuple-element.31), channel_id=1, replica_groups=mesh['y'=4,'h'=8,'l'=2,'x'=4,'c'=2] {'h','l'}, dimensions={0}, use_global_device_ids=true | all-gather | bytes 487424 | tf_op jit(solution)/shard_map/all_gather | solution.py:263
  142.1 1.0 update.1
  143.1 17.1 %all_to_all.28.arrived_ref = bf16[4,144,896]{2,1,0:T(8,128)(2,1)S(1)} all-to-all(bf16[4,144,896]{2,1,0:T(8,128)(2,1)S(1)} %update.1), channel_id=1, replica_groups=mesh['y'=4,'h'=8,'l'=2,'x'=4,'c'=2] {'y'}, dimensions={0} | all-to-all | bytes 2064384 | tf_op jit(solution)/shard_map/all_to_all | solution.py:20
  160.3 1.9 %finish.1 = (f32[4,3584]{1,0:T(4,128)}, f32[4,3584]{1,0:T(4,128)}, f32[128,3584]{1,0:T(8,128)}) custom-call(s32[3]{0:T(128)S(1)} %pad_add_fusion.at_ref, bf16[4,144,896]{2,1,0:T(8,128)(2,1)S(1)} %all_to_all.28.arrived_ref, f32[4,3584]{1,0:T(4,128)S(1)} %copy-done.4, f32[4,3584]{1,0:T(4,128)S(1)} %copy-done.3), custom_call_target="tpu_custom_call" | custom-call | tf_op jit(solution)/shard_map/finish/pallas_call | solution.py:36
  (29 shorter events, 0.2 us)
Async XLA Ops:
  0.6 0.8 copy-start
  0.6 24.0 %copy-start.3 = (f32[4,3584]{1,0:T(4,128)S(1)}, f32[4,3584]{1,0:T(4,128)}, u32[]{:S(2)}) copy-start(f32[4,3584]{1,0:T(4,128)} %second_ref.1) | copy-start | bytes 172036
  0.7 24.0 %copy-start.4 = (f32[4,3584]{1,0:T(4,128)S(1)}, f32[4,3584]{1,0:T(4,128)}, u32[]{:S(2)}) copy-start(f32[4,3584]{1,0:T(4,128)} %first_ref.1) | copy-start | bytes 172036
  0.7 24.0 %copy-start.1 = (bf16[256,3584]{1,0:T(8,128)(2,1)S(1)}, bf16[256,3584]{1,0:T(8,128)(2,1)}, u32[]{:S(2)}) copy-start(bf16[256,3584]{1,0:T(8,128)(2,1)} %grad_ref.1) | copy-start | bytes 5505028
  1.7 6.8 %collective-permute-start.1 = (bf16[128,128]{0,1:T(8,128)(2,1)S(1)}, bf16[128,128]{0,1:T(8,128)(2,1)S(1)}, u32[]{:S(2)}, u32[]{:S(2)}) collective-permute-start(bf16[128,128]{0,1:T(8,128)(2,1)S(1)} %fusion.1), channel_id=1, source_target_pairs={{4,0},{132,2},{260,4},{388,6},{6,128},{134,130},{262,132},{390,134... | collective-permute-start | bytes 98312 | tf_op jit(solution)/shard_map/ppermute | solution.py:218
  9.3 32.2 %all-to-all-start = ((bf16[8,128,128]{2,1,0:T(8,128)(2,1)}), bf16[8,128,128]{2,1,0:T(8,128)(2,1)S(1)}, u32[]{:S(2)}, u32[]{:S(2)}) async-start(bf16[8,128,128]{2,1,0:T(8,128)(2,1)} %broadcast_in_dim.2), calls=%async_computation | async-start | bytes 524288 | tf_op jit(solution)/shard_map/all_to_all | solution.py:20
  24.4 6.6 %copy-start.2 = (bf16[256,1024]{1,0:T(8,128)(2,1)S(1)}, bf16[256,1024]{1,0:T(8,128)(2,1)}, u32[]{:S(2)}) copy-start(bf16[256,1024]{1,0:T(8,128)(2,1)} %tokens_ref) | copy-start | bytes 1572868
  26.1 4.9 %copy-start.5 = (bf16[336,896]{1,0:T(8,128)(2,1)}, bf16[336,896]{1,0:T(8,128)(2,1)S(1)}, u32[]{:S(2)}) copy-start(bf16[336,896]{1,0:T(8,128)(2,1)S(1)} %get-tuple-element.30) | copy-start | bytes 1806340
  26.1 4.9 %copy-start.7 = (bf16[336,896]{1,0:T(8,128)(2,1)}, bf16[336,896]{1,0:T(8,128)(2,1)S(1)}, u32[]{:S(2)}) copy-start(bf16[336,896]{1,0:T(8,128)(2,1)S(1)} %get-tuple-element.22) | copy-start | bytes 1806340
  26.2 23.6 %collective-permute-start.3 = (bf16[336,896]{1,0:T(8,128)(2,1)}, bf16[336,896]{1,0:T(8,128)(2,1)S(1)}, u32[]{:S(2)}, u32[]{:S(2)}) collective-permute-start(bf16[336,896]{1,0:T(8,128)(2,1)} %get-tuple-element.20), channel_id=1, source_target_pairs={{0,256},{128,384},{256,0},{384,128},{1,257},{129,385},{257,1},{385... | collective-permute-start | bytes 1806344 | tf_op jit(solution)/shard_map/ppermute | solution.py:28
  31.0 17.7 %collective-permute-start = (bf16[256,1024]{1,0:T(8,128)(2,1)S(1)}, bf16[256,1024]{1,0:T(8,128)(2,1)S(1)}, u32[]{:S(2)}, u32[]{:S(2)}) collective-permute-start(bf16[256,1024]{1,0:T(8,128)(2,1)S(1)} %copy-done.2), channel_id=1, source_target_pairs={{0,1},{1,0},{2,3},{3,2},{4,5},{5,4},{6,7},{7,6},{8,9},{9,8},{10,11... | collective-permute-start | bytes 1572872 | tf_op jit(solution)/shard_map/ppermute | solution.py:239
  41.5 7.2 %collective-permute-start.2 = (bf16[8,128,128]{2,1,0:T(8,128)(2,1)S(1)}, bf16[8,128,128]{2,1,0:T(8,128)(2,1)S(1)}, u32[]{:S(2)}, u32[]{:S(2)}) collective-permute-start(bf16[8,128,128]{2,1,0:T(8,128)(2,1)S(1)} %all-to-all-done.own_ref), channel_id=1, source_target_pairs={{0,8},{8,0},{1,9},{9,1},{2,10},{10,2},{3,11},{11,3},{4,12},{12,4},... | collective-permute-start | bytes 786440 | tf_op jit(solution)/shard_map/ppermute | solution.py:220
  44.2 17.3 %collective-permute-start.4 = (bf16[336,896]{1,0:T(8,128)(2,1)}, bf16[336,896]{1,0:T(8,128)(2,1)S(1)}, u32[]{:S(2)}, u32[]{:S(2)}) collective-permute-start(bf16[336,896]{1,0:T(8,128)(2,1)} %copy-done.7), channel_id=1, source_target_pairs={{0,128},{128,256},{256,384},{384,0},{1,129},{129,257},{257,385},{3... | collective-permute-start | bytes 1806344 | tf_op jit(solution)/shard_map/ppermute | solution.py:28
  48.0 13.5 %collective-permute-start.5 = (bf16[336,896]{1,0:T(8,128)(2,1)}, bf16[336,896]{1,0:T(8,128)(2,1)S(1)}, u32[]{:S(2)}, u32[]{:S(2)}) collective-permute-start(bf16[336,896]{1,0:T(8,128)(2,1)} %copy-done.5), channel_id=1, source_target_pairs={{0,384},{128,0},{256,128},{384,256},{2,386},{130,2},{258,130},{386... | collective-permute-start | bytes 1806344 | tf_op jit(solution)/shard_map/ppermute | solution.py:32
  49.8 33.5 %copy-start.6 = (bf16[336,896]{1,0:T(8,128)(2,1)S(1)}, bf16[336,896]{1,0:T(8,128)(2,1)}, u32[]{:S(2)}) copy-start(bf16[336,896]{1,0:T(8,128)(2,1)} %copy-done.5) | copy-start | bytes 1806340
  83.2 10.7 %collective-permute-start.6 = (bf16[336,896]{1,0:T(8,128)(2,1)S(1)}, bf16[336,896]{1,0:T(8,128)(2,1)S(1)}, u32[]{:S(2)}, u32[]{:S(2)}) collective-permute-start(bf16[336,896]{1,0:T(8,128)(2,1)S(1)} %copy-done.6), channel_id=1, source_target_pairs={{1,385},{129,1},{257,129},{385,257},{3,387},{131,3},{259,131},{387... | collective-permute-start | bytes 1806344 | tf_op jit(solution)/shard_map/ppermute | solution.py:32
